TPU v7x, 512 devices: a whole 4x8x8 slice. The times are simulated.
512 devices in a mesh: dp: 8 (over y_hi, x), expert: 64 (over y_lo, z, core).
Axes of the slice: x: 4, y: 8 (y_hi: 2, y_lo: 4; y = y_hi * 4 + y_lo), z: 8, core: 2. Of those that a mesh axis runs over, the one named last changes fastest.
Arguments:
- tokens: bfloat16 [65536, 2560], P(('dp', 'expert')), may hold values from -6 to 6
- expert_ids: int32 [65536, 6], P(('dp', 'expert')), may hold values from 0 to 159, as said below
- gate_probs: float32 [65536, 6], P(('dp', 'expert')), may hold values from 0.1 to 1
- act_grad: bfloat16 [65536, 6, 1024], P(('dp', 'expert')), may hold values from -0.59765625 to 0.59765625
- hot_experts: int32 [32], replicated, may hold values from 0 to 63, as said below
- w_gate: bfloat16 [64, 2560, 1024], P('expert', None, 'dp'), may hold values from -0.125 to 0.125
- w_up: bfloat16 [64, 2560, 1024], P('expert', None, 'dp'), may hold values from -0.125 to 0.125
Outputs:
- grad_gate: bfloat16 [64, 2560, 1024], P('expert', None, 'dp')
- grad_up: bfloat16 [64, 2560, 1024], P('expert', None, 'dp')
Inputs may be any that keep to these rules, and one draw needn't show every extreme that they name: `expert_ids`: each row names 6 different experts. `hot_experts`: 32 different experts, always including 0, 1, 30, 31, 32, 33, 62 and 63.
All inputs are finite; a program needn't handle non-finite values.
Results may differ from a plain program's by a relative error of at most 0.0061.
Values may be sent and summed in bfloat16 or wider, within the bound.
No kernel may reach another device: no remote copies, remote signals or barrier semaphores. Data moves between devices by JAX's collectives and lax.ppermute only.
A program may use at most 128 MiB of HBM per device.

v0:
```python
import jax
import jax.numpy as jnp
from jax import lax
from jax.sharding import PartitionSpec as P

TOP = 6
CAP = 2
OVF = 2


def passed_along(block, axis, distance):
    devices = range(lax.axis_size(axis))
    route = [((i - distance) % len(devices), i) for i in devices]
    return lax.ppermute(block, axis, route)


def expert_grads(tok_rows, act_rows, weight_gate, weight_up):
    gate_pre = jnp.dot(tok_rows, weight_gate, preferred_element_type=jnp.float32)
    up_pre = jnp.dot(tok_rows, weight_up, preferred_element_type=jnp.float32)
    sigma_gate = jax.nn.sigmoid(gate_pre)
    upstream = act_rows.astype(jnp.float32)
    grad_up_rows = (upstream * gate_pre * sigma_gate).astype(jnp.bfloat16)
    grad_gate_rows = (
        upstream * up_pre * sigma_gate * (1.0 + gate_pre * (1.0 - sigma_gate))
    ).astype(jnp.bfloat16)
    contract = (((0,), (0,)), ((), ()))
    gate_sum = lax.dot_general(
        tok_rows, grad_gate_rows, contract, preferred_element_type=jnp.float32
    )
    up_gradient_sum = lax.dot_general(
        tok_rows, grad_up_rows, contract, preferred_element_type=jnp.float32
    )
    return (gate_sum, up_gradient_sum)


def slot_tables(block_ids, hot_experts, experts, offset):
    flat_ids = block_ids.reshape(-1)
    assigned = flat_ids.shape[0]
    matching = flat_ids[:, None] == jnp.arange(experts, dtype=jnp.int32)[None, :]
    running = jnp.cumsum(matching.astype(jnp.int32), axis=0) - 1
    position = jnp.sum(jnp.where(matching, running, 0), axis=1)
    in_window = flat_ids < experts
    is_popular = jnp.any(flat_ids[:, None] == hot_experts[None, :], axis=1)
    own_mask = in_window & (position < CAP)
    lent_mask = in_window & is_popular & (position >= CAP) & (position < CAP + OVF)
    numbers = jnp.arange(assigned, dtype=jnp.int32)
    own_slot = jnp.where(own_mask, flat_ids * CAP + position, experts * CAP)
    own_table = jnp.full((experts * CAP,), -1, jnp.int32).at[own_slot].set(numbers, mode="drop")
    helper = (flat_ids + offset) % experts
    lent_slot = jnp.where(lent_mask, helper * OVF + position - CAP, experts * OVF)
    lent_table = jnp.full((experts * OVF,), -1, jnp.int32).at[lent_slot].set(numbers, mode="drop")
    return (own_table, lent_table)


def pick_rows(source, table, divisor, row_base):
    valid = table >= 0
    index = jnp.maximum(table, 0) // divisor + row_base
    picked = jnp.take(source, index.reshape(-1), axis=0)
    picked = jnp.where(valid.reshape(-1)[:, None], picked, jnp.zeros((), source.dtype))
    return picked.reshape(table.shape + (source.shape[1],))


def body(tokens, expert_ids, gate_probs, act_grad, hot_experts, w_gate, w_up):
    experts = lax.axis_size("expert")
    width = tokens.shape[1]
    hidden = w_gate.shape[2]
    offset = experts // 2
    scaled = (gate_probs[:, :, None] * act_grad.astype(jnp.float32)).astype(jnp.bfloat16)
    scaled = scaled.reshape(-1, act_grad.shape[2])
    own_table, lent_table = slot_tables(expert_ids, hot_experts, experts, offset)
    own_acts = pick_rows(scaled, own_table.reshape(experts, CAP), 1, 0)
    lent_acts = pick_rows(scaled, lent_table.reshape(experts, OVF), 1, 0)
    weight_couple = jnp.stack([w_gate[0], w_up[0]])
    lent_pair = passed_along(weight_couple, "expert", offset)
    own_tok = pick_rows(tokens, own_table.reshape(experts, CAP), TOP, 0)
    lent_tok = pick_rows(tokens, lent_table.reshape(experts, OVF), TOP, 0)
    own_tok, own_acts, lent_tok, lent_acts = (
        lax.all_to_all(own_tok, "expert", split_axis=0, concat_axis=0, tiled=True),
        lax.all_to_all(own_acts, "expert", split_axis=0, concat_axis=0, tiled=True),
        lax.all_to_all(lent_tok, "expert", split_axis=0, concat_axis=0, tiled=True),
        lax.all_to_all(lent_acts, "expert", split_axis=0, concat_axis=0, tiled=True),
    )
    own_acts, lent_acts = (
        lax.all_to_all(own_acts, "dp", split_axis=2, concat_axis=0, tiled=True),
        lax.all_to_all(lent_acts, "dp", split_axis=2, concat_axis=0, tiled=True),
    )
    local_portion = lax.all_gather(own_tok, "dp", axis=0, tiled=True)
    lent_piece = lax.all_gather(lent_tok, "dp", axis=0, tiled=True)
    gate_own, up_own = expert_grads(
        local_portion.reshape(-1, width), own_acts.reshape(-1, hidden), w_gate[0], w_up[0]
    )
    gate_lent, up_lent = expert_grads(
        lent_piece.reshape(-1, width), lent_acts.reshape(-1, hidden), lent_pair[0], lent_pair[1]
    )
    helper_sums = jnp.stack([gate_lent, up_lent]).astype(jnp.bfloat16)
    returned = passed_along(helper_sums, "expert", experts - offset)
    grad_gate = (gate_own + returned[0].astype(jnp.float32)).astype(jnp.bfloat16)
    grad_up = (up_own + returned[1].astype(jnp.float32)).astype(jnp.bfloat16)
    return (grad_gate[None], grad_up[None])


def solution(mesh):
    return jax.shard_map(
        body,
        mesh=mesh,
        in_specs=(
            P(("dp", "expert"), None),
            P(("dp", "expert"), None),
            P(("dp", "expert"), None),
            P(("dp", "expert"), None, None),
            P(),
            P("expert", None, "dp"),
            P("expert", None, "dp"),
        ),
        out_specs=(P("expert", None, "dp"), P("expert", None, "dp")),
        check_vma=False,
    )
```

profile of v0, /device:TPU:1, one launch (start us, length us, event | category | flops | bytes accessed | tf_op | source)
XLA Modules:
  0.0 406.9 jit_solution(11672382692374478922)
XLA Ops:
  7.2 0.9 copy.48
  9.8 1.8 reduce-window.6
  13.6 3.4 scatter_custom_fusion.1
  17.1 1.0 gather_fusion.2
  18.5 35.5 %all_to_all.38 = bf16[64,2,2560]{2,1,0:T(2,128)(2,1)} all-to-all(bf16[64,2,2560]{2,1,0:T(2,128)(2,1)S(1)} %reshape.232), channel_id=1, replica_groups=mesh['dp'=8,'expert'=64] {'expert'}, dimensions={0} | all-to-all | bytes 1310720 | tf_op jit(solution)/shard_map/all_to_all | solution.py:80
  54.0 3.4 scatter_custom_fusion
  57.9 1.0 gather_fusion
  59.4 39.5 %all_to_all.39 = bf16[64,2,2560]{2,1,0:T(2,128)(2,1)} all-to-all(bf16[64,2,2560]{2,1,0:T(2,128)(2,1)S(1)} %reshape.228), channel_id=1, replica_groups=mesh['dp'=8,'expert'=64] {'expert'}, dimensions={0} | all-to-all | bytes 1310720 | tf_op jit(solution)/shard_map/all_to_all | solution.py:78
  98.9 1.2 pad_maximum_fusion
  100.1 2.9 collective-permute-start
  103.3 2.2 copy.52
  105.5 2.6 reshape.230
  108.2 0.9 gather_fusion.3
  109.3 115.5 %all_to_all.40 = bf16[64,2,1024]{2,1,0:T(2,128)(2,1)} all-to-all(bf16[64,2,1024]{2,1,0:T(2,128)(2,1)S(1)} %reshape.234), channel_id=1, replica_groups=mesh['dp'=8,'expert'=64] {'expert'}, dimensions={0} | all-to-all | bytes 524288 | tf_op jit(solution)/shard_map/all_to_all | solution.py:81
  224.8 1.4 copy.57
  226.2 1.1 reshape.308
  227.3 6.6 %all-to-all-start.5 = ((bf16[8,2,8192]{2,1,0:T(2,128)(2,1)}), bf16[8,2,8192]{2,1,0:T(2,128)(2,1)S(1)}, u32[]{:S(2)}, u32[]{:S(2)}) async-start(bf16[8,2,8192]{2,1,0:T(2,128)(2,1)} %reshape.308), calls=%async_computation.5 | async-start | bytes 524288 | tf_op jit(solution)/shard_map/all_to_all | solution.py:85
  234.0 0.9 gather_fusion.1
  235.8 10.4 %all-to-all-done.5 = bf16[8,2,8192]{2,1,0:T(2,128)(2,1)S(1)} async-done(((bf16[8,2,8192]{2,1,0:T(2,128)(2,1)}), bf16[8,2,8192]{2,1,0:T(2,128)(2,1)S(1)}, u32[]{:S(2)}, u32[]{:S(2)}) %all-to-all-start.5) | async-done | bytes 262176 | tf_op jit(solution)/shard_map/all_to_all | solution.py:85
  246.1 11.7 %all-to-all-start.1 = ((bf16[64,2,1024]{2,1,0:T(2,128)(2,1)}), bf16[64,2,1024]{2,1,0:T(2,128)(2,1)S(1)}, u32[]{:S(2)}, u32[]{:S(2)}) async-start(bf16[64,2,1024]{2,1,0:T(2,128)(2,1)} %reshape.231), calls=%async_computation.1 | async-start | bytes 524288 | tf_op jit(solution)/shard_map/all_to_all | solution.py:79
  259.2 11.7 %reshape.233 = bf16[1024,2560]{1,0:T(8,128)(2,1)} reshape(bf16[512,2,2560]{2,1,0:T(2,128)(2,1)} %all-gather.5.cloned.1.call-done) | data formatting | bytes 10485760 | tf_op jit(solution)/shard_map/reshape | solution.py:93
  271.0 4.3 %fusion.13 = f32[1024,128]{1,0:T(8,128)S(1)} fusion(bf16[1024,2560]{1,0:T(8,128)(2,1)} %reshape.233, bf16[2,2560,128]{2,1,0:T(8,128)(2,1)} %collective-permute-done), kind=kOutput, calls=%fused_computation.31 | convolution fusion | flops 671088640 | bytes 6422528 | tf_op jit(solution)/shard_map/dot_general | solution.py:18
  276.1 1.6 fusion.1
  277.7 10.0 %fusion = bf16[1,2560,128]{2,1,0:T(8,128)(2,1)S(1)} fusion(bf16[1024,2560]{1,0:T(8,128)(2,1)} %reshape.233, f32[1024,128]{1,0:T(8,128)S(1)} %bitcast.90, bf16[2,2560,128]{2,1,0:T(8,128)(2,1)} %collective-permute-done, f32[1024,128]{1,0:T(8,128)} %copy-done.13), kind=kOutput, calls=%fused_computation.8 | convolution fusion | flops 1343815680 | bytes 12845056 | tf_op jit(solution)/shard_map/dot_general | solution.py:27
  287.6 1.2 pad_maximum_fusion.1
  288.8 4.3 %collective-permute-start.1 = (bf16[2,2560,128]{2,1,0:T(8,128)(2,1)}, bf16[2,2560,128]{2,1,0:T(8,128)(2,1)}, u32[]{:S(2)}, u32[]{:S(2)}) collective-permute-start(bf16[2,2560,128]{2,1,0:T(8,128)(2,1)} %pad_maximum_fusion.1), channel_id=1, source_target_pairs={{32,0},{33,1},{34,2},{35,3},{36,4},{37,5},{38,6},{39,7},{40,8},{41... | collective-permute-start | bytes 3932168 | tf_op jit(solution)/shard_map/ppermute | solution.py:14
  294.0 67.6 %all_to_all.41 = bf16[8,2,8192]{2,1,0:T(2,128)(2,1)S(1)} all-to-all(bf16[8,2,8192]{2,1,0:T(2,128)(2,1)S(1)} %reshape.310), channel_id=1, replica_groups=mesh['dp'=8,'expert'=64] {'dp'}, dimensions={0} | all-to-all | bytes 524288 | tf_op jit(solution)/shard_map/all_to_all | solution.py:84
  362.9 11.6 %reshape.229 = bf16[1024,2560]{1,0:T(8,128)(2,1)} reshape(bf16[512,2,2560]{2,1,0:T(2,128)(2,1)} %all-gather.3.cloned.1.call-done) | data formatting | bytes 10485760 | tf_op jit(solution)/shard_map/reshape | solution.py:90
  374.6 4.1 %fusion.14 = f32[1024,128]{1,0:T(8,128)S(1)} fusion(bf16[1024,2560]{1,0:T(8,128)(2,1)} %reshape.229, bf16[1,2560,128]{2,1,0:T(8,128)(2,1)S(1)} %copy-done.3), kind=kOutput, calls=%fused_computation.33 | convolution fusion | flops 671088640 | bytes 6422528 | tf_op jit(solution)/shard_map/dot_general | solution.py:18
  378.7 7.2 %collective-permute-done.1 = bf16[2,2560,128]{2,1,0:T(8,128)(2,1)} collective-permute-done((bf16[2,2560,128]{2,1,0:T(8,128)(2,1)}, bf16[2,2560,128]{2,1,0:T(8,128)(2,1)}, u32[]{:S(2)}, u32[]{:S(2)}) %collective-permute-start.1) | collective-permute-done | bytes 1310752 | tf_op jit(solution)/shard_map/ppermute | solution.py:14
  386.0 3.6 fusion.12
  389.6 10.5 %fusion.11 = bf16[1,2560,128]{2,1,0:T(8,128)(2,1)} fusion(bf16[2,2560,128]{2,1,0:T(8,128)(2,1)} %collective-permute-done.1, bf16[1024,2560]{1,0:T(8,128)(2,1)} %reshape.229, f32[1024,128]{1,0:T(8,128)S(1)} %bitcast.92, bf16[1,2560,128]{2,1,0:T(8,128)(2,1)S(1)} %copy-done.6, f32[1024,128]{1,0:T(8,128)S(1)} %fusion.14), kind=kOutput, calls=%fused_computation.26 | convolution fusion | flops 1344471040 | bytes 13500416 | tf_op jit(solution)/shard_map/dot_general | solution.py:27
  (83 shorter events, 10.9 us)
Async XLA Ops:
  7.2 9.9 %copy-start = (bf16[128,2560]{1,0:T(8,128)(2,1)S(1)}, bf16[128,2560]{1,0:T(8,128)(2,1)}, u32[]{:S(2)}) copy-start(bf16[128,2560]{1,0:T(8,128)(2,1)} %param.11) | copy-start | bytes 1966084
  7.2 252.0 %all-gather.5.cloned.1.call-start = ((), (), s32[]{:S(2)}) async-start(), calls=%async_computation.7 | async-start | bytes 5898240 | tf_op jit(solution)/shard_map/all_gather | solution.py:88
  17.0 1.0 copy-start.9
  54.0 309.0 %all-gather.3.cloned.1.call-start = ((), (), s32[]{:S(2)}) async-start(), calls=%async_computation.6 | async-start | bytes 5898240 | tf_op jit(solution)/shard_map/all_gather | solution.py:87
  57.4 1.5 copy-start.11
  58.9 40.0 %copy-start.3 = (bf16[1,2560,128]{2,1,0:T(8,128)(2,1)S(1)}, bf16[1,2560,128]{2,1,0:T(8,128)(2,1)}, u32[]{:S(2)}) copy-start(bf16[1,2560,128]{2,1,0:T(8,128)(2,1)} %param.16) | copy-start | bytes 1966084
  58.9 39.9 %copy-start.5 = (bf16[1,2560,128]{2,1,0:T(8,128)(2,1)S(1)}, bf16[1,2560,128]{2,1,0:T(8,128)(2,1)}, u32[]{:S(2)}) copy-start(bf16[1,2560,128]{2,1,0:T(8,128)(2,1)} %param.17) | copy-start | bytes 1966084
  59.4 43.6 %copy-start.7 = (f32[128,6]{0,1:T(8,128)S(1)}, f32[128,6]{0,1:T(8,128)}, u32[]{:S(2)}) copy-start(f32[128,6]{0,1:T(8,128)} %param.13) | copy-start | bytes 9220
  98.8 4.1 %copy-start.4 = (bf16[128,6,1024]{2,0,1:T(8,128)(2,1)S(1)}, bf16[128,6,1024]{2,0,1:T(8,128)(2,1)}, u32[]{:S(2)}) copy-start(bf16[128,6,1024]{2,0,1:T(8,128)(2,1)} %param.14) | copy-start | bytes 4718596
  100.1 170.9 %collective-permute-start = (bf16[2,2560,128]{2,1,0:T(8,128)(2,1)}, bf16[2,2560,128]{2,1,0:T(8,128)(2,1)}, u32[]{:S(2)}, u32[]{:S(2)}) collective-permute-start(bf16[2,2560,128]{2,1,0:T(8,128)(2,1)} %pad_maximum_fusion), channel_id=1, source_target_pairs={{32,0},{33,1},{34,2},{35,3},{36,4},{37,5},{38,6},{39,7},{40,8},{41... | collective-permute-start | bytes 3932168 | tf_op jit(solution)/shard_map/ppermute | solution.py:14
  105.5 2.6 copy-start.10
  109.0 124.9 %copy-start.12 = (s32[128]{0:T(128)S(1)}, s32[128]{0:T(128)}, u32[]{:S(2)}) copy-start(s32[128]{0:T(128)} %copy-done.11) | copy-start | bytes 1540
  224.8 10.1 %copy-start.8 = (pred[128]{0:T(512)(128)(4,1)S(1)}, pred[128]{0:T(512)(128)(4,1)}, u32[]{:S(2)}) copy-start(pred[128]{0:T(512)(128)(4,1)} %get-tuple-element.12) | copy-start | bytes 388
  227.3 18.8 %all-to-all-start.5 = ((bf16[8,2,8192]{2,1,0:T(2,128)(2,1)}), bf16[8,2,8192]{2,1,0:T(2,128)(2,1)S(1)}, u32[]{:S(2)}, u32[]{:S(2)}) async-start(bf16[8,2,8192]{2,1,0:T(2,128)(2,1)} %reshape.308), calls=%async_computation.5 | async-start | bytes 524288 | tf_op jit(solution)/shard_map/all_to_all | solution.py:85
  246.1 47.0 %all-to-all-start.1 = ((bf16[64,2,1024]{2,1,0:T(2,128)(2,1)}), bf16[64,2,1024]{2,1,0:T(2,128)(2,1)S(1)}, u32[]{:S(2)}, u32[]{:S(2)}) async-start(bf16[64,2,1024]{2,1,0:T(2,128)(2,1)} %reshape.231), calls=%async_computation.1 | async-start | bytes 524288 | tf_op jit(solution)/shard_map/all_to_all | solution.py:79
  270.9 5.1 %copy-start.2 = (bf16[1024,2560]{1,0:T(8,128)(2,1)S(1)}, bf16[1024,2560]{1,0:T(8,128)(2,1)}, u32[]{:S(2)}) copy-start(bf16[1024,2560]{1,0:T(8,128)(2,1)} %reshape.233) | copy-start | bytes 15728644
  275.3 0.8 copy-start.13
  288.8 97.2 %collective-permute-start.1 = (bf16[2,2560,128]{2,1,0:T(8,128)(2,1)}, bf16[2,2560,128]{2,1,0:T(8,128)(2,1)}, u32[]{:S(2)}, u32[]{:S(2)}) collective-permute-start(bf16[2,2560,128]{2,1,0:T(8,128)(2,1)} %pad_maximum_fusion.1), channel_id=1, source_target_pairs={{32,0},{33,1},{34,2},{35,3},{36,4},{37,5},{38,6},{39,7},{40,8},{41... | collective-permute-start | bytes 3932168 | tf_op jit(solution)/shard_map/ppermute | solution.py:14
  374.6 11.4 %copy-start.1 = (bf16[1024,2560]{1,0:T(8,128)(2,1)S(1)}, bf16[1024,2560]{1,0:T(8,128)(2,1)}, u32[]{:S(2)}) copy-start(bf16[1024,2560]{1,0:T(8,128)(2,1)} %reshape.229) | copy-start | bytes 15728644
  386.0 3.6 copy-start.6
Sparse Core Ops, SparseCore 0:
  54.1 154.5 all-gather.4
  211.9 141.6 all-gather.2
where the time goes:
time: 408 us; the launch traced here: 407 us
  blocking collectives  258 us (63%)
  local copies, waits for them, and re-layouts  48.9 us (12%)
  matrix products  34.1 us (8%)
  starting transfers between devices  25.6 us (6%)
  waiting for transfers between devices  17.7 us (4%)
  between operations  14.5 us (4%)
  other arithmetic  8.03 us (2%)
    all_to_all x1, blocking collectives, body(): lax.all_to_all(lent_acts, 'expert', split_axis=0, concat_axis=0, tiled=True)  116 us
    all_to_all x1, blocking collectives, body(): lax.all_to_all(own_acts, 'dp', split_axis=2, concat_axis=0, tiled=True)  67.6 us
    all_to_all x1, blocking collectives, body(): lax.all_to_all(own_tok, 'expert', split_axis=0, concat_axis=0, tiled=True)  39.5 us
    all_to_all x1, blocking collectives, body(): lax.all_to_all(lent_tok, 'expert', split_axis=0, concat_axis=0, tiled=True)  35.5 us
    dot_general x2, matrix products, expert_grads(): lax.dot_general(tok_rows, grad_gate_rows, contract, preferred_element_typ...  20.5 us
    all_to_all x1, starting transfers between devices, body(): lax.all_to_all(own_acts, 'expert', split_axis=0, concat_axis=0, tiled=True)  11.7 us
    reshape x1, local copies, waits for them, and re-layouts, body(): lent_piece.reshape(-1, width)  11.7 us
    reshape x1, local copies, waits for them, and re-layouts, body(): local_portion.reshape(-1, width)  11.6 us
  transfers between devices with their start and end apart: 6, of which 2 were waited for; matrix products, arithmetic and copies ran while one was open for 16% of the time, Pallas kernels for 0%

commit v1 on v0

v1 whole, which is shorter than its diff:
```python
import jax
import jax.numpy as jnp
from jax import lax
from jax.experimental import pallas as pl
from jax.experimental.pallas import tpu as pltpu
from jax.sharding import Mesh, PartitionSpec as P

CAP = 2
OVF = 2
SLOTS = CAP + OVF
AXES = ("yh", "x", "yl", "z", "c")
PLANE = ("yh", "yl", "z", "c")
EXPERT = ("yl", "z", "c")


def pack_kernel(ids_ref, probs_ref, hot_ref, tok_ref, act_ref, out_ref):
    top, block = ids_ref.shape
    experts = out_ref.shape[1] // SLOTS
    rows = experts * SLOTS
    width = tok_ref.shape[1]
    half = out_ref.shape[2] - width
    row = lax.broadcasted_iota(jnp.int32, (rows, block), 0)
    expert, slot = row // SLOTS, row % SLOTS
    hits = [ids_ref[k : k + 1, :] == expert for k in range(top)]
    named = hits[0]
    for hit in hits[1:]:
        named = named | hit
    before = lax.broadcasted_iota(jnp.int32, (block, block), 0) < lax.broadcasted_iota(
        jnp.int32, (block, block), 1
    )
    position = jnp.dot(
        jnp.where(named, 1.0, 0.0).astype(jnp.bfloat16),
        jnp.where(before, 1.0, 0.0).astype(jnp.bfloat16),
        preferred_element_type=jnp.float32,
    ).astype(jnp.int32)
    hots = hot_ref.shape[1]
    owner = lax.broadcasted_iota(jnp.int32, (rows, hots), 0) // SLOTS
    hot = jnp.max(jnp.where(hot_ref[...] == owner, 1, 0), axis=1, keepdims=True)
    kept = named & (position == slot) & ((slot < CAP) | (hot > 0))
    pick = jnp.where(kept, 1.0, 0.0).astype(jnp.bfloat16)
    toks = jnp.dot(pick, tok_ref[...], preferred_element_type=jnp.float32)
    toks = toks.astype(jnp.bfloat16)
    out_ref[0, :, :width] = toks
    out_ref[1, :, :width] = toks
    acts = jnp.zeros((rows, act_ref.shape[2]), jnp.float32)
    for k in range(top):
        scaled = (probs_ref[:, k : k + 1] * act_ref[k].astype(jnp.float32)).astype(jnp.bfloat16)
        chosen = jnp.where(kept & hits[k], 1.0, 0.0).astype(jnp.bfloat16)
        acts += jnp.dot(chosen, scaled, preferred_element_type=jnp.float32)
    acts = acts.astype(jnp.bfloat16)
    out_ref[0, :, width:] = acts[:, :half]
    out_ref[1, :, width:] = acts[:, half:]


def body(tokens, expert_ids, gate_probs, act_grad, hot_experts, w_gate, w_up):
    width = tokens.shape[1]
    ff = act_grad.shape[2]
    copies = lax.axis_size("yh")
    experts = lax.axis_size(EXPERT)
    wg = lax.all_gather(w_gate[0], "x", axis=0)
    wu = lax.all_gather(w_up[0], "x", axis=0)
    send = pl.pallas_call(
        pack_kernel,
        out_shape=jax.ShapeDtypeStruct(
            (copies, experts * SLOTS, width + ff // copies), jnp.bfloat16
        ),
        compiler_params=pltpu.CompilerParams(vmem_limit_bytes=40 * 2**20),
        name="pack_rows",
    )(
        expert_ids.T,
        gate_probs,
        hot_experts.reshape(1, -1),
        tokens,
        jnp.swapaxes(act_grad, 0, 1),
    )
    send = send.reshape(copies * experts, SLOTS, -1)
    recv = lax.all_to_all(send, PLANE, 0, 0, tiled=True)
    recv = recv.reshape(copies * experts * SLOTS, -1)
    toks = recv[:, :width]
    upstream = recv[:, width:].astype(jnp.float32)
    wg = jnp.swapaxes(wg, 0, 1).reshape(width, -1)
    wu = jnp.swapaxes(wu, 0, 1).reshape(width, -1)
    gate = jnp.dot(toks, wg, preferred_element_type=jnp.float32)
    up = jnp.dot(toks, wu, preferred_element_type=jnp.float32)
    sig = jax.nn.sigmoid(gate)
    d_up = (upstream * gate * sig).astype(jnp.bfloat16)
    d_gate = (upstream * up * sig * (1.0 + gate * (1.0 - sig))).astype(jnp.bfloat16)
    planes = lax.axis_size("x")
    parts = []
    for d in (d_gate, d_up):
        total = lax.dot_general(
            toks, d, (((0,), (0,)), ((), ())), preferred_element_type=jnp.float32
        )
        parts.append(jnp.swapaxes(total.astype(jnp.bfloat16).reshape(width, planes, -1), 0, 1))
    parts = jnp.stack(parts, 1)
    out = lax.psum_scatter(parts, "x", scatter_dimension=0, tiled=True)[0]
    return (out[0:1], out[1:2])


def solution(mesh):
    grid = Mesh(mesh.devices.reshape(2, 4, 4, 8, 2), AXES)
    rows = P(AXES)
    weights = P(EXPERT, None, ("yh", "x"))
    return jax.shard_map(
        body,
        mesh=grid,
        in_specs=(rows, rows, rows, rows, P(), weights, weights),
        out_specs=(weights, weights),
        check_vma=False,
    )
```

time: 408 us -> 205 us (0.50)
  blocking collectives: 258 us -> 0 us
  waiting for transfers between devices: 17.7 us -> 123 us
  local copies, waits for them, and re-layouts: 48.9 us -> 28.7 us
  matrix products: 34.1 us -> 14.1 us
  starting transfers between devices: 25.6 us -> 18.5 us
    all_to_all x4 -> x0, blocking collectives: 258 us -> none  [the longest x1 116 us: body(): lax.all_to_all(lent_acts, 'expert', split_axis=0, concat_axis=0, tiled=True)]
    all_gather x2, waiting for transfers between devices: 0.04 us -> 58.5 us  [the longest x1 38.4 us: body(): wu = lax.all_gather(w_up[0], 'x', axis=0)]
    reduce_scatter x0 -> x1, waiting for transfers between devices: none -> 57.9 us  [body(): out = lax.psum_scatter(parts, 'x', scatter_dimension=0, tiled=True)[0]]
    dot_general x6 -> x3, matrix products: 34.1 us -> 14.1 us  [the longest x2 9.9 us: body(): lax.dot_general(toks, d, (((0,), (0,)), ((), ())), preferred_element_type...]
    reshape x7 -> x4, local copies, waits for them, and re-layouts: 27.4 us -> 12.7 us  [the longest x2 7.63 us: body(): total.astype(jnp.bfloat16).reshape(width, planes, -1)]
    all_gather x0 -> x2, local copies, waits for them, and re-layouts: none -> 8.86 us  [the longest x1 4.45 us: body(): wg = lax.all_gather(w_gate[0], 'x', axis=0)]
    ppermute x2 -> x0, waiting for transfers between devices: 7.24 us -> none  [passed_along(): return lax.ppermute(block, axis, route)]
    ppermute x2 -> x0, starting transfers between devices: 7.16 us -> none  [passed_along(): return lax.ppermute(block, axis, route)]
  transfers between devices with their start and end apart: 6 -> 4, of which waited for: 2 -> 4; matrix products, arithmetic and copies ran while one was open for 16% -> 6% of each run, Pallas kernels for 0% -> 1%
where the time goes in v1:
time: 205 us; the launch traced here: 204 us
  waiting for transfers between devices  123 us (60%)
  local copies, waits for them, and re-layouts  28.7 us (14%)
  starting transfers between devices  18.5 us (9%)
  matrix products  14.1 us (7%)
  between operations  13.8 us (7%)
  other arithmetic  4.53 us (2%)
    reduce_scatter x1, waiting for transfers between devices, body(): out = lax.psum_scatter(parts, 'x', scatter_dimension=0, tiled=True)[0]  57.9 us
    all_gather x1, waiting for transfers between devices, body(): wu = lax.all_gather(w_up[0], 'x', axis=0)  38.4 us
    all_gather x1, waiting for transfers between devices, body(): wg = lax.all_gather(w_gate[0], 'x', axis=0)  20.2 us
    all_to_all x1, starting transfers between devices, body(): recv = lax.all_to_all(send, PLANE, 0, 0, tiled=True)  18.4 us
    dot_general x2, matrix products, body(): lax.dot_general(toks, d, (((0,), (0,)), ((), ())), preferred_element_type...  9.9 us
    reshape x2, local copies, waits for them, and re-layouts, body(): total.astype(jnp.bfloat16).reshape(width, planes, -1)  7.63 us
    all_to_all x1, waiting for transfers between devices, body(): recv = lax.all_to_all(send, PLANE, 0, 0, tiled=True)  4.93 us
    unnamed x13, local copies, waits for them, and re-layouts  4.63 us
  transfers between devices with their start and end apart: 4, of which 4 were waited for; matrix products, arithmetic and copies ran while one was open for 6% of the time, Pallas kernels for 1%

profile of v1, /device:TPU:1, one launch (start us, length us, event | category | flops | bytes accessed | tf_op | source)
XLA Modules:
  0.0 203.9 jit_solution(5050372723025498823)
XLA Ops:
  7.2 0.0 all-gather.5.cloned.1.call-start
  7.2 0.7 all-gather.5.cloned.1.call-update
  7.9 0.8 copy.17.probs_ref
  8.7 0.0 copy-start
  8.7 1.4 copy-done
  10.1 1.1 copy-done.1
  11.2 0.7 copy-done.2
  11.9 0.7 copy-done.3
  12.5 1.5 pack_rows.1
  14.0 2.7 %reshape.28 = bf16[128,4,3072]{2,1,0:T(4,128)(2,1)} reshape(bf16[2,256,3072]{2,1,0:T(8,128)(2,1)S(1)} %pack_rows.1) | data formatting | bytes 6291456 | tf_op jit(solution)/shard_map/reshape | solution.py:76
  16.7 18.4 %all-to-all-start = ((bf16[128,4,3072]{2,1,0:T(4,128)(2,1)}), bf16[128,4,3072]{2,1,0:T(4,128)(2,1)S(1)}, u32[]{:S(2)}, u32[]{:S(2)}) async-start(bf16[128,4,3072]{2,1,0:T(4,128)(2,1)} %reshape.28), calls=%async_computation | async-start | bytes 6291456 | tf_op jit(solution)/shard_map/all_to_all | solution.py:77
  35.2 0.0 all-gather.3.cloned.1.call-start
  35.2 0.7 all-gather.3.cloned.1.call-update
  35.9 0.0 reduce-scatter.2.cloned.1.call-start
  36.0 20.2 %all-gather.5.cloned.1.call-done = bf16[4,2560,128]{2,1,0:T(8,128)(2,1)} async-done(((bf16[1,2560,128]{2,1,0:T(8,128)(2,1)}), bf16[4,2560,128]{2,1,0:T(8,128)(2,1)}) %all-gather.5.cloned.1.call-update) | async-done | bytes 2621456 | tf_op jit(solution)/shard_map/all_gather | solution.py:60
  56.1 4.4 %copy.19 = bf16[4,2560,128]{1,2,0:T(8,128)(2,1)} copy(bf16[4,2560,128]{2,1,0:T(8,128)(2,1)} %all-gather.5.cloned.1.call-done) | data formatting | bytes 5242880 | tf_op jit(solution)/shard_map/all_gather | solution.py:60
  60.6 38.4 %all-gather.3.cloned.1.call-done = bf16[4,2560,128]{2,1,0:T(8,128)(2,1)} async-done(((bf16[1,2560,128]{2,1,0:T(8,128)(2,1)}), bf16[4,2560,128]{2,1,0:T(8,128)(2,1)}) %all-gather.3.cloned.1.call-update) | async-done | bytes 2621456 | tf_op jit(solution)/shard_map/all_gather | solution.py:61
  98.9 4.4 %copy.18 = bf16[4,2560,128]{1,2,0:T(8,128)(2,1)} copy(bf16[4,2560,128]{2,1,0:T(8,128)(2,1)} %all-gather.3.cloned.1.call-done) | data formatting | bytes 5242880 | tf_op jit(solution)/shard_map/all_gather | solution.py:61
  103.4 4.9 %all-to-all-done = bf16[128,4,3072]{2,1,0:T(4,128)(2,1)S(1)} async-done(((bf16[128,4,3072]{2,1,0:T(4,128)(2,1)}), bf16[128,4,3072]{2,1,0:T(4,128)(2,1)S(1)}, u32[]{:S(2)}, u32[]{:S(2)}) %all-to-all-start) | async-done | bytes 3145760 | tf_op jit(solution)/shard_map/all_to_all | solution.py:77
  108.3 2.4 %reshape.29 = bf16[512,3072]{1,0:T(8,128)(2,1)} reshape(bf16[128,4,3072]{2,1,0:T(4,128)(2,1)S(1)} %all-to-all-done) | data formatting | bytes 6291456 | tf_op jit(solution)/shard_map/reshape | solution.py:78
  110.7 4.2 %fusion.2 = f32[512,512]{1,0:T(8,128)S(1)} fusion(bf16[2560,512]{0,1:T(8,128)(2,1)} %bitcast.28, bf16[512,3072]{1,0:T(8,128)(2,1)} %reshape.29), kind=kOutput, calls=%fused_computation.5 | convolution fusion | flops 1342177280 | bytes 6291456 | tf_op jit(solution)/shard_map/dot_general | solution.py:83
  114.9 0.0 copy-done.4
  114.9 0.0 copy-start.5
  114.9 3.1 %convolution_convert_fusion = bf16[2560,512]{0,1:T(8,128)(2,1)} fusion(bf16[512,3072]{1,0:T(8,128)(2,1)S(1)} %copy-done.4, f32[512,512]{1,0:T(8,128)S(1)} %fusion.2), kind=kOutput, calls=%fused_computation.1 | convolution fusion | flops 1345323008 | bytes 6815744 | tf_op jit(solution)/shard_map/dot_general | solution.py:91
  118.1 0.0 copy-done.5
  118.1 6.7 %convolution_convert_fusion.1 = bf16[2560,512]{0,1:T(8,128)(2,1)} fusion(bf16[512,3072]{1,0:T(8,128)(2,1)S(1)} %copy-done.4, bf16[2560,512]{0,1:T(8,128)(2,1)} %bitcast.29, f32[512,512]{1,0:T(8,128)} %copy-done.5), kind=kOutput, calls=%fused_computation.2 | convolution fusion | flops 2688548864 | bytes 12058624 | tf_op jit(solution)/shard_map/dot_general | solution.py:91
  124.8 3.2 %copy.20 = bf16[2560,4,128]{2,0,1:T(8,128)(2,1)S(1)} copy(bf16[2560,4,128]{0,2,1:T(8,128)(2,1)} %bitcast.31) | data formatting | bytes 5242880 | tf_op jit(solution)/shard_map/reshape | solution.py:94
  128.1 4.4 %copy.21 = bf16[2560,4,128]{2,0,1:T(8,128)(2,1)} copy(bf16[2560,4,128]{0,2,1:T(8,128)(2,1)} %bitcast.30) | data formatting | bytes 5242880 | tf_op jit(solution)/shard_map/reshape | solution.py:94
  132.5 4.5 %pad_maximum_fusion = bf16[4,2,2560,128]{3,2,1,0:T(8,128)(2,1)} fusion(bf16[4,1,2560,128]{3,2,1,0:T(8,128)(2,1)} %bitcast.27, bf16[4,1,2560,128]{3,2,1,0:T(8,128)(2,1)S(1)} %bitcast.26), kind=kLoop, calls=%fused_computation | loop fusion | flops 2621440 | bytes 10485760 | tf_op jit(solution)/shard_map/stack | solution.py:95
  137.0 0.0 reduce-scatter.2.cloned.1.call-update
  137.0 57.9 %reduce-scatter.2.cloned.1.call-done = bf16[1,2,2560,128]{3,2,1,0:T(8,128)(2,1)} async-done(((bf16[4,2,2560,128]{3,2,1,0:T(8,128)(2,1)}), bf16[1,2,2560,128]{3,2,1,0:T(8,128)(2,1)}) %reduce-scatter.2.cloned.1.call-update) | async-done | bytes 1310736 | tf_op jit(solution)/shard_map/reduce_scatter | solution.py:96
  194.9 2.4 %slice_bitcast_fusion = (bf16[1,2560,128]{2,1,0:T(8,128)(2,1)}, bf16[1,2560,128]{2,1,0:T(8,128)(2,1)}) fusion(bf16[1,2,2560,128]{3,2,1,0:T(8,128)(2,1)} %reduce-scatter.2.cloned.1.call-done), kind=kLoop, calls=%fused_computation.17 | loop fusion | bytes 2621440 | tf_op jit(solution)/shard_map/slice | solution.py:97
  (4 shorter events, 0.0 us)
Async XLA Ops:
  7.2 49.0 %all-gather.5.cloned.1.call-start = ((), (), s32[]{:S(2)}) async-start(), calls=%async_computation.3 | async-start | bytes 3276800 | tf_op jit(solution)/shard_map/all_gather | solution.py:60
  8.7 1.4 copy-start
  10.1 1.1 copy-start.1
  11.2 0.7 copy-start.2
  11.9 0.7 copy-start.3
  16.7 91.5 %all-to-all-start = ((bf16[128,4,3072]{2,1,0:T(4,128)(2,1)}), bf16[128,4,3072]{2,1,0:T(4,128)(2,1)S(1)}, u32[]{:S(2)}, u32[]{:S(2)}) async-start(bf16[128,4,3072]{2,1,0:T(4,128)(2,1)} %reshape.28), calls=%async_computation | async-start | bytes 6291456 | tf_op jit(solution)/shard_map/all_to_all | solution.py:77
  35.2 63.8 %all-gather.3.cloned.1.call-start = ((), (), s32[]{:S(2)}) async-start(), calls=%async_computation.2 | async-start | bytes 3276800 | tf_op jit(solution)/shard_map/all_gather | solution.py:61
  35.9 159.0 %reduce-scatter.2.cloned.1.call-start = ((), (), s32[]{:S(2)}) async-start(), calls=%async_computation.4 | async-start | bytes 6553600 | tf_op jit(solution)/shard_map/reduce_scatter | solution.py:96
  110.7 4.2 %copy-start.4 = (bf16[512,3072]{1,0:T(8,128)(2,1)S(1)}, bf16[512,3072]{1,0:T(8,128)(2,1)}, u32[]{:S(2)}) copy-start(bf16[512,3072]{1,0:T(8,128)(2,1)} %reshape.29) | copy-start | bytes 9437188
  114.9 3.2 %copy-start.5 = (f32[512,512]{1,0:T(8,128)}, f32[512,512]{1,0:T(8,128)S(1)}, u32[]{:S(2)}) copy-start(f32[512,512]{1,0:T(8,128)S(1)} %fusion.2) | copy-start | bytes 3145732
Sparse Core Ops, SparseCore 0:
  10.1 45.9 all-gather.4
  58.2 40.6 all-gather.2
  137.2 57.7 reduce-scatter.1

commit v2 on v1

--- a/solution.py
+++ b/solution.py
@@ -52,11 +52,67 @@
     out_ref[1, :, width:] = acts[:, half:]
 
 
+def slice_kernel(which_ref, rows_ref, act_ref, wg_ref, wu_ref, gate_ref, up_ref):
+    hidden = act_ref.shape[1]
+    toks = rows_ref[...]
+    pair = jnp.concatenate([wg_ref[0], wu_ref[0]], axis=1)
+    both = jnp.dot(toks, pair, preferred_element_type=jnp.float32)
+    gate, up = both[:, :hidden], both[:, hidden:]
+    upstream = act_ref[...].astype(jnp.float32)
+    sig = 1.0 / (1.0 + jnp.exp(-gate))
+    d_up = upstream * gate * sig
+    d_gate = upstream * up * sig * (1.0 + gate * (1.0 - sig))
+    d = jnp.concatenate([d_gate, d_up], axis=1).astype(jnp.bfloat16)
+    total = lax.dot_general(
+        toks, d, (((0,), (0,)), ((), ())), preferred_element_type=jnp.float32
+    )
+    gate_ref[0] = total[:, :hidden].astype(gate_ref.dtype)
+    up_ref[0] = total[:, hidden:].astype(up_ref.dtype)
+
+
+def slice_grads(which, recv, wg, wu, dtype):
+    rows, columns = recv.shape
+    _, width, hidden = wg.shape
+    return pl.pallas_call(
+        slice_kernel,
+        grid_spec=pltpu.PrefetchScalarGridSpec(
+            num_scalar_prefetch=1,
+            grid=(1,),
+            in_specs=[
+                pl.BlockSpec((rows, width), lambda i, w: (0, 0)),
+                pl.BlockSpec((rows, hidden), lambda i, w: (0, width // hidden + w[0])),
+                pl.BlockSpec((1, width, hidden), lambda i, w: (w[0], 0, 0)),
+                pl.BlockSpec((1, width, hidden), lambda i, w: (w[0], 0, 0)),
+            ],
+            out_specs=[pl.BlockSpec((1, width, hidden), lambda i, w: (0, 0, 0))] * 2,
+        ),
+        out_shape=[jax.ShapeDtypeStruct((1, width, hidden), dtype)] * 2,
+        compiler_params=pltpu.CompilerParams(vmem_limit_bytes=48 * 2**20),
+        cost_estimate=pl.CostEstimate(
+            flops=8 * rows * width * hidden,
+            bytes_accessed=2 * rows * width + 8 * width * hidden,
+            transcendentals=rows * hidden,
+        ),
+        name="slice_grads",
+    )(which.reshape(1), recv, recv, wg, wu)
+
+
+def moved(block, distance):
+    planes = lax.axis_size("x")
+    return lax.ppermute(block, "x", [(i, (i + distance) % planes) for i in range(planes)])
+
+
+def add(*blocks):
+    return sum(block.astype(jnp.float32) for block in blocks)
+
+
 def body(tokens, expert_ids, gate_probs, act_grad, hot_experts, w_gate, w_up):
     width = tokens.shape[1]
     ff = act_grad.shape[2]
     copies = lax.axis_size("yh")
     experts = lax.axis_size(EXPERT)
+    planes = lax.axis_size("x")
+    here = lax.axis_index("x")
     wg = lax.all_gather(w_gate[0], "x", axis=0)
     wu = lax.all_gather(w_up[0], "x", axis=0)
     send = pl.pallas_call(
@@ -76,25 +132,23 @@
     send = send.reshape(copies * experts, SLOTS, -1)
     recv = lax.all_to_all(send, PLANE, 0, 0, tiled=True)
     recv = recv.reshape(copies * experts * SLOTS, -1)
-    toks = recv[:, :width]
-    upstream = recv[:, width:].astype(jnp.float32)
-    wg = jnp.swapaxes(wg, 0, 1).reshape(width, -1)
-    wu = jnp.swapaxes(wu, 0, 1).reshape(width, -1)
-    gate = jnp.dot(toks, wg, preferred_element_type=jnp.float32)
-    up = jnp.dot(toks, wu, preferred_element_type=jnp.float32)
-    sig = jax.nn.sigmoid(gate)
-    d_up = (upstream * gate * sig).astype(jnp.bfloat16)
-    d_gate = (upstream * up * sig * (1.0 + gate * (1.0 - sig))).astype(jnp.bfloat16)
-    planes = lax.axis_size("x")
-    parts = []
-    for d in (d_gate, d_up):
-        total = lax.dot_general(
-            toks, d, (((0,), (0,)), ((), ())), preferred_element_type=jnp.float32
-        )
-        parts.append(jnp.swapaxes(total.astype(jnp.bfloat16).reshape(width, planes, -1), 0, 1))
-    parts = jnp.stack(parts, 1)
-    out = lax.psum_scatter(parts, "x", scatter_dimension=0, tiled=True)[0]
-    return (out[0:1], out[1:2])
+
+    def part(offset, dtype=jnp.bfloat16):
+        return slice_grads((here + offset) % planes, recv, wg, wu, dtype)
+
+    far_gate, far_up = part(2)
+    far_gate = moved(far_gate, 1)
+    far_up = moved(far_up, -1)
+    right_gate, right_up = part(1)
+    from_left_up = moved(right_up, 1)
+    left_gate, left_up = part(3)
+    from_right_gate = moved(left_gate, -1)
+    own_gate, own_up = part(0, jnp.float32)
+    from_left_gate = moved(add(right_gate, far_gate).astype(jnp.bfloat16), 1)
+    from_right_up = moved(add(left_up, far_up).astype(jnp.bfloat16), -1)
+    grad_gate = add(own_gate, from_right_gate, from_left_gate)
+    grad_up = add(own_up, from_left_up, from_right_up)
+    return (grad_gate.astype(jnp.bfloat16), grad_up.astype(jnp.bfloat16))
 
 
 def solution(mesh):

time: 205 us -> 180 us (0.88); the launches traced: 204 us -> 176 us
  waiting for transfers between devices: 123 us -> 88.2 us
  Pallas kernels: 1.51 us -> 22 us
  starting transfers between devices: 18.5 us -> 36.8 us
  local copies, waits for them, and re-layouts: 28.7 us -> 11.5 us
  matrix products: 14.1 us -> 0 us
    all_to_all x1, waiting for transfers between devices: 4.93 us -> 72.3 us  [body(): recv = lax.all_to_all(send, PLANE, 0, 0, tiled=True)]
    reduce_scatter x1 -> x0, waiting for transfers between devices: 57.9 us -> none  [body(): out = lax.psum_scatter(parts, 'x', scatter_dimension=0, tiled=True)[0]]
    all_gather x1, waiting for transfers between devices: 38.4 us -> 0.01 us  [body(): wu = lax.all_gather(w_up[0], 'x', axis=0)]
    pallas_call x0 -> x4, Pallas kernels: none -> 20.5 us  [slice_grads(): pl.pallas_call(slice_kernel, grid_spec=pltpu.PrefetchScalarGridSpec(num_s...]
    all_gather x1, waiting for transfers between devices: 20.2 us -> 0.01 us  [body(): wg = lax.all_gather(w_gate[0], 'x', axis=0)]
    ppermute x0 -> x6, starting transfers between devices: none -> 18.2 us  [moved(): lax.ppermute(block, 'x', [(i, (i + distance) % planes) for i in range(pla...]
    ppermute x0 -> x6, waiting for transfers between devices: none -> 14.5 us  [moved(): lax.ppermute(block, 'x', [(i, (i + distance) % planes) for i in range(pla...]
    dot_general x3 -> x0, matrix products: 14.1 us -> none  [the longest x2 9.9 us: body(): lax.dot_general(toks, d, (((0,), (0,)), ((), ())), preferred_element_type...]
  transfers between devices with their start and end apart: 4 -> 9, of which waited for: 4 -> 3; matrix products, arithmetic and copies ran while one was open for 6% -> 5% of each run, Pallas kernels for 1% -> 9%
where the time goes in v2:
time: 180 us; the launch traced here: 176 us
  waiting for transfers between devices  88.2 us (49%)
  starting transfers between devices  36.8 us (20%)
  Pallas kernels  22 us (12%)
  between operations  14.2 us (8%)
  local copies, waits for them, and re-layouts  11.5 us (6%)
  other arithmetic  3.58 us (2%)
    all_to_all x1, waiting for transfers between devices, body(): recv = lax.all_to_all(send, PLANE, 0, 0, tiled=True)  72.3 us
    pallas_call x4, Pallas kernels, slice_grads(): pl.pallas_call(slice_kernel, grid_spec=pltpu.PrefetchScalarGridSpec(num_s...  20.5 us
    all_to_all x1, starting transfers between devices, body(): recv = lax.all_to_all(send, PLANE, 0, 0, tiled=True)  18.4 us
    ppermute x6, starting transfers between devices, moved(): lax.ppermute(block, 'x', [(i, (i + distance) % planes) for i in range(pla...  18.2 us
    ppermute x6, waiting for transfers between devices, moved(): lax.ppermute(block, 'x', [(i, (i + distance) % planes) for i in range(pla...  14.5 us
    unnamed x13, local copies, waits for them, and re-layouts  6.37 us
  transfers between devices with their start and end apart: 9, of which 3 were waited for; matrix products, arithmetic and copies ran while one was open for 5% of the time, Pallas kernels for 9%

profile of v2, /device:TPU:1, one launch (start us, length us, event | category | flops | bytes accessed | tf_op | source)
XLA Modules:
  0.0 176.3 jit_solution(9765356798616207208)
XLA Ops:
  7.2 0.0 all-gather.3.cloned.1.call-start
  7.2 0.7 all-gather.3.cloned.1.call-update
  7.9 0.8 copy.10.probs_ref
  8.7 1.4 copy-done.2
  10.1 1.1 copy-done.3
  11.2 0.7 copy-done.4
  11.9 0.7 copy-done.5
  12.5 1.5 pack_rows.1
  14.0 2.7 %reshape.27 = bf16[128,4,3072]{2,1,0:T(4,128)(2,1)} reshape(bf16[2,256,3072]{2,1,0:T(8,128)(2,1)S(1)} %pack_rows.1) | data formatting | bytes 6291456 | tf_op jit(solution)/shard_map/reshape | solution.py:132
  16.7 18.4 %all-to-all-start = ((bf16[128,4,3072]{2,1,0:T(4,128)(2,1)}), bf16[128,4,3072]{2,1,0:T(4,128)(2,1)S(1)}, u32[]{:S(2)}, u32[]{:S(2)}) async-start(bf16[128,4,3072]{2,1,0:T(4,128)(2,1)} %reshape.27), calls=%async_computation | async-start | bytes 6291456 | tf_op jit(solution)/shard_map/all_to_all | solution.py:133
  35.2 0.0 all-gather.5.cloned.1.call-start
  35.2 0.7 all-gather.5.cloned.1.call-update
  35.9 72.3 %all-to-all-done = bf16[128,4,3072]{2,1,0:T(4,128)(2,1)S(1)} async-done(((bf16[128,4,3072]{2,1,0:T(4,128)(2,1)}), bf16[128,4,3072]{2,1,0:T(4,128)(2,1)S(1)}, u32[]{:S(2)}, u32[]{:S(2)}) %all-to-all-start) | async-done | bytes 3145760 | tf_op jit(solution)/shard_map/all_to_all | solution.py:133
  108.3 2.4 %reshape.28.rows_ref.act_ref = bf16[512,3072]{1,0:T(8,128)(2,1)} reshape(bf16[128,4,3072]{2,1,0:T(4,128)(2,1)S(1)} %all-to-all-done) | data formatting | bytes 6291456 | tf_op jit(solution)/shard_map/reshape | solution.py:134
  110.7 1.7 copy-done
  112.4 5.9 %slice_grads.7 = (bf16[1,2560,128]{2,1,0:T(8,128)(2,1)S(1)}, bf16[1,2560,128]{2,1,0:T(8,128)(2,1)}) custom-call(s32[1]{0:T(128)} %bitcast.6.which_ref, bf16[512,3072]{1,0:T(8,128)(2,1)} %reshape.28.rows_ref.act_ref, bf16[512,3072]{1,0:T(8,128)(2,1)} %reshape.28.rows_ref.act_ref, bf16[4,2560,128]{2,1,0:T(8,128)(2,1)S(1)} %copy-done, ...), custom_call_target="tpu_custom_call" | custom-call | flops 1342177280 | bytes 5242880 | tf_op jit(solution)/shard_map/slice_grads/pallas_call | solution.py:76
  118.3 4.4 %collective-permute-start.4 = (bf16[1,2560,128]{2,1,0:T(8,128)(2,1)}, bf16[1,2560,128]{2,1,0:T(8,128)(2,1)}, u32[]{:S(2)}, u32[]{:S(2)}) collective-permute-start(bf16[1,2560,128]{2,1,0:T(8,128)(2,1)} %get-tuple-element.17), channel_id=1, source_target_pairs={{0,192},{64,0},{128,64},{192,128},{1,193},{65,1},{129,65},{193,129... | collective-permute-start | bytes 1966088 | tf_op jit(solution)/shard_map/ppermute | solution.py:102
  122.7 1.9 %collective-permute-start.1 = (bf16[1,2560,128]{2,1,0:T(8,128)(2,1)S(1)}, bf16[1,2560,128]{2,1,0:T(8,128)(2,1)S(1)}, u32[]{:S(2)}, u32[]{:S(2)}) collective-permute-start(bf16[1,2560,128]{2,1,0:T(8,128)(2,1)S(1)} %get-tuple-element.13), channel_id=1, source_target_pairs={{0,64},{64,128},{128,192},{192,0},{1,65},{65,129},{129,193},{193,1... | collective-permute-start | bytes 1966088 | tf_op jit(solution)/shard_map/ppermute | solution.py:102
  124.6 4.9 %slice_grads.6 = (bf16[1,2560,128]{2,1,0:T(8,128)(2,1)S(1)}, bf16[1,2560,128]{2,1,0:T(8,128)(2,1)S(1)}) custom-call(s32[1]{0:T(128)} %bitcast.5.which_ref, bf16[512,3072]{1,0:T(8,128)(2,1)} %reshape.28.rows_ref.act_ref, bf16[512,3072]{1,0:T(8,128)(2,1)} %reshape.28.rows_ref.act_ref, bf16[4,2560,128]{2,1,0:T(8,128)(2,1)S(1)} %copy-done.1, ...), custom_call_target="tpu_custom_call" | custom-call | flops 1342177280 | bytes 5242880 | tf_op jit(solution)/shard_map/slice_grads/pallas_call | solution.py:76
  129.5 2.1 %collective-permute-start.3 = (bf16[1,2560,128]{2,1,0:T(8,128)(2,1)S(1)}, bf16[1,2560,128]{2,1,0:T(8,128)(2,1)S(1)}, u32[]{:S(2)}, u32[]{:S(2)}) collective-permute-start(bf16[1,2560,128]{2,1,0:T(8,128)(2,1)S(1)} %get-tuple-element.15), channel_id=1, source_target_pairs={{0,64},{64,128},{128,192},{192,0},{1,65},{65,129},{129,193},{193,1... | collective-permute-start | bytes 1966088 | tf_op jit(solution)/shard_map/ppermute | solution.py:102
  131.6 4.9 %slice_grads.5 = (bf16[1,2560,128]{2,1,0:T(8,128)(2,1)S(1)}, bf16[1,2560,128]{2,1,0:T(8,128)(2,1)S(1)}) custom-call(s32[1]{0:T(128)} %bitcast.4.which_ref, bf16[512,3072]{1,0:T(8,128)(2,1)} %reshape.28.rows_ref.act_ref, bf16[512,3072]{1,0:T(8,128)(2,1)} %reshape.28.rows_ref.act_ref, bf16[4,2560,128]{2,1,0:T(8,128)(2,1)S(1)} %copy-done.1, ...), custom_call_target="tpu_custom_call" | custom-call | flops 1342177280 | bytes 5242880 | tf_op jit(solution)/shard_map/slice_grads/pallas_call | solution.py:76
  136.5 4.6 %collective-permute-start = (bf16[1,2560,128]{2,1,0:T(8,128)(2,1)S(1)}, bf16[1,2560,128]{2,1,0:T(8,128)(2,1)S(1)}, u32[]{:S(2)}, u32[]{:S(2)}) collective-permute-start(bf16[1,2560,128]{2,1,0:T(8,128)(2,1)S(1)} %get-tuple-element.11), channel_id=1, source_target_pairs={{0,192},{64,0},{128,64},{192,128},{1,193},{65,1},{129,65},{193,129... | collective-permute-start | bytes 1966088 | tf_op jit(solution)/shard_map/ppermute | solution.py:102
  141.1 4.9 %slice_grads.4 = (f32[1,2560,128]{2,1,0:T(8,128)S(1)}, f32[1,2560,128]{2,1,0:T(8,128)S(1)}) custom-call(s32[1]{0:T(128)} %bitcast.which_ref, bf16[512,3072]{1,0:T(8,128)(2,1)} %reshape.28.rows_ref.act_ref, bf16[512,3072]{1,0:T(8,128)(2,1)} %reshape.28.rows_ref.act_ref, bf16[4,2560,128]{2,1,0:T(8,128)(2,1)S(1)} %copy-done.1, ...), custom_call_target="tpu_custom_call" | custom-call | flops 1342177280 | bytes 5242880 | tf_op jit(solution)/shard_map/slice_grads/pallas_call | solution.py:76
  146.0 0.0 collective-permute-done.4
  146.0 1.3 add_convert_fusion.1
  147.3 3.4 %collective-permute-start.5 = (bf16[1,2560,128]{2,1,0:T(8,128)(2,1)S(1)}, bf16[1,2560,128]{2,1,0:T(8,128)(2,1)S(1)}, u32[]{:S(2)}, u32[]{:S(2)}) collective-permute-start(bf16[1,2560,128]{2,1,0:T(8,128)(2,1)S(1)} %add_convert_fusion.1), channel_id=1, source_target_pairs={{0,192},{64,0},{128,64},{192,128},{1,193},{65,1},{129,65},{193,129... | collective-permute-start | bytes 1966088 | tf_op jit(solution)/shard_map/ppermute | solution.py:102
  150.7 0.2 add_convert_fusion.3
  150.9 1.9 %collective-permute-start.2 = (bf16[1,2560,128]{2,1,0:T(8,128)(2,1)S(1)}, bf16[1,2560,128]{2,1,0:T(8,128)(2,1)S(1)}, u32[]{:S(2)}, u32[]{:S(2)}) collective-permute-start(bf16[1,2560,128]{2,1,0:T(8,128)(2,1)S(1)} %add_convert_fusion.3), channel_id=1, source_target_pairs={{0,64},{64,128},{128,192},{192,0},{1,65},{65,129},{129,193},{193,1... | collective-permute-start | bytes 1966088 | tf_op jit(solution)/shard_map/ppermute | solution.py:102
  152.8 1.9 %collective-permute-done.3 = bf16[1,2560,128]{2,1,0:T(8,128)(2,1)S(1)} collective-permute-done((bf16[1,2560,128]{2,1,0:T(8,128)(2,1)S(1)}, bf16[1,2560,128]{2,1,0:T(8,128)(2,1)S(1)}, u32[]{:S(2)}, u32[]{:S(2)}) %collective-permute-start.3) | collective-permute-done | bytes 655392 | tf_op jit(solution)/shard_map/ppermute | solution.py:102
  154.6 12.6 %collective-permute-done.5 = bf16[1,2560,128]{2,1,0:T(8,128)(2,1)S(1)} collective-permute-done((bf16[1,2560,128]{2,1,0:T(8,128)(2,1)S(1)}, bf16[1,2560,128]{2,1,0:T(8,128)(2,1)S(1)}, u32[]{:S(2)}, u32[]{:S(2)}) %collective-permute-start.5) | collective-permute-done | bytes 655392 | tf_op jit(solution)/shard_map/ppermute | solution.py:102
  167.3 1.1 add_convert_fusion
  168.4 1.1 add_convert_fusion.2
  (12 shorter events, 0.0 us)
Async XLA Ops:
  7.2 103.5 %all-gather.3.cloned.1.call-start = ((), (), s32[]{:S(2)}) async-start(), calls=%async_computation.1 | async-start | bytes 3276800 | tf_op jit(solution)/shard_map/all_gather | solution.py:116
  8.7 1.4 copy-start.2
  10.1 1.1 copy-start.3
  11.2 0.7 copy-start.4
  11.9 0.7 copy-start.5
  16.7 91.5 %all-to-all-start = ((bf16[128,4,3072]{2,1,0:T(4,128)(2,1)}), bf16[128,4,3072]{2,1,0:T(4,128)(2,1)S(1)}, u32[]{:S(2)}, u32[]{:S(2)}) async-start(bf16[128,4,3072]{2,1,0:T(4,128)(2,1)} %reshape.27), calls=%async_computation | async-start | bytes 6291456 | tf_op jit(solution)/shard_map/all_to_all | solution.py:133
  35.2 75.5 %all-gather.5.cloned.1.call-start = ((), (), s32[]{:S(2)}) async-start(), calls=%async_computation.2 | async-start | bytes 3276800 | tf_op jit(solution)/shard_map/all_gather | solution.py:117
  110.7 1.7 copy-start
  112.4 12.2 %copy-start.1 = (bf16[4,2560,128]{2,1,0:T(8,128)(2,1)S(1)}, bf16[4,2560,128]{2,1,0:T(8,128)(2,1)}, u32[]{:S(2)}) copy-start(bf16[4,2560,128]{2,1,0:T(8,128)(2,1)} %all-gather.3.cloned.1.call-done.wg_ref) | copy-start | bytes 7864324
  118.3 27.7 %collective-permute-start.4 = (bf16[1,2560,128]{2,1,0:T(8,128)(2,1)}, bf16[1,2560,128]{2,1,0:T(8,128)(2,1)}, u32[]{:S(2)}, u32[]{:S(2)}) collective-permute-start(bf16[1,2560,128]{2,1,0:T(8,128)(2,1)} %get-tuple-element.17), channel_id=1, source_target_pairs={{0,192},{64,0},{128,64},{192,128},{1,193},{65,1},{129,65},{193,129... | collective-permute-start | bytes 1966088 | tf_op jit(solution)/shard_map/ppermute | solution.py:102
  122.7 28.0 %collective-permute-start.1 = (bf16[1,2560,128]{2,1,0:T(8,128)(2,1)S(1)}, bf16[1,2560,128]{2,1,0:T(8,128)(2,1)S(1)}, u32[]{:S(2)}, u32[]{:S(2)}) collective-permute-start(bf16[1,2560,128]{2,1,0:T(8,128)(2,1)S(1)} %get-tuple-element.13), channel_id=1, source_target_pairs={{0,64},{64,128},{128,192},{192,0},{1,65},{65,129},{129,193},{193,1... | collective-permute-start | bytes 1966088 | tf_op jit(solution)/shard_map/ppermute | solution.py:102
  129.5 25.1 %collective-permute-start.3 = (bf16[1,2560,128]{2,1,0:T(8,128)(2,1)S(1)}, bf16[1,2560,128]{2,1,0:T(8,128)(2,1)S(1)}, u32[]{:S(2)}, u32[]{:S(2)}) collective-permute-start(bf16[1,2560,128]{2,1,0:T(8,128)(2,1)S(1)} %get-tuple-element.15), channel_id=1, source_target_pairs={{0,64},{64,128},{128,192},{192,0},{1,65},{65,129},{129,193},{193,1... | collective-permute-start | bytes 1966088 | tf_op jit(solution)/shard_map/ppermute | solution.py:102
  136.5 31.8 %collective-permute-start = (bf16[1,2560,128]{2,1,0:T(8,128)(2,1)S(1)}, bf16[1,2560,128]{2,1,0:T(8,128)(2,1)S(1)}, u32[]{:S(2)}, u32[]{:S(2)}) collective-permute-start(bf16[1,2560,128]{2,1,0:T(8,128)(2,1)S(1)} %get-tuple-element.11), channel_id=1, source_target_pairs={{0,192},{64,0},{128,64},{192,128},{1,193},{65,1},{129,65},{193,129... | collective-permute-start | bytes 1966088 | tf_op jit(solution)/shard_map/ppermute | solution.py:102
  147.3 20.0 %collective-permute-start.5 = (bf16[1,2560,128]{2,1,0:T(8,128)(2,1)S(1)}, bf16[1,2560,128]{2,1,0:T(8,128)(2,1)S(1)}, u32[]{:S(2)}, u32[]{:S(2)}) collective-permute-start(bf16[1,2560,128]{2,1,0:T(8,128)(2,1)S(1)} %add_convert_fusion.1), channel_id=1, source_target_pairs={{0,192},{64,0},{128,64},{192,128},{1,193},{65,1},{129,65},{193,129... | collective-permute-start | bytes 1966088 | tf_op jit(solution)/shard_map/ppermute | solution.py:102
  150.9 17.5 %collective-permute-start.2 = (bf16[1,2560,128]{2,1,0:T(8,128)(2,1)S(1)}, bf16[1,2560,128]{2,1,0:T(8,128)(2,1)S(1)}, u32[]{:S(2)}, u32[]{:S(2)}) collective-permute-start(bf16[1,2560,128]{2,1,0:T(8,128)(2,1)S(1)} %add_convert_fusion.3), channel_id=1, source_target_pairs={{0,64},{64,128},{128,192},{192,0},{1,65},{65,129},{129,193},{193,1... | collective-permute-start | bytes 1966088 | tf_op jit(solution)/shard_map/ppermute | solution.py:102
Sparse Core Ops, SparseCore 0:
  10.1 45.9 all-gather.2
  58.2 40.6 all-gather.4

commit v3 on v2

v3 whole, which is shorter than its diff:
```python
import functools

import jax
import jax.numpy as jnp
from jax import lax
from jax.experimental import pallas as pl
from jax.experimental.pallas import tpu as pltpu
from jax.sharding import Mesh, PartitionSpec as P

CAP = 2
OVF = 2
SLOTS = CAP + OVF
VMEM = 60 * 2**20
SLICE_VMEM = 60 * 2**20
AXES = ("yh", "x", "yl", "z", "c")
PLANE = ("yh", "yl", "z", "c")
EXPERT = ("yl", "z", "c")


def pack_kernel(ids_ref, probs_ref, hot_ref, tok_ref, act_ref, out_ref):
    top, block = ids_ref.shape
    experts = out_ref.shape[0] // 2
    rows = experts * SLOTS
    width = tok_ref.shape[1]
    half = out_ref.shape[2] - width
    row = lax.broadcasted_iota(jnp.int32, (rows, block), 0)
    expert, slot = row // SLOTS, row % SLOTS
    hits = [ids_ref[k : k + 1, :] == expert for k in range(top)]
    named = hits[0]
    for hit in hits[1:]:
        named = named | hit
    before = lax.broadcasted_iota(jnp.int32, (block, block), 0) < lax.broadcasted_iota(
        jnp.int32, (block, block), 1
    )
    position = jnp.dot(
        jnp.where(named, 1.0, 0.0).astype(jnp.bfloat16),
        jnp.where(before, 1.0, 0.0).astype(jnp.bfloat16),
        preferred_element_type=jnp.float32,
    ).astype(jnp.int32)
    hots = hot_ref.shape[1]
    owner = lax.broadcasted_iota(jnp.int32, (rows, hots), 0) // SLOTS
    hot = jnp.max(jnp.where(hot_ref[...] == owner, 1, 0), axis=1, keepdims=True)
    kept = named & (position == slot) & ((slot < CAP) | (hot > 0))
    pick = jnp.where(kept, 1.0, 0.0).astype(jnp.bfloat16)
    toks = jnp.dot(pick, tok_ref[...], preferred_element_type=jnp.float32)
    toks = toks.astype(jnp.bfloat16).reshape(experts, SLOTS, width)
    out_ref[:experts, :, :width] = toks
    out_ref[experts:, :, :width] = toks
    acts = jnp.zeros((rows, act_ref.shape[2]), jnp.float32)
    scale = jnp.zeros((rows, block), jnp.float32)
    for k in range(top):
        chosen = jnp.where(kept & hits[k], 1.0, 0.0)
        acts += jnp.dot(chosen.astype(jnp.bfloat16), act_ref[k], preferred_element_type=jnp.float32)
        scale += chosen * probs_ref[k : k + 1, :]
    acts = jnp.sum(scale, axis=1, keepdims=True) * acts
    acts = acts.astype(jnp.bfloat16)
    out_ref[:experts, :, width:] = acts[:, :half].reshape(experts, SLOTS, half)
    out_ref[experts:, :, width:] = acts[:, half:].reshape(experts, SLOTS, half)


def pre_grads(toks, act, w_gate, w_up):
    hidden = act.shape[1]
    pair = jnp.concatenate([w_gate, w_up], axis=1)
    both = jnp.dot(toks, pair, preferred_element_type=jnp.float32)
    gate, up = both[:, :hidden], both[:, hidden:]
    upstream = act.astype(jnp.float32)
    sig = 1.0 / (1.0 + jnp.exp(-gate))
    d_up = upstream * gate * sig
    d_gate = upstream * up * sig * (1.0 + gate * (1.0 - sig))
    return jnp.concatenate([d_gate, d_up], axis=1).astype(jnp.bfloat16)


def store_grads(toks, d, gate_ref, up_ref):
    hidden = gate_ref.shape[2]
    total = lax.dot_general(
        toks, d, (((0,), (0,)), ((), ())), preferred_element_type=jnp.float32
    )
    gate_ref[0] = total[:, :hidden].astype(gate_ref.dtype)
    up_ref[0] = total[:, hidden:].astype(up_ref.dtype)


CHUNKS = 4


def slices_kernel(count, which_ref, recv_ref, *refs):
    weights, grads, (rows, sems) = refs[: 2 * count], refs[2 * count : -2], refs[-2:]
    width, hidden = weights[0].shape[1:]
    chunk = rows.shape[0] // CHUNKS
    parts = [pl.ds(c * chunk, chunk) for c in range(CHUNKS)]
    copies = [
        pltpu.make_async_copy(recv_ref.at[part], rows.at[part], sems.at[c])
        for c, part in enumerate(parts)
    ]
    for copy in copies:
        copy.start()
    d = [[] for _ in range(count)]
    for part, copy in zip(parts, copies):
        copy.wait()
        for k in range(count):
            start = pl.multiple_of(width + which_ref[k] * hidden, hidden)
            d[k].append(
                pre_grads(
                    rows[part, :width],
                    rows[part, pl.ds(start, hidden)],
                    weights[2 * k][0],
                    weights[2 * k + 1][0],
                )
            )
    for k in range(count):
        store_grads(rows[:, :width], jnp.concatenate(d[k]), *grads[2 * k : 2 * k + 2])


def slice_grads(which, recv, weights, dtype):
    shape = weights[0].shape
    w_size = weights[0].size * len(weights) // 2
    whole = pl.BlockSpec(shape, lambda i, w: (0, 0, 0))
    return pl.pallas_call(
        functools.partial(slices_kernel, len(weights) // 2),
        grid_spec=pltpu.PrefetchScalarGridSpec(
            num_scalar_prefetch=1,
            grid=(1,),
            in_specs=[pl.BlockSpec(memory_space=pl.ANY)] + [whole] * len(weights),
            out_specs=[whole] * len(weights),
            scratch_shapes=[
                pltpu.VMEM(recv.shape, recv.dtype),
                pltpu.SemaphoreType.DMA((CHUNKS,)),
            ],
        ),
        out_shape=[jax.ShapeDtypeStruct(shape, dtype)] * len(weights),
        compiler_params=pltpu.CompilerParams(vmem_limit_bytes=SLICE_VMEM),
        cost_estimate=pl.CostEstimate(
            flops=8 * recv.shape[0] * w_size,
            bytes_accessed=2 * recv.size + 8 * w_size,
            transcendentals=0,
        ),
        name="slice_grads",
    )(which, recv, *weights)


def moved(block, distance):
    planes = lax.axis_size("x")
    return lax.ppermute(block, "x", [(i, (i + distance) % planes) for i in range(planes)])


def add(*blocks):
    return sum(block.astype(jnp.float32) for block in blocks)


def body(tokens, expert_ids, gate_probs, act_grad, hot_experts, w_gate, w_up):
    width = tokens.shape[1]
    ff = act_grad.shape[2]
    copies = lax.axis_size("yh")
    experts = lax.axis_size(EXPERT)
    planes = lax.axis_size("x")
    here = lax.axis_index("x")
    send = pl.pallas_call(
        pack_kernel,
        out_shape=jax.ShapeDtypeStruct(
            (copies * experts, SLOTS, width + ff // copies), jnp.bfloat16
        ),
        compiler_params=pltpu.CompilerParams(vmem_limit_bytes=VMEM),
        name="pack_rows",
    )(
        expert_ids.T,
        gate_probs.T,
        hot_experts.reshape(1, -1),
        tokens,
        jnp.swapaxes(act_grad, 0, 1),
    )
    send, w_gate, w_up = lax.optimization_barrier((send, w_gate, w_up))
    recv = lax.all_to_all(send, PLANE, 0, 0, tiled=True)
    mine = (w_gate, w_up)
    theirs = {d: tuple(moved(w, -d) for w in mine) for d in (2, 1, 3)}
    at = jnp.stack([(here + d) % planes for d in range(planes)])

    recv, theirs = lax.optimization_barrier((recv.reshape(-1, recv.shape[2]), theirs))
    far_gate, far_up = slice_grads(at[2:3], recv, theirs[2], jnp.bfloat16)
    far_gate = moved(far_gate, 1)
    far_up = moved(far_up, -1)
    right_gate, right_up, left_gate, left_up = slice_grads(
        at[1::2], recv, theirs[1] + theirs[3], jnp.bfloat16
    )
    from_left_up = moved(right_up, 1)
    from_right_gate = moved(left_gate, -1)
    own_gate, own_up = slice_grads(at[0:1], recv, mine, jnp.float32)
    from_left_gate = moved(add(right_gate, far_gate).astype(jnp.bfloat16), 1)
    from_right_up = moved(add(left_up, far_up).astype(jnp.bfloat16), -1)
    grad_gate = add(own_gate, from_right_gate, from_left_gate)
    grad_up = add(own_up, from_left_up, from_right_up)
    return (grad_gate.astype(jnp.bfloat16), grad_up.astype(jnp.bfloat16))


def solution(mesh):
    grid = Mesh(mesh.devices.reshape(2, 4, 4, 8, 2), AXES)
    rows = P(AXES)
    weights = P(EXPERT, None, ("yh", "x"))
    return jax.shard_map(
        body,
        mesh=grid,
        in_specs=(rows, rows, rows, rows, P(), weights, weights),
        out_specs=(weights, weights),
        check_vma=False,
    )
```

time: 180 us -> 172 us (0.956)
  the two profiles are of different devices: /device:TPU:1 before, /device:TPU:30 now
where the time goes in v3:
time: 172 us; the launch traced here: 171 us
  waiting for transfers between devices  84.2 us (49%)
  starting transfers between devices  53.6 us (31%)
  Pallas kernels  26.7 us (16%)
  local copies, waits for them, and re-layouts  3.1 us (2%)
  other arithmetic  2.57 us (1%)
    ppermute x12, waiting for transfers between devices, moved(): lax.ppermute(block, 'x', [(i, (i + distance) % planes) for i in range(pla...  47.4 us
    all_to_all x1, waiting for transfers between devices, body(): recv = lax.all_to_all(send, PLANE, 0, 0, tiled=True)  36.8 us
    ppermute x12, starting transfers between devices, moved(): lax.ppermute(block, 'x', [(i, (i + distance) % planes) for i in range(pla...  36.3 us
    pallas_call x3, Pallas kernels, slice_grads(): pl.pallas_call(functools.partial(slices_kernel, len(weights) // 2), grid_...  21.9 us
    all_to_all x1, starting transfers between devices, body(): recv = lax.all_to_all(send, PLANE, 0, 0, tiled=True)  17.3 us
    pallas_call x1, Pallas kernels, body(): pl.pallas_call(pack_kernel, out_shape=jax.ShapeDtypeStruct((copies * expe...  4.86 us
  transfers between devices with their start and end apart: 13, of which 5 were waited for; matrix products, arithmetic and copies ran while one was open for 3% of the time, Pallas kernels for 9%

profile of v3, /device:TPU:30, one launch (start us, length us, event | category | flops | bytes accessed | tf_op | source)
XLA Modules:
  0.0 171.1 jit_solution(1995466836344410703)
XLA Ops:
  0.6 4.9 %pack_rows.1 = bf16[128,4,3072]{2,1,0:T(4,128)(2,1)} custom-call(s32[6,128]{1,0:T(8,128)} %bitcast.9, f32[6,128]{1,0:T(8,128)} %bitcast.10, s32[1,32]{1,0:T(1,128)} %bitcast.11, bf16[128,2560]{1,0:T(8,128)(2,1)} %tok_ref.1, bf16[6,128,1024]{2,1,0:T(8,128)(2,1)} %bitcast.8), custom_call_target="tpu_custom_call" | custom-call | tf_op jit(solution)/shard_map/pack_rows/pallas_call | solution.py:156
  5.5 17.3 %all-to-all-start = ((bf16[128,4,3072]{2,1,0:T(4,128)(2,1)}), bf16[128,4,3072]{2,1,0:T(4,128)(2,1)S(1)}, u32[]{:S(2)}, u32[]{:S(2)}) async-start(bf16[128,4,3072]{2,1,0:T(4,128)(2,1)} %pack_rows.1), calls=%async_computation | async-start | bytes 6291456 | tf_op jit(solution)/shard_map/all_to_all | solution.py:171
  22.9 2.7 %collective-permute-start = (bf16[1,2560,128]{2,1,0:T(8,128)(2,1)}, bf16[1,2560,128]{2,1,0:T(8,128)(2,1)}, u32[]{:S(2)}, u32[]{:S(2)}) collective-permute-start(bf16[1,2560,128]{2,1,0:T(8,128)(2,1)} %refs_0_), channel_id=1, source_target_pairs={{0,192},{64,0},{128,64},{192,128},{1,193},{65,1},{129,65},{193,129... | collective-permute-start | bytes 1966088 | tf_op jit(solution)/shard_map/ppermute | solution.py:142
  25.6 3.0 %collective-permute-start.2 = (bf16[1,2560,128]{2,1,0:T(8,128)(2,1)}, bf16[1,2560,128]{2,1,0:T(8,128)(2,1)}, u32[]{:S(2)}, u32[]{:S(2)}) collective-permute-start(bf16[1,2560,128]{2,1,0:T(8,128)(2,1)} %refs_0_), channel_id=1, source_target_pairs={{0,128},{64,192},{128,0},{192,64},{1,129},{65,193},{129,1},{193,65... | collective-permute-start | bytes 1966088 | tf_op jit(solution)/shard_map/ppermute | solution.py:142
  28.6 4.1 %collective-permute-start.1 = (bf16[1,2560,128]{2,1,0:T(8,128)(2,1)}, bf16[1,2560,128]{2,1,0:T(8,128)(2,1)}, u32[]{:S(2)}, u32[]{:S(2)}) collective-permute-start(bf16[1,2560,128]{2,1,0:T(8,128)(2,1)} %refs_1_), channel_id=1, source_target_pairs={{0,192},{64,0},{128,64},{192,128},{1,193},{65,1},{129,65},{193,129... | collective-permute-start | bytes 1966088 | tf_op jit(solution)/shard_map/ppermute | solution.py:142
  32.7 3.3 %collective-permute-start.3 = (bf16[1,2560,128]{2,1,0:T(8,128)(2,1)}, bf16[1,2560,128]{2,1,0:T(8,128)(2,1)}, u32[]{:S(2)}, u32[]{:S(2)}) collective-permute-start(bf16[1,2560,128]{2,1,0:T(8,128)(2,1)} %refs_1_), channel_id=1, source_target_pairs={{0,128},{64,192},{128,0},{192,64},{1,129},{65,193},{129,1},{193,65... | collective-permute-start | bytes 1966088 | tf_op jit(solution)/shard_map/ppermute | solution.py:142
  36.0 3.4 %collective-permute-start.4 = (bf16[1,2560,128]{2,1,0:T(8,128)(2,1)}, bf16[1,2560,128]{2,1,0:T(8,128)(2,1)}, u32[]{:S(2)}, u32[]{:S(2)}) collective-permute-start(bf16[1,2560,128]{2,1,0:T(8,128)(2,1)} %refs_0_), channel_id=1, source_target_pairs={{0,64},{64,128},{128,192},{192,0},{1,65},{65,129},{129,193},{193,1... | collective-permute-start | bytes 1966088 | tf_op jit(solution)/shard_map/ppermute | solution.py:142
  39.4 18.5 %collective-permute-done.refs_0_ = bf16[1,2560,128]{2,1,0:T(8,128)(2,1)} collective-permute-done((bf16[1,2560,128]{2,1,0:T(8,128)(2,1)}, bf16[1,2560,128]{2,1,0:T(8,128)(2,1)}, u32[]{:S(2)}, u32[]{:S(2)}) %collective-permute-start) | collective-permute-done | bytes 655392 | tf_op jit(solution)/shard_map/ppermute | solution.py:142
  57.9 1.9 %collective-permute-start.5 = (bf16[1,2560,128]{2,1,0:T(8,128)(2,1)}, bf16[1,2560,128]{2,1,0:T(8,128)(2,1)}, u32[]{:S(2)}, u32[]{:S(2)}) collective-permute-start(bf16[1,2560,128]{2,1,0:T(8,128)(2,1)} %refs_1_), channel_id=1, source_target_pairs={{0,64},{64,128},{128,192},{192,0},{1,65},{65,129},{129,193},{193,1... | collective-permute-start | bytes 1966088 | tf_op jit(solution)/shard_map/ppermute | solution.py:142
  59.8 36.8 %all-to-all-done = bf16[128,4,3072]{2,1,0:T(4,128)(2,1)S(1)} async-done(((bf16[128,4,3072]{2,1,0:T(4,128)(2,1)}), bf16[128,4,3072]{2,1,0:T(4,128)(2,1)S(1)}, u32[]{:S(2)}, u32[]{:S(2)}) %all-to-all-start) | async-done | bytes 3145760 | tf_op jit(solution)/shard_map/all_to_all | solution.py:171
  96.7 2.4 %reshape.11.recv_ref = bf16[512,3072]{1,0:T(8,128)(2,1)} reshape(bf16[128,4,3072]{2,1,0:T(4,128)(2,1)S(1)} %all-to-all-done) | data formatting | bytes 6291456 | tf_op jit(solution)/shard_map/reshape | solution.py:176
  99.1 0.0 collective-permute-done.4.refs_2_
  99.1 0.0 collective-permute-done.5.refs_3_
  99.1 6.3 %slice_grads.5 = (bf16[1,2560,128]{2,1,0:T(8,128)(2,1)}, bf16[1,2560,128]{2,1,0:T(8,128)(2,1)}) custom-call(s32[1]{0:T(128)} %bitcast.6.which_ref, bf16[512,3072]{1,0:T(8,128)(2,1)} %reshape.11.recv_ref, bf16[1,2560,128]{2,1,0:T(8,128)(2,1)} %collective-permute-done.2.refs_0_, bf16[1,2560,128]{2,1,0:T(8,128)(2,1)} %collective-permute-done.3.refs_1_), custom_call_target="tpu_custom_call" | custom-call | flops 1342177280 | bytes 5767168 | tf_op jit(solution)/shard_map/slice_grads/pallas_call | solution.py:117
  105.5 2.4 %collective-permute-start.7 = (bf16[1,2560,128]{2,1,0:T(8,128)(2,1)}, bf16[1,2560,128]{2,1,0:T(8,128)(2,1)S(1)}, u32[]{:S(2)}, u32[]{:S(2)}) collective-permute-start(bf16[1,2560,128]{2,1,0:T(8,128)(2,1)} %get-tuple-element.33), channel_id=1, source_target_pairs={{0,64},{64,128},{128,192},{192,0},{1,65},{65,129},{129,193},{193,1... | collective-permute-start | bytes 1966088 | tf_op jit(solution)/shard_map/ppermute | solution.py:142
  107.9 0.1 pad_add_fusion
  108.0 0.7 slice.3.which_ref
  108.6 8.6 %slice_grads.4 = (bf16[1,2560,128]{2,1,0:T(8,128)(2,1)}, bf16[1,2560,128]{2,1,0:T(8,128)(2,1)}, bf16[1,2560,128]{2,1,0:T(8,128)(2,1)}, bf16[1,2560,128]{2,1,0:T(8,128)(2,1)}) custom-call(s32[2]{0:T(128)} %slice.3.which_ref, bf16[512,3072]{1,0:T(8,128)(2,1)} %reshape.11.recv_ref, bf16[1,2560,128]{2,1,0:T(8,128)(2,1)} %collective-permute-done.refs_0_, ...), custom_call_target="tpu_custom_call" | custom-call | flops 2684354560 | bytes 8388608 | tf_op jit(solution)/shard_map/slice_grads/pallas_call | solution.py:117
  117.3 3.5 %collective-permute-start.6 = (bf16[1,2560,128]{2,1,0:T(8,128)(2,1)}, bf16[1,2560,128]{2,1,0:T(8,128)(2,1)S(1)}, u32[]{:S(2)}, u32[]{:S(2)}) collective-permute-start(bf16[1,2560,128]{2,1,0:T(8,128)(2,1)} %get-tuple-element.29), channel_id=1, source_target_pairs={{0,192},{64,0},{128,64},{192,128},{1,193},{65,1},{129,65},{193,129... | collective-permute-start | bytes 1966088 | tf_op jit(solution)/shard_map/ppermute | solution.py:142
  120.7 2.7 %collective-permute-start.10 = (bf16[1,2560,128]{2,1,0:T(8,128)(2,1)}, bf16[1,2560,128]{2,1,0:T(8,128)(2,1)S(1)}, u32[]{:S(2)}, u32[]{:S(2)}) collective-permute-start(bf16[1,2560,128]{2,1,0:T(8,128)(2,1)} %get-tuple-element.37), channel_id=1, source_target_pairs={{0,192},{64,0},{128,64},{192,128},{1,193},{65,1},{129,65},{193,129... | collective-permute-start | bytes 1966088 | tf_op jit(solution)/shard_map/ppermute | solution.py:142
  123.5 4.5 %collective-permute-start.9 = (bf16[1,2560,128]{2,1,0:T(8,128)(2,1)}, bf16[1,2560,128]{2,1,0:T(8,128)(2,1)S(1)}, u32[]{:S(2)}, u32[]{:S(2)}) collective-permute-start(bf16[1,2560,128]{2,1,0:T(8,128)(2,1)} %get-tuple-element.35), channel_id=1, source_target_pairs={{0,64},{64,128},{128,192},{192,0},{1,65},{65,129},{129,193},{193,1... | collective-permute-start | bytes 1966088 | tf_op jit(solution)/shard_map/ppermute | solution.py:142
  128.0 6.9 %slice_grads.3 = (f32[1,2560,128]{2,1,0:T(8,128)}, f32[1,2560,128]{2,1,0:T(8,128)}) custom-call(s32[1]{0:T(128)} %bitcast.which_ref, bf16[512,3072]{1,0:T(8,128)(2,1)} %reshape.11.recv_ref, bf16[1,2560,128]{2,1,0:T(8,128)(2,1)} %refs_0_, bf16[1,2560,128]{2,1,0:T(8,128)(2,1)} %refs_1_), custom_call_target="tpu_custom_call" | custom-call | flops 1342177280 | bytes 5767168 | tf_op jit(solution)/shard_map/slice_grads/pallas_call | solution.py:117
  134.9 0.0 collective-permute-done.7
  134.9 0.2 add_convert_fusion.3
  135.1 2.5 %collective-permute-start.8 = (bf16[1,2560,128]{2,1,0:T(8,128)(2,1)S(1)}, bf16[1,2560,128]{2,1,0:T(8,128)(2,1)S(1)}, u32[]{:S(2)}, u32[]{:S(2)}) collective-permute-start(bf16[1,2560,128]{2,1,0:T(8,128)(2,1)S(1)} %add_convert_fusion.3), channel_id=1, source_target_pairs={{0,64},{64,128},{128,192},{192,0},{1,65},{65,129},{129,193},{193,1... | collective-permute-start | bytes 1966088 | tf_op jit(solution)/shard_map/ppermute | solution.py:142
  137.6 13.5 %collective-permute-done.10 = bf16[1,2560,128]{2,1,0:T(8,128)(2,1)S(1)} collective-permute-done((bf16[1,2560,128]{2,1,0:T(8,128)(2,1)}, bf16[1,2560,128]{2,1,0:T(8,128)(2,1)S(1)}, u32[]{:S(2)}, u32[]{:S(2)}) %collective-permute-start.10) | collective-permute-done | bytes 655392 | tf_op jit(solution)/shard_map/ppermute | solution.py:142
  151.1 0.2 add_convert_fusion.1
  151.3 2.2 %collective-permute-start.11 = (bf16[1,2560,128]{2,1,0:T(8,128)(2,1)S(1)}, bf16[1,2560,128]{2,1,0:T(8,128)(2,1)S(1)}, u32[]{:S(2)}, u32[]{:S(2)}) collective-permute-start(bf16[1,2560,128]{2,1,0:T(8,128)(2,1)S(1)} %add_convert_fusion.1), channel_id=1, source_target_pairs={{0,192},{64,0},{128,64},{192,128},{1,193},{65,1},{129,65},{193,129... | collective-permute-start | bytes 1966088 | tf_op jit(solution)/shard_map/ppermute | solution.py:142
  153.6 2.0 %collective-permute-done.8 = bf16[1,2560,128]{2,1,0:T(8,128)(2,1)S(1)} collective-permute-done((bf16[1,2560,128]{2,1,0:T(8,128)(2,1)S(1)}, bf16[1,2560,128]{2,1,0:T(8,128)(2,1)S(1)}, u32[]{:S(2)}, u32[]{:S(2)}) %collective-permute-start.8) | collective-permute-done | bytes 655392 | tf_op jit(solution)/shard_map/ppermute | solution.py:142
  155.6 1.1 add_convert_fusion.2
  156.7 13.4 %collective-permute-done.11 = bf16[1,2560,128]{2,1,0:T(8,128)(2,1)S(1)} collective-permute-done((bf16[1,2560,128]{2,1,0:T(8,128)(2,1)S(1)}, bf16[1,2560,128]{2,1,0:T(8,128)(2,1)S(1)}, u32[]{:S(2)}, u32[]{:S(2)}) %collective-permute-start.11) | collective-permute-done | bytes 655392 | tf_op jit(solution)/shard_map/ppermute | solution.py:142
  170.1 1.1 add_convert_fusion
  (13 shorter events, 0.0 us)
Async XLA Ops:
  5.5 91.2 %all-to-all-start = ((bf16[128,4,3072]{2,1,0:T(4,128)(2,1)}), bf16[128,4,3072]{2,1,0:T(4,128)(2,1)S(1)}, u32[]{:S(2)}, u32[]{:S(2)}) async-start(bf16[128,4,3072]{2,1,0:T(4,128)(2,1)} %pack_rows.1), calls=%async_computation | async-start | bytes 6291456 | tf_op jit(solution)/shard_map/all_to_all | solution.py:171
  22.9 35.0 %collective-permute-start = (bf16[1,2560,128]{2,1,0:T(8,128)(2,1)}, bf16[1,2560,128]{2,1,0:T(8,128)(2,1)}, u32[]{:S(2)}, u32[]{:S(2)}) collective-permute-start(bf16[1,2560,128]{2,1,0:T(8,128)(2,1)} %refs_0_), channel_id=1, source_target_pairs={{0,192},{64,0},{128,64},{192,128},{1,193},{65,1},{129,65},{193,129... | collective-permute-start | bytes 1966088 | tf_op jit(solution)/shard_map/ppermute | solution.py:142
  25.6 73.5 %collective-permute-start.2 = (bf16[1,2560,128]{2,1,0:T(8,128)(2,1)}, bf16[1,2560,128]{2,1,0:T(8,128)(2,1)}, u32[]{:S(2)}, u32[]{:S(2)}) collective-permute-start(bf16[1,2560,128]{2,1,0:T(8,128)(2,1)} %refs_0_), channel_id=1, source_target_pairs={{0,128},{64,192},{128,0},{192,64},{1,129},{65,193},{129,1},{193,65... | collective-permute-start | bytes 1966088 | tf_op jit(solution)/shard_map/ppermute | solution.py:142
  28.6 70.5 %collective-permute-start.1 = (bf16[1,2560,128]{2,1,0:T(8,128)(2,1)}, bf16[1,2560,128]{2,1,0:T(8,128)(2,1)}, u32[]{:S(2)}, u32[]{:S(2)}) collective-permute-start(bf16[1,2560,128]{2,1,0:T(8,128)(2,1)} %refs_1_), channel_id=1, source_target_pairs={{0,192},{64,0},{128,64},{192,128},{1,193},{65,1},{129,65},{193,129... | collective-permute-start | bytes 1966088 | tf_op jit(solution)/shard_map/ppermute | solution.py:142
  32.7 66.4 %collective-permute-start.3 = (bf16[1,2560,128]{2,1,0:T(8,128)(2,1)}, bf16[1,2560,128]{2,1,0:T(8,128)(2,1)}, u32[]{:S(2)}, u32[]{:S(2)}) collective-permute-start(bf16[1,2560,128]{2,1,0:T(8,128)(2,1)} %refs_1_), channel_id=1, source_target_pairs={{0,128},{64,192},{128,0},{192,64},{1,129},{65,193},{129,1},{193,65... | collective-permute-start | bytes 1966088 | tf_op jit(solution)/shard_map/ppermute | solution.py:142
  36.0 63.1 %collective-permute-start.4 = (bf16[1,2560,128]{2,1,0:T(8,128)(2,1)}, bf16[1,2560,128]{2,1,0:T(8,128)(2,1)}, u32[]{:S(2)}, u32[]{:S(2)}) collective-permute-start(bf16[1,2560,128]{2,1,0:T(8,128)(2,1)} %refs_0_), channel_id=1, source_target_pairs={{0,64},{64,128},{128,192},{192,0},{1,65},{65,129},{129,193},{193,1... | collective-permute-start | bytes 1966088 | tf_op jit(solution)/shard_map/ppermute | solution.py:142
  57.9 41.2 %collective-permute-start.5 = (bf16[1,2560,128]{2,1,0:T(8,128)(2,1)}, bf16[1,2560,128]{2,1,0:T(8,128)(2,1)}, u32[]{:S(2)}, u32[]{:S(2)}) collective-permute-start(bf16[1,2560,128]{2,1,0:T(8,128)(2,1)} %refs_1_), channel_id=1, source_target_pairs={{0,64},{64,128},{128,192},{192,0},{1,65},{65,129},{129,193},{193,1... | collective-permute-start | bytes 1966088 | tf_op jit(solution)/shard_map/ppermute | solution.py:142
  105.5 29.4 %collective-permute-start.7 = (bf16[1,2560,128]{2,1,0:T(8,128)(2,1)}, bf16[1,2560,128]{2,1,0:T(8,128)(2,1)S(1)}, u32[]{:S(2)}, u32[]{:S(2)}) collective-permute-start(bf16[1,2560,128]{2,1,0:T(8,128)(2,1)} %get-tuple-element.33), channel_id=1, source_target_pairs={{0,64},{64,128},{128,192},{192,0},{1,65},{65,129},{129,193},{193,1... | collective-permute-start | bytes 1966088 | tf_op jit(solution)/shard_map/ppermute | solution.py:142
  117.3 36.3 %collective-permute-start.6 = (bf16[1,2560,128]{2,1,0:T(8,128)(2,1)}, bf16[1,2560,128]{2,1,0:T(8,128)(2,1)S(1)}, u32[]{:S(2)}, u32[]{:S(2)}) collective-permute-start(bf16[1,2560,128]{2,1,0:T(8,128)(2,1)} %get-tuple-element.29), channel_id=1, source_target_pairs={{0,192},{64,0},{128,64},{192,128},{1,193},{65,1},{129,65},{193,129... | collective-permute-start | bytes 1966088 | tf_op jit(solution)/shard_map/ppermute | solution.py:142
  120.7 30.4 %collective-permute-start.10 = (bf16[1,2560,128]{2,1,0:T(8,128)(2,1)}, bf16[1,2560,128]{2,1,0:T(8,128)(2,1)S(1)}, u32[]{:S(2)}, u32[]{:S(2)}) collective-permute-start(bf16[1,2560,128]{2,1,0:T(8,128)(2,1)} %get-tuple-element.37), channel_id=1, source_target_pairs={{0,192},{64,0},{128,64},{192,128},{1,193},{65,1},{129,65},{193,129... | collective-permute-start | bytes 1966088 | tf_op jit(solution)/shard_map/ppermute | solution.py:142
  123.5 33.2 %collective-permute-start.9 = (bf16[1,2560,128]{2,1,0:T(8,128)(2,1)}, bf16[1,2560,128]{2,1,0:T(8,128)(2,1)S(1)}, u32[]{:S(2)}, u32[]{:S(2)}) collective-permute-start(bf16[1,2560,128]{2,1,0:T(8,128)(2,1)} %get-tuple-element.35), channel_id=1, source_target_pairs={{0,64},{64,128},{128,192},{192,0},{1,65},{65,129},{129,193},{193,1... | collective-permute-start | bytes 1966088 | tf_op jit(solution)/shard_map/ppermute | solution.py:142
  128.0 6.9 %copy-start.3 = (bf16[1,2560,128]{2,1,0:T(8,128)(2,1)S(1)}, bf16[1,2560,128]{2,1,0:T(8,128)(2,1)}, u32[]{:S(2)}) copy-start(bf16[1,2560,128]{2,1,0:T(8,128)(2,1)} %get-tuple-element.30) | copy-start | bytes 1966084
  134.9 16.2 %copy-start.2 = (bf16[1,2560,128]{2,1,0:T(8,128)(2,1)S(1)}, bf16[1,2560,128]{2,1,0:T(8,128)(2,1)}, u32[]{:S(2)}) copy-start(bf16[1,2560,128]{2,1,0:T(8,128)(2,1)} %get-tuple-element.36) | copy-start | bytes 1966084
  135.1 20.5 %copy-start.1 = (f32[1,2560,128]{2,1,0:T(8,128)S(1)}, f32[1,2560,128]{2,1,0:T(8,128)}, u32[]{:S(2)}) copy-start(f32[1,2560,128]{2,1,0:T(8,128)} %get-tuple-element.24) | copy-start | bytes 3932164
  135.1 20.5 %collective-permute-start.8 = (bf16[1,2560,128]{2,1,0:T(8,128)(2,1)S(1)}, bf16[1,2560,128]{2,1,0:T(8,128)(2,1)S(1)}, u32[]{:S(2)}, u32[]{:S(2)}) collective-permute-start(bf16[1,2560,128]{2,1,0:T(8,128)(2,1)S(1)} %add_convert_fusion.3), channel_id=1, source_target_pairs={{0,64},{64,128},{128,192},{192,0},{1,65},{65,129},{129,193},{193,1... | collective-permute-start | bytes 1966088 | tf_op jit(solution)/shard_map/ppermute | solution.py:142
  151.3 18.7 %collective-permute-start.11 = (bf16[1,2560,128]{2,1,0:T(8,128)(2,1)S(1)}, bf16[1,2560,128]{2,1,0:T(8,128)(2,1)S(1)}, u32[]{:S(2)}, u32[]{:S(2)}) collective-permute-start(bf16[1,2560,128]{2,1,0:T(8,128)(2,1)S(1)} %add_convert_fusion.1), channel_id=1, source_target_pairs={{0,192},{64,0},{128,64},{192,128},{1,193},{65,1},{129,65},{193,129... | collective-permute-start | bytes 1966088 | tf_op jit(solution)/shard_map/ppermute | solution.py:142
  155.6 14.5 %copy-start = (f32[1,2560,128]{2,1,0:T(8,128)S(1)}, f32[1,2560,128]{2,1,0:T(8,128)}, u32[]{:S(2)}) copy-start(f32[1,2560,128]{2,1,0:T(8,128)} %get-tuple-element.34) | copy-start | bytes 3932164

commit v4 on v3

--- a/solution.py
+++ b/solution.py
@@ -58,28 +58,16 @@
     out_ref[experts:, :, width:] = acts[:, half:].reshape(experts, SLOTS, half)
 
 
-def pre_grads(toks, act, w_gate, w_up):
-    hidden = act.shape[1]
-    pair = jnp.concatenate([w_gate, w_up], axis=1)
-    both = jnp.dot(toks, pair, preferred_element_type=jnp.float32)
-    gate, up = both[:, :hidden], both[:, hidden:]
+def pre_grads(gate, up, act):
     upstream = act.astype(jnp.float32)
     sig = 1.0 / (1.0 + jnp.exp(-gate))
     d_up = upstream * gate * sig
     d_gate = upstream * up * sig * (1.0 + gate * (1.0 - sig))
-    return jnp.concatenate([d_gate, d_up], axis=1).astype(jnp.bfloat16)
+    return [d_gate.astype(jnp.bfloat16), d_up.astype(jnp.bfloat16)]
 
 
-def store_grads(toks, d, gate_ref, up_ref):
-    hidden = gate_ref.shape[2]
-    total = lax.dot_general(
-        toks, d, (((0,), (0,)), ((), ())), preferred_element_type=jnp.float32
-    )
-    gate_ref[0] = total[:, :hidden].astype(gate_ref.dtype)
-    up_ref[0] = total[:, hidden:].astype(up_ref.dtype)
-
-
-CHUNKS = 4
+CHUNKS = 2
+TILES = 5
 
 
 def slices_kernel(count, which_ref, recv_ref, *refs):
@@ -93,21 +81,25 @@
     ]
     for copy in copies:
         copy.start()
-    d = [[] for _ in range(count)]
+    d = []
     for part, copy in zip(parts, copies):
         copy.wait()
+        row = []
         for k in range(count):
+            pair = jnp.concatenate([weights[2 * k][0], weights[2 * k + 1][0]], axis=1)
+            both = jnp.dot(rows[part, :width], pair, preferred_element_type=jnp.float32)
             start = pl.multiple_of(width + which_ref[k] * hidden, hidden)
-            d[k].append(
-                pre_grads(
-                    rows[part, :width],
-                    rows[part, pl.ds(start, hidden)],
-                    weights[2 * k][0],
-                    weights[2 * k + 1][0],
-                )
-            )
-    for k in range(count):
-        store_grads(rows[:, :width], jnp.concatenate(d[k]), *grads[2 * k : 2 * k + 2])
+            row += pre_grads(both[:, :hidden], both[:, hidden:], rows[part, pl.ds(start, hidden)])
+        d.append(jnp.concatenate(row, axis=1))
+    d = jnp.concatenate(d)
+    tile = width // TILES
+    for t in range(TILES):
+        cols = slice(t * tile, (t + 1) * tile)
+        total = lax.dot_general(
+            rows[:, cols], d, (((0,), (0,)), ((), ())), preferred_element_type=jnp.float32
+        )
+        for k, ref in enumerate(grads):
+            ref[0, cols, :] = total[:, k * hidden : (k + 1) * hidden].astype(ref.dtype)
 
 
 def slice_grads(which, recv, weights, dtype):
@@ -175,16 +167,19 @@
 
     recv, theirs = lax.optimization_barrier((recv.reshape(-1, recv.shape[2]), theirs))
     far_gate, far_up = slice_grads(at[2:3], recv, theirs[2], jnp.bfloat16)
-    far_gate = moved(far_gate, 1)
-    far_up = moved(far_up, -1)
+    far_gate_in = moved(far_gate, 1)
+    far_up_in = moved(far_up, -1)
     right_gate, right_up, left_gate, left_up = slice_grads(
         at[1::2], recv, theirs[1] + theirs[3], jnp.bfloat16
     )
     from_left_up = moved(right_up, 1)
     from_right_gate = moved(left_gate, -1)
+    sum_gate = add(right_gate, far_gate_in).astype(jnp.bfloat16)
+    sum_up = add(left_up, far_up_in).astype(jnp.bfloat16)
+    from_left_gate = moved(sum_gate, 1)
+    from_right_up = moved(sum_up, -1)
+    recv, _, _ = lax.optimization_barrier((recv, sum_gate, sum_up))
     own_gate, own_up = slice_grads(at[0:1], recv, mine, jnp.float32)
-    from_left_gate = moved(add(right_gate, far_gate).astype(jnp.bfloat16), 1)
-    from_right_up = moved(add(left_up, far_up).astype(jnp.bfloat16), -1)
     grad_gate = add(own_gate, from_right_gate, from_left_gate)
     grad_up = add(own_up, from_left_up, from_right_up)
     return (grad_gate.astype(jnp.bfloat16), grad_up.astype(jnp.bfloat16))

time: 172 us -> 163 us (0.948)
  the two profiles are of different devices: /device:TPU:30 before, /device:TPU:1 now
where the time goes in v4:
time: 163 us; the launch traced here: 160 us
  waiting for transfers between devices  69.2 us (42%)
  starting transfers between devices  54.7 us (34%)
  Pallas kernels  26.3 us (16%)
  other arithmetic  6.13 us (4%)
  local copies, waits for them, and re-layouts  3.04 us (2%)
    all_to_all x1, waiting for transfers between devices, body(): recv = lax.all_to_all(send, PLANE, 0, 0, tiled=True)  52.4 us
    ppermute x12, starting transfers between devices, moved(): lax.ppermute(block, 'x', [(i, (i + distance) % planes) for i in range(pla...  36.3 us
    pallas_call x3, Pallas kernels, slice_grads(): pl.pallas_call(functools.partial(slices_kernel, len(weights) // 2), grid_...  21.5 us
    all_to_all x1, starting transfers between devices, body(): recv = lax.all_to_all(send, PLANE, 0, 0, tiled=True)  18.4 us
    ppermute x12, waiting for transfers between devices, moved(): lax.ppermute(block, 'x', [(i, (i + distance) % planes) for i in range(pla...  16.8 us
    pallas_call x1, Pallas kernels, body(): pl.pallas_call(pack_kernel, out_shape=jax.ShapeDtypeStruct((copies * expe...  4.86 us
    convert_element_type x2, other arithmetic, body(): return (grad_gate.astype(jnp.bfloat16), grad_up.astype(jnp.bfloat16))  3.78 us
  transfers between devices with their start and end apart: 13, of which 3 were waited for; matrix products, arithmetic and copies ran while one was open for 5% of the time, Pallas kernels for 9%

profile of v4, /device:TPU:1, one launch (start us, length us, event | category | flops | bytes accessed | tf_op | source)
XLA Modules:
  0.0 160.3 jit_solution(8102266103150119475)
XLA Ops:
  0.6 4.9 %pack_rows.1 = bf16[128,4,3072]{2,1,0:T(4,128)(2,1)} custom-call(s32[6,128]{1,0:T(8,128)} %bitcast.9, f32[6,128]{1,0:T(8,128)} %bitcast.10, s32[1,32]{1,0:T(1,128)} %bitcast.11, bf16[128,2560]{1,0:T(8,128)(2,1)} %tok_ref.1, bf16[6,128,1024]{2,1,0:T(8,128)(2,1)} %bitcast.8), custom_call_target="tpu_custom_call" | custom-call | tf_op jit(solution)/shard_map/pack_rows/pallas_call | solution.py:148
  5.5 18.4 %all-to-all-start = ((bf16[128,4,3072]{2,1,0:T(4,128)(2,1)}), bf16[128,4,3072]{2,1,0:T(4,128)(2,1)S(1)}, u32[]{:S(2)}, u32[]{:S(2)}) async-start(bf16[128,4,3072]{2,1,0:T(4,128)(2,1)} %pack_rows.1), calls=%async_computation | async-start | bytes 6291456 | tf_op jit(solution)/shard_map/all_to_all | solution.py:163
  23.9 4.4 %collective-permute-start = (bf16[1,2560,128]{2,1,0:T(8,128)(2,1)}, bf16[1,2560,128]{2,1,0:T(8,128)(2,1)}, u32[]{:S(2)}, u32[]{:S(2)}) collective-permute-start(bf16[1,2560,128]{2,1,0:T(8,128)(2,1)} %refs_0_), channel_id=1, source_target_pairs={{0,192},{64,0},{128,64},{192,128},{1,193},{65,1},{129,65},{193,129... | collective-permute-start | bytes 1966088 | tf_op jit(solution)/shard_map/ppermute | solution.py:134
  28.3 2.4 %collective-permute-start.2 = (bf16[1,2560,128]{2,1,0:T(8,128)(2,1)}, bf16[1,2560,128]{2,1,0:T(8,128)(2,1)}, u32[]{:S(2)}, u32[]{:S(2)}) collective-permute-start(bf16[1,2560,128]{2,1,0:T(8,128)(2,1)} %refs_0_), channel_id=1, source_target_pairs={{0,128},{64,192},{128,0},{192,64},{1,129},{65,193},{129,1},{193,65... | collective-permute-start | bytes 1966088 | tf_op jit(solution)/shard_map/ppermute | solution.py:134
  30.8 2.8 %collective-permute-start.1 = (bf16[1,2560,128]{2,1,0:T(8,128)(2,1)}, bf16[1,2560,128]{2,1,0:T(8,128)(2,1)}, u32[]{:S(2)}, u32[]{:S(2)}) collective-permute-start(bf16[1,2560,128]{2,1,0:T(8,128)(2,1)} %refs_1_), channel_id=1, source_target_pairs={{0,192},{64,0},{128,64},{192,128},{1,193},{65,1},{129,65},{193,129... | collective-permute-start | bytes 1966088 | tf_op jit(solution)/shard_map/ppermute | solution.py:134
  33.5 3.5 %collective-permute-start.3 = (bf16[1,2560,128]{2,1,0:T(8,128)(2,1)}, bf16[1,2560,128]{2,1,0:T(8,128)(2,1)}, u32[]{:S(2)}, u32[]{:S(2)}) collective-permute-start(bf16[1,2560,128]{2,1,0:T(8,128)(2,1)} %refs_1_), channel_id=1, source_target_pairs={{0,128},{64,192},{128,0},{192,64},{1,129},{65,193},{129,1},{193,65... | collective-permute-start | bytes 1966088 | tf_op jit(solution)/shard_map/ppermute | solution.py:134
  37.1 2.8 %collective-permute-start.4 = (bf16[1,2560,128]{2,1,0:T(8,128)(2,1)}, bf16[1,2560,128]{2,1,0:T(8,128)(2,1)}, u32[]{:S(2)}, u32[]{:S(2)}) collective-permute-start(bf16[1,2560,128]{2,1,0:T(8,128)(2,1)} %refs_0_), channel_id=1, source_target_pairs={{0,64},{64,128},{128,192},{192,0},{1,65},{65,129},{129,193},{193,1... | collective-permute-start | bytes 1966088 | tf_op jit(solution)/shard_map/ppermute | solution.py:134
  39.8 2.7 %collective-permute-done.refs_0_ = bf16[1,2560,128]{2,1,0:T(8,128)(2,1)} collective-permute-done((bf16[1,2560,128]{2,1,0:T(8,128)(2,1)}, bf16[1,2560,128]{2,1,0:T(8,128)(2,1)}, u32[]{:S(2)}, u32[]{:S(2)}) %collective-permute-start) | collective-permute-done | bytes 655392 | tf_op jit(solution)/shard_map/ppermute | solution.py:134
  42.6 2.0 %collective-permute-start.5 = (bf16[1,2560,128]{2,1,0:T(8,128)(2,1)}, bf16[1,2560,128]{2,1,0:T(8,128)(2,1)}, u32[]{:S(2)}, u32[]{:S(2)}) collective-permute-start(bf16[1,2560,128]{2,1,0:T(8,128)(2,1)} %refs_1_), channel_id=1, source_target_pairs={{0,64},{64,128},{128,192},{192,0},{1,65},{65,129},{129,193},{193,1... | collective-permute-start | bytes 1966088 | tf_op jit(solution)/shard_map/ppermute | solution.py:134
  44.6 52.4 %all-to-all-done = bf16[128,4,3072]{2,1,0:T(4,128)(2,1)S(1)} async-done(((bf16[128,4,3072]{2,1,0:T(4,128)(2,1)}), bf16[128,4,3072]{2,1,0:T(4,128)(2,1)S(1)}, u32[]{:S(2)}, u32[]{:S(2)}) %all-to-all-start) | async-done | bytes 3145760 | tf_op jit(solution)/shard_map/all_to_all | solution.py:163
  97.0 2.4 %reshape.11.recv_ref = bf16[512,3072]{1,0:T(8,128)(2,1)} reshape(bf16[128,4,3072]{2,1,0:T(4,128)(2,1)S(1)} %all-to-all-done) | data formatting | bytes 6291456 | tf_op jit(solution)/shard_map/reshape | solution.py:168
  99.4 0.0 collective-permute-done.1.refs_1_
  99.4 0.0 collective-permute-done.3.refs_1_
  99.5 0.0 collective-permute-done.5.refs_3_
  99.5 6.3 %slice_grads.4 = (bf16[1,2560,128]{2,1,0:T(8,128)(2,1)}, bf16[1,2560,128]{2,1,0:T(8,128)(2,1)}) custom-call(s32[1]{0:T(128)} %bitcast.6.which_ref, bf16[512,3072]{1,0:T(8,128)(2,1)} %reshape.11.recv_ref, bf16[1,2560,128]{2,1,0:T(8,128)(2,1)} %collective-permute-done.2.refs_0_, bf16[1,2560,128]{2,1,0:T(8,128)(2,1)} %collective-permute-done.3.refs_1_), custom_call_target="tpu_custom_call" | custom-call | flops 1342177280 | bytes 5767168 | tf_op jit(solution)/shard_map/slice_grads/pallas_call | solution.py:109
  105.7 3.1 %collective-permute-start.6 = (bf16[1,2560,128]{2,1,0:T(8,128)(2,1)}, bf16[1,2560,128]{2,1,0:T(8,128)(2,1)S(1)}, u32[]{:S(2)}, u32[]{:S(2)}) collective-permute-start(bf16[1,2560,128]{2,1,0:T(8,128)(2,1)} %get-tuple-element.32), channel_id=1, source_target_pairs={{0,64},{64,128},{128,192},{192,0},{1,65},{65,129},{129,193},{193,1... | collective-permute-start | bytes 1966088 | tf_op jit(solution)/shard_map/ppermute | solution.py:134
  108.9 0.1 pad_add_fusion
  109.0 0.6 slice.3.which_ref
  109.6 3.4 %collective-permute-start.7 = (bf16[1,2560,128]{2,1,0:T(8,128)(2,1)}, bf16[1,2560,128]{2,1,0:T(8,128)(2,1)S(1)}, u32[]{:S(2)}, u32[]{:S(2)}) collective-permute-start(bf16[1,2560,128]{2,1,0:T(8,128)(2,1)} %get-tuple-element.34), channel_id=1, source_target_pairs={{0,192},{64,0},{128,64},{192,128},{1,193},{65,1},{129,65},{193,129... | collective-permute-start | bytes 1966088 | tf_op jit(solution)/shard_map/ppermute | solution.py:134
  112.9 8.5 %slice_grads.3 = (bf16[1,2560,128]{2,1,0:T(8,128)(2,1)}, bf16[1,2560,128]{2,1,0:T(8,128)(2,1)}, bf16[1,2560,128]{2,1,0:T(8,128)(2,1)}, bf16[1,2560,128]{2,1,0:T(8,128)(2,1)}) custom-call(s32[2]{0:T(128)} %slice.3.which_ref, bf16[512,3072]{1,0:T(8,128)(2,1)} %reshape.11.recv_ref, bf16[1,2560,128]{2,1,0:T(8,128)(2,1)} %collective-permute-done.refs_0_, ...), custom_call_target="tpu_custom_call" | custom-call | flops 2684354560 | bytes 8388608 | tf_op jit(solution)/shard_map/slice_grads/pallas_call | solution.py:109
  121.5 3.3 %collective-permute-start.8 = (bf16[1,2560,128]{2,1,0:T(8,128)(2,1)}, bf16[1,2560,128]{2,1,0:T(8,128)(2,1)S(1)}, u32[]{:S(2)}, u32[]{:S(2)}) collective-permute-start(bf16[1,2560,128]{2,1,0:T(8,128)(2,1)} %get-tuple-element.37), channel_id=1, source_target_pairs={{0,192},{64,0},{128,64},{192,128},{1,193},{65,1},{129,65},{193,129... | collective-permute-start | bytes 1966088 | tf_op jit(solution)/shard_map/ppermute | solution.py:134
  124.8 2.1 %collective-permute-start.10 = (bf16[1,2560,128]{2,1,0:T(8,128)(2,1)}, bf16[1,2560,128]{2,1,0:T(8,128)(2,1)S(1)}, u32[]{:S(2)}, u32[]{:S(2)}) collective-permute-start(bf16[1,2560,128]{2,1,0:T(8,128)(2,1)} %get-tuple-element.39), channel_id=1, source_target_pairs={{0,64},{64,128},{128,192},{192,0},{1,65},{65,129},{129,193},{193,1... | collective-permute-start | bytes 1966088 | tf_op jit(solution)/shard_map/ppermute | solution.py:134
  126.9 1.3 add_convert_fusion.3
  128.2 1.9 %collective-permute-start.9 = (bf16[1,2560,128]{2,1,0:T(8,128)(2,1)S(1)}, bf16[1,2560,128]{2,1,0:T(8,128)(2,1)}, u32[]{:S(2)}, u32[]{:S(2)}) collective-permute-start(bf16[1,2560,128]{2,1,0:T(8,128)(2,1)S(1)} %add_convert_fusion.3), channel_id=1, source_target_pairs={{0,64},{64,128},{128,192},{192,0},{1,65},{65,129},{129,193},{193,1... | collective-permute-start | bytes 1966088 | tf_op jit(solution)/shard_map/ppermute | solution.py:134
  130.1 1.0 add_convert_fusion.2
  131.1 4.6 %collective-permute-start.11 = (bf16[1,2560,128]{2,1,0:T(8,128)(2,1)}, bf16[1,2560,128]{2,1,0:T(8,128)(2,1)S(1)}, u32[]{:S(2)}, u32[]{:S(2)}) collective-permute-start(bf16[1,2560,128]{2,1,0:T(8,128)(2,1)} %add_convert_fusion.2), channel_id=1, source_target_pairs={{0,192},{64,0},{128,64},{192,128},{1,193},{65,1},{129,65},{193,129... | collective-permute-start | bytes 1966088 | tf_op jit(solution)/shard_map/ppermute | solution.py:134
  135.7 6.7 %slice_grads.5 = (f32[1,2560,128]{2,1,0:T(8,128)}, f32[1,2560,128]{2,1,0:T(8,128)}) custom-call(s32[1]{0:T(128)} %bitcast.which_ref, bf16[512,3072]{1,0:T(8,128)(2,1)} %reshape.11.recv_ref, bf16[1,2560,128]{2,1,0:T(8,128)(2,1)} %refs_0_, bf16[1,2560,128]{2,1,0:T(8,128)(2,1)} %refs_1_), custom_call_target="tpu_custom_call" | custom-call | flops 1342177280 | bytes 5767168 | tf_op jit(solution)/shard_map/slice_grads/pallas_call | solution.py:109
  142.4 14.0 %collective-permute-done.9 = bf16[1,2560,128]{2,1,0:T(8,128)(2,1)} collective-permute-done((bf16[1,2560,128]{2,1,0:T(8,128)(2,1)S(1)}, bf16[1,2560,128]{2,1,0:T(8,128)(2,1)}, u32[]{:S(2)}, u32[]{:S(2)}) %collective-permute-start.9) | collective-permute-done | bytes 655392 | tf_op jit(solution)/shard_map/ppermute | solution.py:134
  156.5 2.7 %add_convert_fusion.1 = bf16[1,2560,128]{2,1,0:T(8,128)(2,1)} fusion(bf16[1,2560,128]{2,1,0:T(8,128)(2,1)} %collective-permute-done.9, f32[1,2560,128]{2,1,0:T(8,128)} %get-tuple-element.36, bf16[1,2560,128]{2,1,0:T(8,128)(2,1)S(1)} %collective-permute-done.8), kind=kLoop, calls=%fused_computation.1 | loop fusion | flops 1638400 | bytes 3276800 | tf_op jit(solution)/shard_map/convert_element_type | solution.py:185
  159.2 0.0 collective-permute-done.10
  159.2 0.0 collective-permute-done.11
  159.2 1.1 add_convert_fusion
  (9 shorter events, 0.0 us)
Async XLA Ops:
  5.5 91.5 %all-to-all-start = ((bf16[128,4,3072]{2,1,0:T(4,128)(2,1)}), bf16[128,4,3072]{2,1,0:T(4,128)(2,1)S(1)}, u32[]{:S(2)}, u32[]{:S(2)}) async-start(bf16[128,4,3072]{2,1,0:T(4,128)(2,1)} %pack_rows.1), calls=%async_computation | async-start | bytes 6291456 | tf_op jit(solution)/shard_map/all_to_all | solution.py:163
  23.9 18.6 %collective-permute-start = (bf16[1,2560,128]{2,1,0:T(8,128)(2,1)}, bf16[1,2560,128]{2,1,0:T(8,128)(2,1)}, u32[]{:S(2)}, u32[]{:S(2)}) collective-permute-start(bf16[1,2560,128]{2,1,0:T(8,128)(2,1)} %refs_0_), channel_id=1, source_target_pairs={{0,192},{64,0},{128,64},{192,128},{1,193},{65,1},{129,65},{193,129... | collective-permute-start | bytes 1966088 | tf_op jit(solution)/shard_map/ppermute | solution.py:134
  28.3 71.1 %collective-permute-start.2 = (bf16[1,2560,128]{2,1,0:T(8,128)(2,1)}, bf16[1,2560,128]{2,1,0:T(8,128)(2,1)}, u32[]{:S(2)}, u32[]{:S(2)}) collective-permute-start(bf16[1,2560,128]{2,1,0:T(8,128)(2,1)} %refs_0_), channel_id=1, source_target_pairs={{0,128},{64,192},{128,0},{192,64},{1,129},{65,193},{129,1},{193,65... | collective-permute-start | bytes 1966088 | tf_op jit(solution)/shard_map/ppermute | solution.py:134
  30.8 68.7 %collective-permute-start.1 = (bf16[1,2560,128]{2,1,0:T(8,128)(2,1)}, bf16[1,2560,128]{2,1,0:T(8,128)(2,1)}, u32[]{:S(2)}, u32[]{:S(2)}) collective-permute-start(bf16[1,2560,128]{2,1,0:T(8,128)(2,1)} %refs_1_), channel_id=1, source_target_pairs={{0,192},{64,0},{128,64},{192,128},{1,193},{65,1},{129,65},{193,129... | collective-permute-start | bytes 1966088 | tf_op jit(solution)/shard_map/ppermute | solution.py:134
  33.5 65.9 %collective-permute-start.3 = (bf16[1,2560,128]{2,1,0:T(8,128)(2,1)}, bf16[1,2560,128]{2,1,0:T(8,128)(2,1)}, u32[]{:S(2)}, u32[]{:S(2)}) collective-permute-start(bf16[1,2560,128]{2,1,0:T(8,128)(2,1)} %refs_1_), channel_id=1, source_target_pairs={{0,128},{64,192},{128,0},{192,64},{1,129},{65,193},{129,1},{193,65... | collective-permute-start | bytes 1966088 | tf_op jit(solution)/shard_map/ppermute | solution.py:134
  37.1 62.4 %collective-permute-start.4 = (bf16[1,2560,128]{2,1,0:T(8,128)(2,1)}, bf16[1,2560,128]{2,1,0:T(8,128)(2,1)}, u32[]{:S(2)}, u32[]{:S(2)}) collective-permute-start(bf16[1,2560,128]{2,1,0:T(8,128)(2,1)} %refs_0_), channel_id=1, source_target_pairs={{0,64},{64,128},{128,192},{192,0},{1,65},{65,129},{129,193},{193,1... | collective-permute-start | bytes 1966088 | tf_op jit(solution)/shard_map/ppermute | solution.py:134
  42.6 56.9 %collective-permute-start.5 = (bf16[1,2560,128]{2,1,0:T(8,128)(2,1)}, bf16[1,2560,128]{2,1,0:T(8,128)(2,1)}, u32[]{:S(2)}, u32[]{:S(2)}) collective-permute-start(bf16[1,2560,128]{2,1,0:T(8,128)(2,1)} %refs_1_), channel_id=1, source_target_pairs={{0,64},{64,128},{128,192},{192,0},{1,65},{65,129},{129,193},{193,1... | collective-permute-start | bytes 1966088 | tf_op jit(solution)/shard_map/ppermute | solution.py:134
  105.7 21.2 %collective-permute-start.6 = (bf16[1,2560,128]{2,1,0:T(8,128)(2,1)}, bf16[1,2560,128]{2,1,0:T(8,128)(2,1)S(1)}, u32[]{:S(2)}, u32[]{:S(2)}) collective-permute-start(bf16[1,2560,128]{2,1,0:T(8,128)(2,1)} %get-tuple-element.32), channel_id=1, source_target_pairs={{0,64},{64,128},{128,192},{192,0},{1,65},{65,129},{129,193},{193,1... | collective-permute-start | bytes 1966088 | tf_op jit(solution)/shard_map/ppermute | solution.py:134
  109.6 20.5 %collective-permute-start.7 = (bf16[1,2560,128]{2,1,0:T(8,128)(2,1)}, bf16[1,2560,128]{2,1,0:T(8,128)(2,1)S(1)}, u32[]{:S(2)}, u32[]{:S(2)}) collective-permute-start(bf16[1,2560,128]{2,1,0:T(8,128)(2,1)} %get-tuple-element.34), channel_id=1, source_target_pairs={{0,192},{64,0},{128,64},{192,128},{1,193},{65,1},{129,65},{193,129... | collective-permute-start | bytes 1966088 | tf_op jit(solution)/shard_map/ppermute | solution.py:134
  121.5 8.7 %copy-start.1 = (bf16[1,2560,128]{2,1,0:T(8,128)(2,1)S(1)}, bf16[1,2560,128]{2,1,0:T(8,128)(2,1)}, u32[]{:S(2)}) copy-start(bf16[1,2560,128]{2,1,0:T(8,128)(2,1)} %get-tuple-element.33) | copy-start | bytes 1966084
  121.5 21.0 %collective-permute-start.8 = (bf16[1,2560,128]{2,1,0:T(8,128)(2,1)}, bf16[1,2560,128]{2,1,0:T(8,128)(2,1)S(1)}, u32[]{:S(2)}, u32[]{:S(2)}) collective-permute-start(bf16[1,2560,128]{2,1,0:T(8,128)(2,1)} %get-tuple-element.37), channel_id=1, source_target_pairs={{0,192},{64,0},{128,64},{192,128},{1,193},{65,1},{129,65},{193,129... | collective-permute-start | bytes 1966088 | tf_op jit(solution)/shard_map/ppermute | solution.py:134
  124.8 34.4 %collective-permute-start.10 = (bf16[1,2560,128]{2,1,0:T(8,128)(2,1)}, bf16[1,2560,128]{2,1,0:T(8,128)(2,1)S(1)}, u32[]{:S(2)}, u32[]{:S(2)}) collective-permute-start(bf16[1,2560,128]{2,1,0:T(8,128)(2,1)} %get-tuple-element.39), channel_id=1, source_target_pairs={{0,64},{64,128},{128,192},{192,0},{1,65},{65,129},{129,193},{193,1... | collective-permute-start | bytes 1966088 | tf_op jit(solution)/shard_map/ppermute | solution.py:134
  128.2 28.3 %collective-permute-start.9 = (bf16[1,2560,128]{2,1,0:T(8,128)(2,1)S(1)}, bf16[1,2560,128]{2,1,0:T(8,128)(2,1)}, u32[]{:S(2)}, u32[]{:S(2)}) collective-permute-start(bf16[1,2560,128]{2,1,0:T(8,128)(2,1)S(1)} %add_convert_fusion.3), channel_id=1, source_target_pairs={{0,64},{64,128},{128,192},{192,0},{1,65},{65,129},{129,193},{193,1... | collective-permute-start | bytes 1966088 | tf_op jit(solution)/shard_map/ppermute | solution.py:134
  131.1 28.0 %collective-permute-start.11 = (bf16[1,2560,128]{2,1,0:T(8,128)(2,1)}, bf16[1,2560,128]{2,1,0:T(8,128)(2,1)S(1)}, u32[]{:S(2)}, u32[]{:S(2)}) collective-permute-start(bf16[1,2560,128]{2,1,0:T(8,128)(2,1)} %add_convert_fusion.2), channel_id=1, source_target_pairs={{0,192},{64,0},{128,64},{192,128},{1,193},{65,1},{129,65},{193,129... | collective-permute-start | bytes 1966088 | tf_op jit(solution)/shard_map/ppermute | solution.py:134
  156.5 2.7 %copy-start = (f32[1,2560,128]{2,1,0:T(8,128)S(1)}, f32[1,2560,128]{2,1,0:T(8,128)}, u32[]{:S(2)}) copy-start(f32[1,2560,128]{2,1,0:T(8,128)} %get-tuple-element.38) | copy-start | bytes 3932164

commit v5 on v4

--- a/solution.py
+++ b/solution.py
@@ -11,7 +11,7 @@
 OVF = 2
 SLOTS = CAP + OVF
 VMEM = 60 * 2**20
-SLICE_VMEM = 60 * 2**20
+SLICE_VMEM = 36 * 2**20
 AXES = ("yh", "x", "yl", "z", "c")
 PLANE = ("yh", "yl", "z", "c")
 EXPERT = ("yl", "z", "c")
@@ -71,58 +71,66 @@
 
 
 def slices_kernel(count, which_ref, recv_ref, *refs):
-    weights, grads, (rows, sems) = refs[: 2 * count], refs[2 * count : -2], refs[-2:]
-    width, hidden = weights[0].shape[1:]
-    chunk = rows.shape[0] // CHUNKS
-    parts = [pl.ds(c * chunk, chunk) for c in range(CHUNKS)]
-    copies = [
-        pltpu.make_async_copy(recv_ref.at[part], rows.at[part], sems.at[c])
-        for c, part in enumerate(parts)
+    weights_hbm, grads = refs[: 2 * count], refs[2 * count : 4 * count]
+    rows, weights, d, sems = refs[4 * count :]
+    width, hidden = weights_hbm[0].shape[1:]
+    loads = [
+        pltpu.make_async_copy(
+            source.at[0], weights.at[j // 2, :, pl.ds(j % 2 * hidden, hidden)], sems.at[j]
+        )
+        for j, source in enumerate(weights_hbm)
     ]
-    for copy in copies:
-        copy.start()
-    d = []
-    for part, copy in zip(parts, copies):
-        copy.wait()
-        row = []
-        for k in range(count):
-            pair = jnp.concatenate([weights[2 * k][0], weights[2 * k + 1][0]], axis=1)
-            both = jnp.dot(rows[part, :width], pair, preferred_element_type=jnp.float32)
-            start = pl.multiple_of(width + which_ref[k] * hidden, hidden)
-            row += pre_grads(both[:, :hidden], both[:, hidden:], rows[part, pl.ds(start, hidden)])
-        d.append(jnp.concatenate(row, axis=1))
-    d = jnp.concatenate(d)
+    for load in loads:
+        load.start()
+    messages = recv_ref.shape[0] // CHUNKS
+    chunk = messages * SLOTS
+    for c in range(CHUNKS):
+        got = recv_ref[c * messages : (c + 1) * messages]
+        rows[c * chunk : (c + 1) * chunk, :] = got.reshape(chunk, rows.shape[1])
+    for k in range(count):
+        for load in loads[2 * k : 2 * k + 2]:
+            load.wait()
+        start = pl.multiple_of(width + which_ref[k] * hidden, hidden)
+        for c in range(CHUNKS):
+            part = slice(c * chunk, (c + 1) * chunk)
+            both = jnp.dot(rows[part, :width], weights[k], preferred_element_type=jnp.float32)
+            upstream = rows[part, pl.ds(start, hidden)]
+            d_gate, d_up = pre_grads(both[:, :hidden], both[:, hidden:], upstream)
+            d[part, 2 * k * hidden : (2 * k + 1) * hidden] = d_gate
+            d[part, (2 * k + 1) * hidden : (2 * k + 2) * hidden] = d_up
     tile = width // TILES
     for t in range(TILES):
         cols = slice(t * tile, (t + 1) * tile)
         total = lax.dot_general(
-            rows[:, cols], d, (((0,), (0,)), ((), ())), preferred_element_type=jnp.float32
+            rows[:, cols], d[...], (((0,), (0,)), ((), ())), preferred_element_type=jnp.float32
         )
         for k, ref in enumerate(grads):
             ref[0, cols, :] = total[:, k * hidden : (k + 1) * hidden].astype(ref.dtype)
 
 
 def slice_grads(which, recv, weights, dtype):
+    messages, slots, columns = recv.shape
     shape = weights[0].shape
-    w_size = weights[0].size * len(weights) // 2
-    whole = pl.BlockSpec(shape, lambda i, w: (0, 0, 0))
+    _, width, hidden = shape
+    count = len(weights) // 2
+    rows = messages * slots
+    local = pl.BlockSpec(memory_space=pltpu.VMEM)
+    anywhere = pl.BlockSpec(memory_space=pl.ANY)
     return pl.pallas_call(
-        functools.partial(slices_kernel, len(weights) // 2),
-        grid_spec=pltpu.PrefetchScalarGridSpec(
-            num_scalar_prefetch=1,
-            grid=(1,),
-            in_specs=[pl.BlockSpec(memory_space=pl.ANY)] + [whole] * len(weights),
-            out_specs=[whole] * len(weights),
-            scratch_shapes=[
-                pltpu.VMEM(recv.shape, recv.dtype),
-                pltpu.SemaphoreType.DMA((CHUNKS,)),
-            ],
-        ),
+        functools.partial(slices_kernel, count),
+        in_specs=[pl.BlockSpec(memory_space=pltpu.SMEM), local] + [anywhere] * len(weights),
+        out_specs=[local] * len(weights),
         out_shape=[jax.ShapeDtypeStruct(shape, dtype)] * len(weights),
+        scratch_shapes=[
+            pltpu.VMEM((rows, columns), recv.dtype),
+            pltpu.VMEM((count, width, 2 * hidden), recv.dtype),
+            pltpu.VMEM((rows, 2 * count * hidden), recv.dtype),
+            pltpu.SemaphoreType.DMA((2 * count,)),
+        ],
         compiler_params=pltpu.CompilerParams(vmem_limit_bytes=SLICE_VMEM),
         cost_estimate=pl.CostEstimate(
-            flops=8 * recv.shape[0] * w_size,
-            bytes_accessed=2 * recv.size + 8 * w_size,
+            flops=8 * rows * count * width * hidden,
+            bytes_accessed=2 * recv.size + 8 * count * width * hidden,
             transcendentals=0,
         ),
         name="slice_grads",
@@ -165,7 +173,7 @@
     theirs = {d: tuple(moved(w, -d) for w in mine) for d in (2, 1, 3)}
     at = jnp.stack([(here + d) % planes for d in range(planes)])
 
-    recv, theirs = lax.optimization_barrier((recv.reshape(-1, recv.shape[2]), theirs))
+    recv, theirs = lax.optimization_barrier((recv, theirs))
     far_gate, far_up = slice_grads(at[2:3], recv, theirs[2], jnp.bfloat16)
     far_gate_in = moved(far_gate, 1)
     far_up_in = moved(far_up, -1)

time: 163 us -> 154 us (0.945)
  Pallas kernels: 26.3 us -> 16.3 us
  waiting for transfers between devices: 69.2 us -> 72.9 us
  other arithmetic: 6.13 us -> 3.73 us
    ppermute x12, waiting for transfers between devices: 16.8 us -> 66.7 us  [moved(): lax.ppermute(block, 'x', [(i, (i + distance) % planes) for i in range(pla...]
    all_to_all x1, waiting for transfers between devices: 52.4 us -> 6.21 us  [body(): recv = lax.all_to_all(send, PLANE, 0, 0, tiled=True)]
    pallas_call x3, Pallas kernels: 21.5 us -> 11.5 us  [slice_grads(): pl.pallas_call(functools.partial(slices_kernel, count), in_specs=[pl.Bloc...]
    unnamed x4 -> x10, local copies, waits for them, and re-layouts: 0.01 us -> 2.78 us
    reshape x1 -> x0, local copies, waits for them, and re-layouts: 2.41 us -> none  [body(): recv.reshape(-1, recv.shape[2])]
  transfers between devices with their start and end apart: 13 -> 13, of which waited for: 3 -> 8; matrix products, arithmetic and copies ran while one was open for 5% -> 2% of each run, Pallas kernels for 9% -> 5%
where the time goes in v5:
time: 154 us; the launch traced here: 152 us
  waiting for transfers between devices  72.9 us (47%)
  starting transfers between devices  54.8 us (36%)
  Pallas kernels  16.3 us (11%)
  other arithmetic  3.73 us (2%)
  local copies, waits for them, and re-layouts  2.88 us (2%)
    ppermute x12, waiting for transfers between devices, moved(): lax.ppermute(block, 'x', [(i, (i + distance) % planes) for i in range(pla...  66.7 us
    ppermute x12, starting transfers between devices, moved(): lax.ppermute(block, 'x', [(i, (i + distance) % planes) for i in range(pla...  36.4 us
    all_to_all x1, starting transfers between devices, body(): recv = lax.all_to_all(send, PLANE, 0, 0, tiled=True)  18.4 us
    pallas_call x3, Pallas kernels, slice_grads(): pl.pallas_call(functools.partial(slices_kernel, count), in_specs=[pl.Bloc...  11.5 us
    all_to_all x1, waiting for transfers between devices, body(): recv = lax.all_to_all(send, PLANE, 0, 0, tiled=True)  6.21 us
    pallas_call x1, Pallas kernels, body(): pl.pallas_call(pack_kernel, out_shape=jax.ShapeDtypeStruct((copies * expe...  4.86 us
  transfers between devices with their start and end apart: 13, of which 8 were waited for; matrix products, arithmetic and copies ran while one was open for 2% of the time, Pallas kernels for 5%

profile of v5, /device:TPU:1, one launch (start us, length us, event | category | flops | bytes accessed | tf_op | source)
XLA Modules:
  0.0 151.5 jit_solution(1481063781746685412)
XLA Ops:
  0.6 4.9 %pack_rows.1 = bf16[128,4,3072]{2,1,0:T(4,128)(2,1)} custom-call(s32[6,128]{1,0:T(8,128)} %bitcast.9, f32[6,128]{1,0:T(8,128)} %bitcast.10, s32[1,32]{1,0:T(1,128)} %bitcast.11, bf16[128,2560]{1,0:T(8,128)(2,1)} %tok_ref.1, bf16[6,128,1024]{2,1,0:T(8,128)(2,1)} %bitcast.8), custom_call_target="tpu_custom_call" | custom-call | tf_op jit(solution)/shard_map/pack_rows/pallas_call | solution.py:156
  5.5 18.4 %all-to-all-start = ((bf16[128,4,3072]{2,1,0:T(4,128)(2,1)}), bf16[128,4,3072]{2,1,0:T(4,128)(2,1)S(1)}, u32[]{:S(2)}, u32[]{:S(2)}) async-start(bf16[128,4,3072]{2,1,0:T(4,128)(2,1)} %pack_rows.1), calls=%async_computation | async-start | bytes 6291456 | tf_op jit(solution)/shard_map/all_to_all | solution.py:171
  23.9 4.4 %collective-permute-start = (bf16[1,2560,128]{2,1,0:T(8,128)(2,1)}, bf16[1,2560,128]{2,1,0:T(8,128)(2,1)S(1)}, u32[]{:S(2)}, u32[]{:S(2)}) collective-permute-start(bf16[1,2560,128]{2,1,0:T(8,128)(2,1)} %refs_0_), channel_id=1, source_target_pairs={{0,192},{64,0},{128,64},{192,128},{1,193},{65,1},{129,65},{193,129... | collective-permute-start | bytes 1966088 | tf_op jit(solution)/shard_map/ppermute | solution.py:142
  28.3 2.4 %collective-permute-start.2 = (bf16[1,2560,128]{2,1,0:T(8,128)(2,1)}, bf16[1,2560,128]{2,1,0:T(8,128)(2,1)}, u32[]{:S(2)}, u32[]{:S(2)}) collective-permute-start(bf16[1,2560,128]{2,1,0:T(8,128)(2,1)} %refs_0_), channel_id=1, source_target_pairs={{0,128},{64,192},{128,0},{192,64},{1,129},{65,193},{129,1},{193,65... | collective-permute-start | bytes 1966088 | tf_op jit(solution)/shard_map/ppermute | solution.py:142
  30.8 2.8 %collective-permute-start.1 = (bf16[1,2560,128]{2,1,0:T(8,128)(2,1)}, bf16[1,2560,128]{2,1,0:T(8,128)(2,1)}, u32[]{:S(2)}, u32[]{:S(2)}) collective-permute-start(bf16[1,2560,128]{2,1,0:T(8,128)(2,1)} %refs_1_), channel_id=1, source_target_pairs={{0,192},{64,0},{128,64},{192,128},{1,193},{65,1},{129,65},{193,129... | collective-permute-start | bytes 1966088 | tf_op jit(solution)/shard_map/ppermute | solution.py:142
  33.5 3.5 %collective-permute-start.3 = (bf16[1,2560,128]{2,1,0:T(8,128)(2,1)}, bf16[1,2560,128]{2,1,0:T(8,128)(2,1)}, u32[]{:S(2)}, u32[]{:S(2)}) collective-permute-start(bf16[1,2560,128]{2,1,0:T(8,128)(2,1)} %refs_1_), channel_id=1, source_target_pairs={{0,128},{64,192},{128,0},{192,64},{1,129},{65,193},{129,1},{193,65... | collective-permute-start | bytes 1966088 | tf_op jit(solution)/shard_map/ppermute | solution.py:142
  37.1 2.8 %collective-permute-start.4 = (bf16[1,2560,128]{2,1,0:T(8,128)(2,1)}, bf16[1,2560,128]{2,1,0:T(8,128)(2,1)}, u32[]{:S(2)}, u32[]{:S(2)}) collective-permute-start(bf16[1,2560,128]{2,1,0:T(8,128)(2,1)} %refs_0_), channel_id=1, source_target_pairs={{0,64},{64,128},{128,192},{192,0},{1,65},{65,129},{129,193},{193,1... | collective-permute-start | bytes 1966088 | tf_op jit(solution)/shard_map/ppermute | solution.py:142
  39.8 2.7 %collective-permute-done.refs_0_ = bf16[1,2560,128]{2,1,0:T(8,128)(2,1)S(1)} collective-permute-done((bf16[1,2560,128]{2,1,0:T(8,128)(2,1)}, bf16[1,2560,128]{2,1,0:T(8,128)(2,1)S(1)}, u32[]{:S(2)}, u32[]{:S(2)}) %collective-permute-start) | collective-permute-done | bytes 655392 | tf_op jit(solution)/shard_map/ppermute | solution.py:142
  42.6 0.8 copy-done.2
  43.4 1.9 %collective-permute-start.5 = (bf16[1,2560,128]{2,1,0:T(8,128)(2,1)}, bf16[1,2560,128]{2,1,0:T(8,128)(2,1)}, u32[]{:S(2)}, u32[]{:S(2)}) collective-permute-start(bf16[1,2560,128]{2,1,0:T(8,128)(2,1)} %refs_1_), channel_id=1, source_target_pairs={{0,64},{64,128},{128,192},{192,0},{1,65},{65,129},{129,193},{193,1... | collective-permute-start | bytes 1966088 | tf_op jit(solution)/shard_map/ppermute | solution.py:142
  45.3 25.2 %collective-permute-done.1.refs_1_ = bf16[1,2560,128]{2,1,0:T(8,128)(2,1)} collective-permute-done((bf16[1,2560,128]{2,1,0:T(8,128)(2,1)}, bf16[1,2560,128]{2,1,0:T(8,128)(2,1)}, u32[]{:S(2)}, u32[]{:S(2)}) %collective-permute-start.1) | collective-permute-done | bytes 655392 | tf_op jit(solution)/shard_map/ppermute | solution.py:142
  70.6 6.2 %collective-permute-done.4.refs_2_ = bf16[1,2560,128]{2,1,0:T(8,128)(2,1)} collective-permute-done((bf16[1,2560,128]{2,1,0:T(8,128)(2,1)}, bf16[1,2560,128]{2,1,0:T(8,128)(2,1)}, u32[]{:S(2)}, u32[]{:S(2)}) %collective-permute-start.4) | collective-permute-done | bytes 655392 | tf_op jit(solution)/shard_map/ppermute | solution.py:142
  76.8 14.0 %collective-permute-done.5.refs_3_ = bf16[1,2560,128]{2,1,0:T(8,128)(2,1)} collective-permute-done((bf16[1,2560,128]{2,1,0:T(8,128)(2,1)}, bf16[1,2560,128]{2,1,0:T(8,128)(2,1)}, u32[]{:S(2)}, u32[]{:S(2)}) %collective-permute-start.5) | collective-permute-done | bytes 655392 | tf_op jit(solution)/shard_map/ppermute | solution.py:142
  90.8 6.2 %all-to-all-done.recv_ref = bf16[128,4,3072]{2,1,0:T(4,128)(2,1)S(1)} async-done(((bf16[128,4,3072]{2,1,0:T(4,128)(2,1)}), bf16[128,4,3072]{2,1,0:T(4,128)(2,1)S(1)}, u32[]{:S(2)}, u32[]{:S(2)}) %all-to-all-start) | async-done | bytes 3145760 | tf_op jit(solution)/shard_map/all_to_all | solution.py:171
  97.0 3.9 %slice_grads.4 = (bf16[1,2560,128]{2,1,0:T(8,128)(2,1)}, bf16[1,2560,128]{2,1,0:T(8,128)(2,1)S(1)}) custom-call(s32[1]{0:T(128)} %bitcast.6.which_ref, bf16[128,4,3072]{2,1,0:T(4,128)(2,1)S(1)} %all-to-all-done.recv_ref, bf16[1,2560,128]{2,1,0:T(8,128)(2,1)} %collective-permute-done.2.refs_0_, bf16[1,2560,128]{2,1,0:T(8,128)(2,1)} %collective-permute-done.3.refs_1_), custom_call_target="tpu_custom_call" | custom-call | flops 1342177280 | bytes 5767168 | tf_op jit(solution)/shard_map/slice_grads/pallas_call | solution.py:119
  101.0 0.8 copy-done.4
  101.8 3.1 %collective-permute-start.6 = (bf16[1,2560,128]{2,1,0:T(8,128)(2,1)}, bf16[1,2560,128]{2,1,0:T(8,128)(2,1)}, u32[]{:S(2)}, u32[]{:S(2)}) collective-permute-start(bf16[1,2560,128]{2,1,0:T(8,128)(2,1)} %get-tuple-element.32), channel_id=1, source_target_pairs={{0,64},{64,128},{128,192},{192,0},{1,65},{65,129},{129,193},{193,1... | collective-permute-start | bytes 1966088 | tf_op jit(solution)/shard_map/ppermute | solution.py:142
  105.2 3.4 %collective-permute-start.7 = (bf16[1,2560,128]{2,1,0:T(8,128)(2,1)}, bf16[1,2560,128]{2,1,0:T(8,128)(2,1)S(1)}, u32[]{:S(2)}, u32[]{:S(2)}) collective-permute-start(bf16[1,2560,128]{2,1,0:T(8,128)(2,1)} %copy-done.4), channel_id=1, source_target_pairs={{0,192},{64,0},{128,64},{192,128},{1,193},{65,1},{129,65},{193,129... | collective-permute-start | bytes 1966088 | tf_op jit(solution)/shard_map/ppermute | solution.py:142
  108.5 1.1 copy-done.3
  109.6 5.1 %slice_grads.3 = (bf16[1,2560,128]{2,1,0:T(8,128)(2,1)S(1)}, bf16[1,2560,128]{2,1,0:T(8,128)(2,1)S(1)}, bf16[1,2560,128]{2,1,0:T(8,128)(2,1)S(1)}, bf16[1,2560,128]{2,1,0:T(8,128)(2,1)S(1)}) custom-call(s32[2]{0:T(128)S(1)} %slice.3.which_ref, bf16[128,4,3072]{2,1,0:T(4,128)(2,1)S(1)} %all-to-all-done.recv_ref, bf16[1,2560,128]{2,1,0:T(8,128)(2,1)S(1)} %copy-done.3, ...), custom_call_target="tpu_custom_call" | custom-call | flops 2684354560 | bytes 8388608 | tf_op jit(solution)/shard_map/slice_grads/pallas_call | solution.py:119
  114.7 3.2 %collective-permute-start.8 = (bf16[1,2560,128]{2,1,0:T(8,128)(2,1)S(1)}, bf16[1,2560,128]{2,1,0:T(8,128)(2,1)S(1)}, u32[]{:S(2)}, u32[]{:S(2)}) collective-permute-start(bf16[1,2560,128]{2,1,0:T(8,128)(2,1)S(1)} %get-tuple-element.37), channel_id=1, source_target_pairs={{0,192},{64,0},{128,64},{192,128},{1,193},{65,1},{129,65},{193,129... | collective-permute-start | bytes 1966088 | tf_op jit(solution)/shard_map/ppermute | solution.py:142
  117.9 2.1 %collective-permute-start.10 = (bf16[1,2560,128]{2,1,0:T(8,128)(2,1)S(1)}, bf16[1,2560,128]{2,1,0:T(8,128)(2,1)S(1)}, u32[]{:S(2)}, u32[]{:S(2)}) collective-permute-start(bf16[1,2560,128]{2,1,0:T(8,128)(2,1)S(1)} %get-tuple-element.39), channel_id=1, source_target_pairs={{0,64},{64,128},{128,192},{192,0},{1,65},{65,129},{129,193},{193,1... | collective-permute-start | bytes 1966088 | tf_op jit(solution)/shard_map/ppermute | solution.py:142
  120.0 0.3 collective-permute-done.6
  120.3 1.3 add_convert_fusion.3
  121.6 2.1 %collective-permute-start.9 = (bf16[1,2560,128]{2,1,0:T(8,128)(2,1)S(1)}, bf16[1,2560,128]{2,1,0:T(8,128)(2,1)S(1)}, u32[]{:S(2)}, u32[]{:S(2)}) collective-permute-start(bf16[1,2560,128]{2,1,0:T(8,128)(2,1)S(1)} %add_convert_fusion.3), channel_id=1, source_target_pairs={{0,64},{64,128},{128,192},{192,0},{1,65},{65,129},{129,193},{193,1... | collective-permute-start | bytes 1966088 | tf_op jit(solution)/shard_map/ppermute | solution.py:142
  123.7 0.2 add_convert_fusion.2
  123.8 4.8 %collective-permute-start.11 = (bf16[1,2560,128]{2,1,0:T(8,128)(2,1)S(1)}, bf16[1,2560,128]{2,1,0:T(8,128)(2,1)S(1)}, u32[]{:S(2)}, u32[]{:S(2)}) collective-permute-start(bf16[1,2560,128]{2,1,0:T(8,128)(2,1)S(1)} %add_convert_fusion.2), channel_id=1, source_target_pairs={{0,192},{64,0},{128,64},{192,128},{1,193},{65,1},{129,65},{193,129... | collective-permute-start | bytes 1966088 | tf_op jit(solution)/shard_map/ppermute | solution.py:142
  128.6 2.4 %slice_grads.5 = (f32[1,2560,128]{2,1,0:T(8,128)S(1)}, f32[1,2560,128]{2,1,0:T(8,128)S(1)}) custom-call(s32[1]{0:T(128)} %bitcast.which_ref, bf16[128,4,3072]{2,1,0:T(4,128)(2,1)S(1)} %all-to-all-done.recv_ref, bf16[1,2560,128]{2,1,0:T(8,128)(2,1)S(1)} %copy-done, bf16[1,2560,128]{2,1,0:T(8,128)(2,1)S(1)} %copy-done.1), custom_call_target="tpu_custom_call" | custom-call | flops 1342177280 | bytes 5767168 | tf_op jit(solution)/shard_map/slice_grads/pallas_call | solution.py:119
  131.0 5.0 %collective-permute-done.8 = bf16[1,2560,128]{2,1,0:T(8,128)(2,1)S(1)} collective-permute-done((bf16[1,2560,128]{2,1,0:T(8,128)(2,1)S(1)}, bf16[1,2560,128]{2,1,0:T(8,128)(2,1)S(1)}, u32[]{:S(2)}, u32[]{:S(2)}) %collective-permute-start.8) | collective-permute-done | bytes 655392 | tf_op jit(solution)/shard_map/ppermute | solution.py:142
  136.1 13.2 %collective-permute-done.9 = bf16[1,2560,128]{2,1,0:T(8,128)(2,1)S(1)} collective-permute-done((bf16[1,2560,128]{2,1,0:T(8,128)(2,1)S(1)}, bf16[1,2560,128]{2,1,0:T(8,128)(2,1)S(1)}, u32[]{:S(2)}, u32[]{:S(2)}) %collective-permute-start.9) | collective-permute-done | bytes 655392 | tf_op jit(solution)/shard_map/ppermute | solution.py:142
  149.3 1.1 add_convert_fusion.1
  150.4 1.1 add_convert_fusion
  (14 shorter events, 0.2 us)
Async XLA Ops:
  5.5 91.5 %all-to-all-start = ((bf16[128,4,3072]{2,1,0:T(4,128)(2,1)}), bf16[128,4,3072]{2,1,0:T(4,128)(2,1)S(1)}, u32[]{:S(2)}, u32[]{:S(2)}) async-start(bf16[128,4,3072]{2,1,0:T(4,128)(2,1)} %pack_rows.1), calls=%async_computation | async-start | bytes 6291456 | tf_op jit(solution)/shard_map/all_to_all | solution.py:171
  23.9 18.6 %collective-permute-start = (bf16[1,2560,128]{2,1,0:T(8,128)(2,1)}, bf16[1,2560,128]{2,1,0:T(8,128)(2,1)S(1)}, u32[]{:S(2)}, u32[]{:S(2)}) collective-permute-start(bf16[1,2560,128]{2,1,0:T(8,128)(2,1)} %refs_0_), channel_id=1, source_target_pairs={{0,192},{64,0},{128,64},{192,128},{1,193},{65,1},{129,65},{193,129... | collective-permute-start | bytes 1966088 | tf_op jit(solution)/shard_map/ppermute | solution.py:142
  28.3 42.3 %collective-permute-start.2 = (bf16[1,2560,128]{2,1,0:T(8,128)(2,1)}, bf16[1,2560,128]{2,1,0:T(8,128)(2,1)}, u32[]{:S(2)}, u32[]{:S(2)}) collective-permute-start(bf16[1,2560,128]{2,1,0:T(8,128)(2,1)} %refs_0_), channel_id=1, source_target_pairs={{0,128},{64,192},{128,0},{192,64},{1,129},{65,193},{129,1},{193,65... | collective-permute-start | bytes 1966088 | tf_op jit(solution)/shard_map/ppermute | solution.py:142
  30.8 39.8 %collective-permute-start.1 = (bf16[1,2560,128]{2,1,0:T(8,128)(2,1)}, bf16[1,2560,128]{2,1,0:T(8,128)(2,1)}, u32[]{:S(2)}, u32[]{:S(2)}) collective-permute-start(bf16[1,2560,128]{2,1,0:T(8,128)(2,1)} %refs_1_), channel_id=1, source_target_pairs={{0,192},{64,0},{128,64},{192,128},{1,193},{65,1},{129,65},{193,129... | collective-permute-start | bytes 1966088 | tf_op jit(solution)/shard_map/ppermute | solution.py:142
  33.5 37.1 %collective-permute-start.3 = (bf16[1,2560,128]{2,1,0:T(8,128)(2,1)}, bf16[1,2560,128]{2,1,0:T(8,128)(2,1)}, u32[]{:S(2)}, u32[]{:S(2)}) collective-permute-start(bf16[1,2560,128]{2,1,0:T(8,128)(2,1)} %refs_1_), channel_id=1, source_target_pairs={{0,128},{64,192},{128,0},{192,64},{1,129},{65,193},{129,1},{193,65... | collective-permute-start | bytes 1966088 | tf_op jit(solution)/shard_map/ppermute | solution.py:142
  37.1 39.7 %collective-permute-start.4 = (bf16[1,2560,128]{2,1,0:T(8,128)(2,1)}, bf16[1,2560,128]{2,1,0:T(8,128)(2,1)}, u32[]{:S(2)}, u32[]{:S(2)}) collective-permute-start(bf16[1,2560,128]{2,1,0:T(8,128)(2,1)} %refs_0_), channel_id=1, source_target_pairs={{0,64},{64,128},{128,192},{192,0},{1,65},{65,129},{129,193},{193,1... | collective-permute-start | bytes 1966088 | tf_op jit(solution)/shard_map/ppermute | solution.py:142
  42.6 0.8 copy-start.2
  43.4 47.4 %collective-permute-start.5 = (bf16[1,2560,128]{2,1,0:T(8,128)(2,1)}, bf16[1,2560,128]{2,1,0:T(8,128)(2,1)}, u32[]{:S(2)}, u32[]{:S(2)}) collective-permute-start(bf16[1,2560,128]{2,1,0:T(8,128)(2,1)} %refs_1_), channel_id=1, source_target_pairs={{0,64},{64,128},{128,192},{192,0},{1,65},{65,129},{129,193},{193,1... | collective-permute-start | bytes 1966088 | tf_op jit(solution)/shard_map/ppermute | solution.py:142
  101.0 0.9 copy-start.4
  101.8 18.5 %collective-permute-start.6 = (bf16[1,2560,128]{2,1,0:T(8,128)(2,1)}, bf16[1,2560,128]{2,1,0:T(8,128)(2,1)}, u32[]{:S(2)}, u32[]{:S(2)}) collective-permute-start(bf16[1,2560,128]{2,1,0:T(8,128)(2,1)} %get-tuple-element.32), channel_id=1, source_target_pairs={{0,64},{64,128},{128,192},{192,0},{1,65},{65,129},{129,193},{193,1... | collective-permute-start | bytes 1966088 | tf_op jit(solution)/shard_map/ppermute | solution.py:142
  105.2 18.5 %collective-permute-start.7 = (bf16[1,2560,128]{2,1,0:T(8,128)(2,1)}, bf16[1,2560,128]{2,1,0:T(8,128)(2,1)S(1)}, u32[]{:S(2)}, u32[]{:S(2)}) collective-permute-start(bf16[1,2560,128]{2,1,0:T(8,128)(2,1)} %copy-done.4), channel_id=1, source_target_pairs={{0,192},{64,0},{128,64},{192,128},{1,193},{65,1},{129,65},{193,129... | collective-permute-start | bytes 1966088 | tf_op jit(solution)/shard_map/ppermute | solution.py:142
  108.5 1.1 copy-start.3
  114.7 21.3 %collective-permute-start.8 = (bf16[1,2560,128]{2,1,0:T(8,128)(2,1)S(1)}, bf16[1,2560,128]{2,1,0:T(8,128)(2,1)S(1)}, u32[]{:S(2)}, u32[]{:S(2)}) collective-permute-start(bf16[1,2560,128]{2,1,0:T(8,128)(2,1)S(1)} %get-tuple-element.37), channel_id=1, source_target_pairs={{0,192},{64,0},{128,64},{192,128},{1,193},{65,1},{129,65},{193,129... | collective-permute-start | bytes 1966088 | tf_op jit(solution)/shard_map/ppermute | solution.py:142
  117.9 32.5 %collective-permute-start.10 = (bf16[1,2560,128]{2,1,0:T(8,128)(2,1)S(1)}, bf16[1,2560,128]{2,1,0:T(8,128)(2,1)S(1)}, u32[]{:S(2)}, u32[]{:S(2)}) collective-permute-start(bf16[1,2560,128]{2,1,0:T(8,128)(2,1)S(1)} %get-tuple-element.39), channel_id=1, source_target_pairs={{0,64},{64,128},{128,192},{192,0},{1,65},{65,129},{129,193},{193,1... | collective-permute-start | bytes 1966088 | tf_op jit(solution)/shard_map/ppermute | solution.py:142
  121.6 7.0 %copy-start = (bf16[1,2560,128]{2,1,0:T(8,128)(2,1)S(1)}, bf16[1,2560,128]{2,1,0:T(8,128)(2,1)}, u32[]{:S(2)}) copy-start(bf16[1,2560,128]{2,1,0:T(8,128)(2,1)} %refs_0_) | copy-start | bytes 1966084
  121.6 7.0 %copy-start.1 = (bf16[1,2560,128]{2,1,0:T(8,128)(2,1)S(1)}, bf16[1,2560,128]{2,1,0:T(8,128)(2,1)}, u32[]{:S(2)}) copy-start(bf16[1,2560,128]{2,1,0:T(8,128)(2,1)} %refs_1_) | copy-start | bytes 1966084
  121.6 27.7 %collective-permute-start.9 = (bf16[1,2560,128]{2,1,0:T(8,128)(2,1)S(1)}, bf16[1,2560,128]{2,1,0:T(8,128)(2,1)S(1)}, u32[]{:S(2)}, u32[]{:S(2)}) collective-permute-start(bf16[1,2560,128]{2,1,0:T(8,128)(2,1)S(1)} %add_convert_fusion.3), channel_id=1, source_target_pairs={{0,64},{64,128},{128,192},{192,0},{1,65},{65,129},{129,193},{193,1... | collective-permute-start | bytes 1966088 | tf_op jit(solution)/shard_map/ppermute | solution.py:142
  123.8 26.6 %collective-permute-start.11 = (bf16[1,2560,128]{2,1,0:T(8,128)(2,1)S(1)}, bf16[1,2560,128]{2,1,0:T(8,128)(2,1)S(1)}, u32[]{:S(2)}, u32[]{:S(2)}) collective-permute-start(bf16[1,2560,128]{2,1,0:T(8,128)(2,1)S(1)} %add_convert_fusion.2), channel_id=1, source_target_pairs={{0,192},{64,0},{128,64},{192,128},{1,193},{65,1},{129,65},{193,129... | collective-permute-start | bytes 1966088 | tf_op jit(solution)/shard_map/ppermute | solution.py:142

commit v6 on v5

--- a/solution.py
+++ b/solution.py
@@ -137,6 +137,24 @@
     )(which, recv, *weights)
 
 
+def last_kernel(*refs):
+    for ref, terms in ((refs[6], refs[:3]), (refs[7], refs[3:6])):
+        ref[...] = sum(term[...].astype(jnp.float32) for term in terms).astype(ref.dtype)
+
+
+def last_sums(*terms):
+    shape = jax.ShapeDtypeStruct(terms[0].shape, jnp.bfloat16)
+    return pl.pallas_call(
+        last_kernel,
+        out_shape=[shape] * 2,
+        compiler_params=pltpu.CompilerParams(vmem_limit_bytes=SLICE_VMEM),
+        cost_estimate=pl.CostEstimate(
+            flops=4 * terms[0].size, bytes_accessed=20 * terms[0].size, transcendentals=0
+        ),
+        name="last_sums",
+    )(*terms)
+
+
 def moved(block, distance):
     planes = lax.axis_size("x")
     return lax.ppermute(block, "x", [(i, (i + distance) % planes) for i in range(planes)])
@@ -171,15 +189,14 @@
     recv = lax.all_to_all(send, PLANE, 0, 0, tiled=True)
     mine = (w_gate, w_up)
     theirs = {d: tuple(moved(w, -d) for w in mine) for d in (2, 1, 3)}
-    at = jnp.stack([(here + d) % planes for d in range(planes)])
+    at = jnp.stack([(here + d) % planes for d in (0, 2, 1, 3)])
 
     recv, theirs = lax.optimization_barrier((recv, theirs))
-    far_gate, far_up = slice_grads(at[2:3], recv, theirs[2], jnp.bfloat16)
+    far_gate, far_up, right_gate, right_up, left_gate, left_up = slice_grads(
+        at[1:], recv, theirs[2] + theirs[1] + theirs[3], jnp.bfloat16
+    )
     far_gate_in = moved(far_gate, 1)
     far_up_in = moved(far_up, -1)
-    right_gate, right_up, left_gate, left_up = slice_grads(
-        at[1::2], recv, theirs[1] + theirs[3], jnp.bfloat16
-    )
     from_left_up = moved(right_up, 1)
     from_right_gate = moved(left_gate, -1)
     sum_gate = add(right_gate, far_gate_in).astype(jnp.bfloat16)
@@ -188,9 +205,9 @@
     from_right_up = moved(sum_up, -1)
     recv, _, _ = lax.optimization_barrier((recv, sum_gate, sum_up))
     own_gate, own_up = slice_grads(at[0:1], recv, mine, jnp.float32)
-    grad_gate = add(own_gate, from_right_gate, from_left_gate)
-    grad_up = add(own_up, from_left_up, from_right_up)
-    return (grad_gate.astype(jnp.bfloat16), grad_up.astype(jnp.bfloat16))
+    return last_sums(
+        own_gate, from_right_gate, from_left_gate, own_up, from_left_up, from_right_up
+    )
 
 
 def solution(mesh):

time: 154 us -> 159 us (1.032)
  waiting for transfers between devices: 72.9 us -> 76.2 us
  other arithmetic: 3.73 us -> 2.11 us
  Pallas kernels: 16.3 us -> 17.9 us
    all_to_all x1, waiting for transfers between devices: 6.21 us -> 9.53 us  [body(): recv = lax.all_to_all(send, PLANE, 0, 0, tiled=True)]
    pallas_call x0 -> x1, Pallas kernels: none -> 2.93 us  [last_sums(): pl.pallas_call(last_kernel, out_shape=[shape] * 2, compiler_params=pltpu....]
    convert_element_type x2 -> x0, other arithmetic: 2.22 us -> none  [body(): return (grad_gate.astype(jnp.bfloat16), grad_up.astype(jnp.bfloat16))]
    pallas_call x3 -> x2, Pallas kernels: 11.5 us -> 10.1 us  [slice_grads(): pl.pallas_call(functools.partial(slices_kernel, count), in_specs=[pl.Bloc...]
    unnamed x10 -> x8, local copies, waits for them, and re-layouts: 2.78 us -> 4.09 us
  transfers between devices with their start and end apart: 13 -> 13, of which waited for: 8 -> 11; matrix products, arithmetic and copies ran while one was open for 2% -> 1% of each run, Pallas kernels for 5% -> 2%
where the time goes in v6:
time: 159 us; the launch traced here: 157 us
  waiting for transfers between devices  76.2 us (48%)
  starting transfers between devices  55.7 us (35%)
  Pallas kernels  17.9 us (11%)
  local copies, waits for them, and re-layouts  4.09 us (3%)
  other arithmetic  2.11 us (1%)
    ppermute x12, waiting for transfers between devices, moved(): lax.ppermute(block, 'x', [(i, (i + distance) % planes) for i in range(pla...  66.7 us
    ppermute x12, starting transfers between devices, moved(): lax.ppermute(block, 'x', [(i, (i + distance) % planes) for i in range(pla...  37.3 us
    all_to_all x1, starting transfers between devices, body(): recv = lax.all_to_all(send, PLANE, 0, 0, tiled=True)  18.4 us
    pallas_call x2, Pallas kernels, slice_grads(): pl.pallas_call(functools.partial(slices_kernel, count), in_specs=[pl.Bloc...  10.1 us
    all_to_all x1, waiting for transfers between devices, body(): recv = lax.all_to_all(send, PLANE, 0, 0, tiled=True)  9.53 us
    pallas_call x1, Pallas kernels, body(): pl.pallas_call(pack_kernel, out_shape=jax.ShapeDtypeStruct((copies * expe...  4.85 us
    unnamed x8, local copies, waits for them, and re-layouts  4.09 us
  transfers between devices with their start and end apart: 13, of which 11 were waited for; matrix products, arithmetic and copies ran while one was open for 1% of the time, Pallas kernels for 2%

profile of v6, /device:TPU:1, one launch (start us, length us, event | category | flops | bytes accessed | tf_op | source)
XLA Modules:
  0.0 156.8 jit_solution(1902701007696178003)
XLA Ops:
  0.6 4.9 %pack_rows.1 = bf16[128,4,3072]{2,1,0:T(4,128)(2,1)} custom-call(s32[6,128]{1,0:T(8,128)} %bitcast.9, f32[6,128]{1,0:T(8,128)} %bitcast.10, s32[1,32]{1,0:T(1,128)} %bitcast.11, bf16[128,2560]{1,0:T(8,128)(2,1)} %tok_ref.1, bf16[6,128,1024]{2,1,0:T(8,128)(2,1)} %bitcast.8), custom_call_target="tpu_custom_call" | custom-call | tf_op jit(solution)/shard_map/pack_rows/pallas_call | solution.py:174
  5.5 18.4 %all-to-all-start = ((bf16[128,4,3072]{2,1,0:T(4,128)(2,1)}), bf16[128,4,3072]{2,1,0:T(4,128)(2,1)S(1)}, u32[]{:S(2)}, u32[]{:S(2)}) async-start(bf16[128,4,3072]{2,1,0:T(4,128)(2,1)} %pack_rows.1), calls=%async_computation | async-start | bytes 6291456 | tf_op jit(solution)/shard_map/all_to_all | solution.py:189
  23.9 3.1 %collective-permute-start.4 = (bf16[1,2560,128]{2,1,0:T(8,128)(2,1)}, bf16[1,2560,128]{2,1,0:T(8,128)(2,1)S(1)}, u32[]{:S(2)}, u32[]{:S(2)}) collective-permute-start(bf16[1,2560,128]{2,1,0:T(8,128)(2,1)} %refs_0_), channel_id=1, source_target_pairs={{0,64},{64,128},{128,192},{192,0},{1,65},{65,129},{129,193},{193,1... | collective-permute-start | bytes 1966088 | tf_op jit(solution)/shard_map/ppermute | solution.py:160
  27.0 4.4 %collective-permute-start.2 = (bf16[1,2560,128]{2,1,0:T(8,128)(2,1)}, bf16[1,2560,128]{2,1,0:T(8,128)(2,1)}, u32[]{:S(2)}, u32[]{:S(2)}) collective-permute-start(bf16[1,2560,128]{2,1,0:T(8,128)(2,1)} %refs_0_), channel_id=1, source_target_pairs={{0,128},{64,192},{128,0},{192,64},{1,129},{65,193},{129,1},{193,65... | collective-permute-start | bytes 1966088 | tf_op jit(solution)/shard_map/ppermute | solution.py:160
  31.4 3.1 %collective-permute-start = (bf16[1,2560,128]{2,1,0:T(8,128)(2,1)}, bf16[1,2560,128]{2,1,0:T(8,128)(2,1)}, u32[]{:S(2)}, u32[]{:S(2)}) collective-permute-start(bf16[1,2560,128]{2,1,0:T(8,128)(2,1)} %refs_0_), channel_id=1, source_target_pairs={{0,192},{64,0},{128,64},{192,128},{1,193},{65,1},{129,65},{193,129... | collective-permute-start | bytes 1966088 | tf_op jit(solution)/shard_map/ppermute | solution.py:160
  34.5 2.2 %collective-permute-start.5 = (bf16[1,2560,128]{2,1,0:T(8,128)(2,1)}, bf16[1,2560,128]{2,1,0:T(8,128)(2,1)}, u32[]{:S(2)}, u32[]{:S(2)}) collective-permute-start(bf16[1,2560,128]{2,1,0:T(8,128)(2,1)} %refs_1_), channel_id=1, source_target_pairs={{0,64},{64,128},{128,192},{192,0},{1,65},{65,129},{129,193},{193,1... | collective-permute-start | bytes 1966088 | tf_op jit(solution)/shard_map/ppermute | solution.py:160
  36.7 2.8 %collective-permute-start.3 = (bf16[1,2560,128]{2,1,0:T(8,128)(2,1)}, bf16[1,2560,128]{2,1,0:T(8,128)(2,1)}, u32[]{:S(2)}, u32[]{:S(2)}) collective-permute-start(bf16[1,2560,128]{2,1,0:T(8,128)(2,1)} %refs_1_), channel_id=1, source_target_pairs={{0,128},{64,192},{128,0},{192,64},{1,129},{65,193},{129,1},{193,65... | collective-permute-start | bytes 1966088 | tf_op jit(solution)/shard_map/ppermute | solution.py:160
  39.5 3.1 %collective-permute-done.4.refs_4_ = bf16[1,2560,128]{2,1,0:T(8,128)(2,1)S(1)} collective-permute-done((bf16[1,2560,128]{2,1,0:T(8,128)(2,1)}, bf16[1,2560,128]{2,1,0:T(8,128)(2,1)S(1)}, u32[]{:S(2)}, u32[]{:S(2)}) %collective-permute-start.4) | collective-permute-done | bytes 655392 | tf_op jit(solution)/shard_map/ppermute | solution.py:160
  43.4 3.3 %collective-permute-start.1 = (bf16[1,2560,128]{2,1,0:T(8,128)(2,1)}, bf16[1,2560,128]{2,1,0:T(8,128)(2,1)}, u32[]{:S(2)}, u32[]{:S(2)}) collective-permute-start(bf16[1,2560,128]{2,1,0:T(8,128)(2,1)} %refs_1_), channel_id=1, source_target_pairs={{0,192},{64,0},{128,64},{192,128},{1,193},{65,1},{129,65},{193,129... | collective-permute-start | bytes 1966088 | tf_op jit(solution)/shard_map/ppermute | solution.py:160
  46.8 11.0 %collective-permute-done.2.refs_0_ = bf16[1,2560,128]{2,1,0:T(8,128)(2,1)} collective-permute-done((bf16[1,2560,128]{2,1,0:T(8,128)(2,1)}, bf16[1,2560,128]{2,1,0:T(8,128)(2,1)}, u32[]{:S(2)}, u32[]{:S(2)}) %collective-permute-start.2) | collective-permute-done | bytes 655392 | tf_op jit(solution)/shard_map/ppermute | solution.py:160
  57.8 2.8 %collective-permute-done.refs_2_ = bf16[1,2560,128]{2,1,0:T(8,128)(2,1)} collective-permute-done((bf16[1,2560,128]{2,1,0:T(8,128)(2,1)}, bf16[1,2560,128]{2,1,0:T(8,128)(2,1)}, u32[]{:S(2)}, u32[]{:S(2)}) %collective-permute-start) | collective-permute-done | bytes 655392 | tf_op jit(solution)/shard_map/ppermute | solution.py:160
  60.6 10.2 %collective-permute-done.5.refs_5_ = bf16[1,2560,128]{2,1,0:T(8,128)(2,1)} collective-permute-done((bf16[1,2560,128]{2,1,0:T(8,128)(2,1)}, bf16[1,2560,128]{2,1,0:T(8,128)(2,1)}, u32[]{:S(2)}, u32[]{:S(2)}) %collective-permute-start.5) | collective-permute-done | bytes 655392 | tf_op jit(solution)/shard_map/ppermute | solution.py:160
  70.8 15.1 %collective-permute-done.3.refs_1_ = bf16[1,2560,128]{2,1,0:T(8,128)(2,1)} collective-permute-done((bf16[1,2560,128]{2,1,0:T(8,128)(2,1)}, bf16[1,2560,128]{2,1,0:T(8,128)(2,1)}, u32[]{:S(2)}, u32[]{:S(2)}) %collective-permute-start.3) | collective-permute-done | bytes 655392 | tf_op jit(solution)/shard_map/ppermute | solution.py:160
  85.8 1.6 %collective-permute-done.1.refs_3_ = bf16[1,2560,128]{2,1,0:T(8,128)(2,1)} collective-permute-done((bf16[1,2560,128]{2,1,0:T(8,128)(2,1)}, bf16[1,2560,128]{2,1,0:T(8,128)(2,1)}, u32[]{:S(2)}, u32[]{:S(2)}) %collective-permute-start.1) | collective-permute-done | bytes 655392 | tf_op jit(solution)/shard_map/ppermute | solution.py:160
  87.5 9.5 %all-to-all-done.recv_ref = bf16[128,4,3072]{2,1,0:T(4,128)(2,1)S(1)} async-done(((bf16[128,4,3072]{2,1,0:T(4,128)(2,1)}), bf16[128,4,3072]{2,1,0:T(4,128)(2,1)S(1)}, u32[]{:S(2)}, u32[]{:S(2)}) %all-to-all-start) | async-done | bytes 3145760 | tf_op jit(solution)/shard_map/all_to_all | solution.py:189
  97.0 1.1 copy-done.3
  98.1 7.7 %slice_grads.2 = (bf16[1,2560,128]{2,1,0:T(8,128)(2,1)S(1)}, bf16[1,2560,128]{2,1,0:T(8,128)(2,1)S(1)}, bf16[1,2560,128]{2,1,0:T(8,128)(2,1)S(1)}, bf16[1,2560,1...) custom-call(s32[3]{0:T(128)S(1)} %pad_add_fusion.which_ref, ...), custom_call_target="tpu_custom_call" | custom-call | flops 4026531840 | bytes 11010048 | tf_op jit(solution)/shard_map/slice_grads/pallas_call | solution.py:119
  105.8 3.1 %collective-permute-start.6 = (bf16[1,2560,128]{2,1,0:T(8,128)(2,1)S(1)}, bf16[1,2560,128]{2,1,0:T(8,128)(2,1)S(1)}, u32[]{:S(2)}, u32[]{:S(2)}) collective-permute-start(bf16[1,2560,128]{2,1,0:T(8,128)(2,1)S(1)} %get-tuple-element.32), channel_id=1, source_target_pairs={{0,64},{64,128},{128,192},{192,0},{1,65},{65,129},{129,193},{193,1... | collective-permute-start | bytes 1966088 | tf_op jit(solution)/shard_map/ppermute | solution.py:160
  109.0 3.4 %collective-permute-start.7 = (bf16[1,2560,128]{2,1,0:T(8,128)(2,1)S(1)}, bf16[1,2560,128]{2,1,0:T(8,128)(2,1)S(1)}, u32[]{:S(2)}, u32[]{:S(2)}) collective-permute-start(bf16[1,2560,128]{2,1,0:T(8,128)(2,1)S(1)} %get-tuple-element.34), channel_id=1, source_target_pairs={{0,192},{64,0},{128,64},{192,128},{1,193},{65,1},{129,65},{193,129... | collective-permute-start | bytes 1966088 | tf_op jit(solution)/shard_map/ppermute | solution.py:160
  112.3 3.2 %collective-permute-start.8 = (bf16[1,2560,128]{2,1,0:T(8,128)(2,1)}, bf16[1,2560,128]{2,1,0:T(8,128)(2,1)}, u32[]{:S(2)}, u32[]{:S(2)}) collective-permute-start(bf16[1,2560,128]{2,1,0:T(8,128)(2,1)} %get-tuple-element.37), channel_id=1, source_target_pairs={{0,192},{64,0},{128,64},{192,128},{1,193},{65,1},{129,65},{193,129... | collective-permute-start | bytes 1966088 | tf_op jit(solution)/shard_map/ppermute | solution.py:160
  115.5 2.1 %collective-permute-start.10 = (bf16[1,2560,128]{2,1,0:T(8,128)(2,1)}, bf16[1,2560,128]{2,1,0:T(8,128)(2,1)}, u32[]{:S(2)}, u32[]{:S(2)}) collective-permute-start(bf16[1,2560,128]{2,1,0:T(8,128)(2,1)} %get-tuple-element.39), channel_id=1, source_target_pairs={{0,64},{64,128},{128,192},{192,0},{1,65},{65,129},{129,193},{193,1... | collective-permute-start | bytes 1966088 | tf_op jit(solution)/shard_map/ppermute | solution.py:160
  117.6 6.4 %collective-permute-done.6 = bf16[1,2560,128]{2,1,0:T(8,128)(2,1)S(1)} collective-permute-done((bf16[1,2560,128]{2,1,0:T(8,128)(2,1)S(1)}, bf16[1,2560,128]{2,1,0:T(8,128)(2,1)S(1)}, u32[]{:S(2)}, u32[]{:S(2)}) %collective-permute-start.6) | collective-permute-done | bytes 655392 | tf_op jit(solution)/shard_map/ppermute | solution.py:160
  125.0 1.9 %collective-permute-start.9 = (bf16[1,2560,128]{2,1,0:T(8,128)(2,1)}, bf16[1,2560,128]{2,1,0:T(8,128)(2,1)}, u32[]{:S(2)}, u32[]{:S(2)}) collective-permute-start(bf16[1,2560,128]{2,1,0:T(8,128)(2,1)} %add_convert_fusion.1), channel_id=1, source_target_pairs={{0,64},{64,128},{128,192},{192,0},{1,65},{65,129},{129,193},{193,1... | collective-permute-start | bytes 1966088 | tf_op jit(solution)/shard_map/ppermute | solution.py:160
  127.0 1.0 add_convert_fusion
  128.0 4.7 %collective-permute-start.11 = (bf16[1,2560,128]{2,1,0:T(8,128)(2,1)}, bf16[1,2560,128]{2,1,0:T(8,128)(2,1)}, u32[]{:S(2)}, u32[]{:S(2)}) collective-permute-start(bf16[1,2560,128]{2,1,0:T(8,128)(2,1)} %add_convert_fusion), channel_id=1, source_target_pairs={{0,192},{64,0},{128,64},{192,128},{1,193},{65,1},{129,65},{193,129... | collective-permute-start | bytes 1966088 | tf_op jit(solution)/shard_map/ppermute | solution.py:160
  132.7 1.1 copy-done
  133.8 1.1 copy-done.1
  134.9 2.4 %slice_grads.3 = (f32[1,2560,128]{2,1,0:T(8,128)S(1)}, f32[1,2560,128]{2,1,0:T(8,128)S(1)}) custom-call(s32[1]{0:T(128)} %bitcast.which_ref, bf16[128,4,3072]{2,1,0:T(4,128)(2,1)S(1)} %all-to-all-done.recv_ref, bf16[1,2560,128]{2,1,0:T(8,128)(2,1)S(1)} %copy-done, bf16[1,2560,128]{2,1,0:T(8,128)(2,1)S(1)} %copy-done.1), custom_call_target="tpu_custom_call" | custom-call | flops 1342177280 | bytes 5767168 | tf_op jit(solution)/shard_map/slice_grads/pallas_call | solution.py:119
  137.3 2.5 %collective-permute-done.8.refs_1_ = bf16[1,2560,128]{2,1,0:T(8,128)(2,1)} collective-permute-done((bf16[1,2560,128]{2,1,0:T(8,128)(2,1)}, bf16[1,2560,128]{2,1,0:T(8,128)(2,1)}, u32[]{:S(2)}, u32[]{:S(2)}) %collective-permute-start.8) | collective-permute-done | bytes 655392 | tf_op jit(solution)/shard_map/ppermute | solution.py:160
  139.8 12.4 %collective-permute-done.9.refs_2_ = bf16[1,2560,128]{2,1,0:T(8,128)(2,1)} collective-permute-done((bf16[1,2560,128]{2,1,0:T(8,128)(2,1)}, bf16[1,2560,128]{2,1,0:T(8,128)(2,1)}, u32[]{:S(2)}, u32[]{:S(2)}) %collective-permute-start.9) | collective-permute-done | bytes 655392 | tf_op jit(solution)/shard_map/ppermute | solution.py:160
  152.2 1.7 %collective-permute-done.11.refs_5_ = bf16[1,2560,128]{2,1,0:T(8,128)(2,1)} collective-permute-done((bf16[1,2560,128]{2,1,0:T(8,128)(2,1)}, bf16[1,2560,128]{2,1,0:T(8,128)(2,1)}, u32[]{:S(2)}, u32[]{:S(2)}) %collective-permute-start.11) | collective-permute-done | bytes 655392 | tf_op jit(solution)/shard_map/ppermute | solution.py:160
  153.9 2.9 %last_sums.1 = (bf16[1,2560,128]{2,1,0:T(8,128)(2,1)}, bf16[1,2560,128]{2,1,0:T(8,128)(2,1)}) custom-call(f32[1,2560,128]{2,1,0:T(8,128)S(1)} %get-tuple-element.36.refs_0_, bf16[1,2560,128]{2,1,0:T(8,128)(2,1)} %collective-permute-done.8.refs_1_, bf16[1,2560,128]{2,1,0:T(8,128)(2,1)} %collective-permute-done.9.refs_2_, ...), custom_call_target="tpu_custom_call" | custom-call | flops 1310720 | bytes 6553600 | tf_op jit(solution)/shard_map/last_sums/pallas_call | solution.py:147
  (9 shorter events, 1.9 us)
Async XLA Ops:
  5.5 91.5 %all-to-all-start = ((bf16[128,4,3072]{2,1,0:T(4,128)(2,1)}), bf16[128,4,3072]{2,1,0:T(4,128)(2,1)S(1)}, u32[]{:S(2)}, u32[]{:S(2)}) async-start(bf16[128,4,3072]{2,1,0:T(4,128)(2,1)} %pack_rows.1), calls=%async_computation | async-start | bytes 6291456 | tf_op jit(solution)/shard_map/all_to_all | solution.py:189
  23.9 18.7 %collective-permute-start.4 = (bf16[1,2560,128]{2,1,0:T(8,128)(2,1)}, bf16[1,2560,128]{2,1,0:T(8,128)(2,1)S(1)}, u32[]{:S(2)}, u32[]{:S(2)}) collective-permute-start(bf16[1,2560,128]{2,1,0:T(8,128)(2,1)} %refs_0_), channel_id=1, source_target_pairs={{0,64},{64,128},{128,192},{192,0},{1,65},{65,129},{129,193},{193,1... | collective-permute-start | bytes 1966088 | tf_op jit(solution)/shard_map/ppermute | solution.py:160
  27.0 30.7 %collective-permute-start.2 = (bf16[1,2560,128]{2,1,0:T(8,128)(2,1)}, bf16[1,2560,128]{2,1,0:T(8,128)(2,1)}, u32[]{:S(2)}, u32[]{:S(2)}) collective-permute-start(bf16[1,2560,128]{2,1,0:T(8,128)(2,1)} %refs_0_), channel_id=1, source_target_pairs={{0,128},{64,192},{128,0},{192,64},{1,129},{65,193},{129,1},{193,65... | collective-permute-start | bytes 1966088 | tf_op jit(solution)/shard_map/ppermute | solution.py:160
  31.4 29.2 %collective-permute-start = (bf16[1,2560,128]{2,1,0:T(8,128)(2,1)}, bf16[1,2560,128]{2,1,0:T(8,128)(2,1)}, u32[]{:S(2)}, u32[]{:S(2)}) collective-permute-start(bf16[1,2560,128]{2,1,0:T(8,128)(2,1)} %refs_0_), channel_id=1, source_target_pairs={{0,192},{64,0},{128,64},{192,128},{1,193},{65,1},{129,65},{193,129... | collective-permute-start | bytes 1966088 | tf_op jit(solution)/shard_map/ppermute | solution.py:160
  34.5 36.3 %collective-permute-start.5 = (bf16[1,2560,128]{2,1,0:T(8,128)(2,1)}, bf16[1,2560,128]{2,1,0:T(8,128)(2,1)}, u32[]{:S(2)}, u32[]{:S(2)}) collective-permute-start(bf16[1,2560,128]{2,1,0:T(8,128)(2,1)} %refs_1_), channel_id=1, source_target_pairs={{0,64},{64,128},{128,192},{192,0},{1,65},{65,129},{129,193},{193,1... | collective-permute-start | bytes 1966088 | tf_op jit(solution)/shard_map/ppermute | solution.py:160
  36.7 49.1 %collective-permute-start.3 = (bf16[1,2560,128]{2,1,0:T(8,128)(2,1)}, bf16[1,2560,128]{2,1,0:T(8,128)(2,1)}, u32[]{:S(2)}, u32[]{:S(2)}) collective-permute-start(bf16[1,2560,128]{2,1,0:T(8,128)(2,1)} %refs_1_), channel_id=1, source_target_pairs={{0,128},{64,192},{128,0},{192,64},{1,129},{65,193},{129,1},{193,65... | collective-permute-start | bytes 1966088 | tf_op jit(solution)/shard_map/ppermute | solution.py:160
  42.6 0.8 copy-start.2
  43.4 44.1 %collective-permute-start.1 = (bf16[1,2560,128]{2,1,0:T(8,128)(2,1)}, bf16[1,2560,128]{2,1,0:T(8,128)(2,1)}, u32[]{:S(2)}, u32[]{:S(2)}) collective-permute-start(bf16[1,2560,128]{2,1,0:T(8,128)(2,1)} %refs_1_), channel_id=1, source_target_pairs={{0,192},{64,0},{128,64},{192,128},{1,193},{65,1},{129,65},{193,129... | collective-permute-start | bytes 1966088 | tf_op jit(solution)/shard_map/ppermute | solution.py:160
  97.0 1.1 copy-start.3
  105.8 18.2 %collective-permute-start.6 = (bf16[1,2560,128]{2,1,0:T(8,128)(2,1)S(1)}, bf16[1,2560,128]{2,1,0:T(8,128)(2,1)S(1)}, u32[]{:S(2)}, u32[]{:S(2)}) collective-permute-start(bf16[1,2560,128]{2,1,0:T(8,128)(2,1)S(1)} %get-tuple-element.32), channel_id=1, source_target_pairs={{0,64},{64,128},{128,192},{192,0},{1,65},{65,129},{129,193},{193,1... | collective-permute-start | bytes 1966088 | tf_op jit(solution)/shard_map/ppermute | solution.py:160
  109.0 18.0 %collective-permute-start.7 = (bf16[1,2560,128]{2,1,0:T(8,128)(2,1)S(1)}, bf16[1,2560,128]{2,1,0:T(8,128)(2,1)S(1)}, u32[]{:S(2)}, u32[]{:S(2)}) collective-permute-start(bf16[1,2560,128]{2,1,0:T(8,128)(2,1)S(1)} %get-tuple-element.34), channel_id=1, source_target_pairs={{0,192},{64,0},{128,64},{192,128},{1,193},{65,1},{129,65},{193,129... | collective-permute-start | bytes 1966088 | tf_op jit(solution)/shard_map/ppermute | solution.py:160
  112.3 27.5 %collective-permute-start.8 = (bf16[1,2560,128]{2,1,0:T(8,128)(2,1)}, bf16[1,2560,128]{2,1,0:T(8,128)(2,1)}, u32[]{:S(2)}, u32[]{:S(2)}) collective-permute-start(bf16[1,2560,128]{2,1,0:T(8,128)(2,1)} %get-tuple-element.37), channel_id=1, source_target_pairs={{0,192},{64,0},{128,64},{192,128},{1,193},{65,1},{129,65},{193,129... | collective-permute-start | bytes 1966088 | tf_op jit(solution)/shard_map/ppermute | solution.py:160
  115.5 24.3 %collective-permute-start.10 = (bf16[1,2560,128]{2,1,0:T(8,128)(2,1)}, bf16[1,2560,128]{2,1,0:T(8,128)(2,1)}, u32[]{:S(2)}, u32[]{:S(2)}) collective-permute-start(bf16[1,2560,128]{2,1,0:T(8,128)(2,1)} %get-tuple-element.39), channel_id=1, source_target_pairs={{0,64},{64,128},{128,192},{192,0},{1,65},{65,129},{129,193},{193,1... | collective-permute-start | bytes 1966088 | tf_op jit(solution)/shard_map/ppermute | solution.py:160
  125.0 27.2 %collective-permute-start.9 = (bf16[1,2560,128]{2,1,0:T(8,128)(2,1)}, bf16[1,2560,128]{2,1,0:T(8,128)(2,1)}, u32[]{:S(2)}, u32[]{:S(2)}) collective-permute-start(bf16[1,2560,128]{2,1,0:T(8,128)(2,1)} %add_convert_fusion.1), channel_id=1, source_target_pairs={{0,64},{64,128},{128,192},{192,0},{1,65},{65,129},{129,193},{193,1... | collective-permute-start | bytes 1966088 | tf_op jit(solution)/shard_map/ppermute | solution.py:160
  128.0 25.9 %collective-permute-start.11 = (bf16[1,2560,128]{2,1,0:T(8,128)(2,1)}, bf16[1,2560,128]{2,1,0:T(8,128)(2,1)}, u32[]{:S(2)}, u32[]{:S(2)}) collective-permute-start(bf16[1,2560,128]{2,1,0:T(8,128)(2,1)} %add_convert_fusion), channel_id=1, source_target_pairs={{0,192},{64,0},{128,64},{192,128},{1,193},{65,1},{129,65},{193,129... | collective-permute-start | bytes 1966088 | tf_op jit(solution)/shard_map/ppermute | solution.py:160
  132.7 1.1 copy-start
  133.8 1.1 copy-start.1

commit v7 on v5

--- a/solution.py
+++ b/solution.py
@@ -183,11 +183,14 @@
     from_left_up = moved(right_up, 1)
     from_right_gate = moved(left_gate, -1)
     sum_gate = add(right_gate, far_gate_in).astype(jnp.bfloat16)
+    from_left_gate = moved(sum_gate, 1)
     sum_up = add(left_up, far_up_in).astype(jnp.bfloat16)
-    from_left_gate = moved(sum_gate, 1)
     from_right_up = moved(sum_up, -1)
     recv, _, _ = lax.optimization_barrier((recv, sum_gate, sum_up))
     own_gate, own_up = slice_grads(at[0:1], recv, mine, jnp.float32)
+    own_gate, own_up, from_left_up, from_right_gate = lax.optimization_barrier(
+        (own_gate, own_up, from_left_up, from_right_gate)
+    )
     grad_gate = add(own_gate, from_right_gate, from_left_gate)
     grad_up = add(own_up, from_left_up, from_right_up)
     return (grad_gate.astype(jnp.bfloat16), grad_up.astype(jnp.bfloat16))

time: 154 us -> 154 us (level)
  transfers between devices with their start and end apart: 13 -> 13, of which waited for: 8 -> 9; matrix products, arithmetic and copies ran while one was open for 2% -> 2% of each run, Pallas kernels for 5% -> 5%
where the time goes in v7:
time: 154 us; the launch traced here: 151 us
  waiting for transfers between devices  71.4 us (46%)
  starting transfers between devices  56 us (36%)
  Pallas kernels  16.3 us (11%)
  other arithmetic  3.73 us (2%)
  local copies, waits for them, and re-layouts  2.88 us (2%)
    ppermute x12, waiting for transfers between devices, moved(): lax.ppermute(block, 'x', [(i, (i + distance) % planes) for i in range(pla...  65.2 us
    ppermute x12, starting transfers between devices, moved(): lax.ppermute(block, 'x', [(i, (i + distance) % planes) for i in range(pla...  37.6 us
    all_to_all x1, starting transfers between devices, body(): recv = lax.all_to_all(send, PLANE, 0, 0, tiled=True)  18.4 us
    pallas_call x3, Pallas kernels, slice_grads(): pl.pallas_call(functools.partial(slices_kernel, count), in_specs=[pl.Bloc...  11.5 us
    all_to_all x1, waiting for transfers between devices, body(): recv = lax.all_to_all(send, PLANE, 0, 0, tiled=True)  6.21 us
    pallas_call x1, Pallas kernels, body(): pl.pallas_call(pack_kernel, out_shape=jax.ShapeDtypeStruct((copies * expe...  4.86 us
  transfers between devices with their start and end apart: 13, of which 9 were waited for; matrix products, arithmetic and copies ran while one was open for 2% of the time, Pallas kernels for 5%

profile of v7, /device:TPU:1, one launch (start us, length us, event | category | flops | bytes accessed | tf_op | source)
XLA Modules:
  0.0 151.2 jit_solution(9587900304319199633)
XLA Ops:
  0.6 4.9 %pack_rows.1 = bf16[128,4,3072]{2,1,0:T(4,128)(2,1)} custom-call(s32[6,128]{1,0:T(8,128)} %bitcast.9, f32[6,128]{1,0:T(8,128)} %bitcast.10, s32[1,32]{1,0:T(1,128)} %bitcast.11, bf16[128,2560]{1,0:T(8,128)(2,1)} %tok_ref.1, bf16[6,128,1024]{2,1,0:T(8,128)(2,1)} %bitcast.8), custom_call_target="tpu_custom_call" | custom-call | tf_op jit(solution)/shard_map/pack_rows/pallas_call | solution.py:156
  5.5 18.4 %all-to-all-start = ((bf16[128,4,3072]{2,1,0:T(4,128)(2,1)}), bf16[128,4,3072]{2,1,0:T(4,128)(2,1)S(1)}, u32[]{:S(2)}, u32[]{:S(2)}) async-start(bf16[128,4,3072]{2,1,0:T(4,128)(2,1)} %pack_rows.1), calls=%async_computation | async-start | bytes 6291456 | tf_op jit(solution)/shard_map/all_to_all | solution.py:171
  23.9 4.4 %collective-permute-start = (bf16[1,2560,128]{2,1,0:T(8,128)(2,1)}, bf16[1,2560,128]{2,1,0:T(8,128)(2,1)S(1)}, u32[]{:S(2)}, u32[]{:S(2)}) collective-permute-start(bf16[1,2560,128]{2,1,0:T(8,128)(2,1)} %refs_0_), channel_id=1, source_target_pairs={{0,192},{64,0},{128,64},{192,128},{1,193},{65,1},{129,65},{193,129... | collective-permute-start | bytes 1966088 | tf_op jit(solution)/shard_map/ppermute | solution.py:142
  28.3 2.4 %collective-permute-start.2 = (bf16[1,2560,128]{2,1,0:T(8,128)(2,1)}, bf16[1,2560,128]{2,1,0:T(8,128)(2,1)}, u32[]{:S(2)}, u32[]{:S(2)}) collective-permute-start(bf16[1,2560,128]{2,1,0:T(8,128)(2,1)} %refs_0_), channel_id=1, source_target_pairs={{0,128},{64,192},{128,0},{192,64},{1,129},{65,193},{129,1},{193,65... | collective-permute-start | bytes 1966088 | tf_op jit(solution)/shard_map/ppermute | solution.py:142
  30.8 2.8 %collective-permute-start.1 = (bf16[1,2560,128]{2,1,0:T(8,128)(2,1)}, bf16[1,2560,128]{2,1,0:T(8,128)(2,1)}, u32[]{:S(2)}, u32[]{:S(2)}) collective-permute-start(bf16[1,2560,128]{2,1,0:T(8,128)(2,1)} %refs_1_), channel_id=1, source_target_pairs={{0,192},{64,0},{128,64},{192,128},{1,193},{65,1},{129,65},{193,129... | collective-permute-start | bytes 1966088 | tf_op jit(solution)/shard_map/ppermute | solution.py:142
  33.5 3.5 %collective-permute-start.3 = (bf16[1,2560,128]{2,1,0:T(8,128)(2,1)}, bf16[1,2560,128]{2,1,0:T(8,128)(2,1)}, u32[]{:S(2)}, u32[]{:S(2)}) collective-permute-start(bf16[1,2560,128]{2,1,0:T(8,128)(2,1)} %refs_1_), channel_id=1, source_target_pairs={{0,128},{64,192},{128,0},{192,64},{1,129},{65,193},{129,1},{193,65... | collective-permute-start | bytes 1966088 | tf_op jit(solution)/shard_map/ppermute | solution.py:142
  37.1 2.8 %collective-permute-start.4 = (bf16[1,2560,128]{2,1,0:T(8,128)(2,1)}, bf16[1,2560,128]{2,1,0:T(8,128)(2,1)}, u32[]{:S(2)}, u32[]{:S(2)}) collective-permute-start(bf16[1,2560,128]{2,1,0:T(8,128)(2,1)} %refs_0_), channel_id=1, source_target_pairs={{0,64},{64,128},{128,192},{192,0},{1,65},{65,129},{129,193},{193,1... | collective-permute-start | bytes 1966088 | tf_op jit(solution)/shard_map/ppermute | solution.py:142
  39.8 2.7 %collective-permute-done.refs_0_ = bf16[1,2560,128]{2,1,0:T(8,128)(2,1)S(1)} collective-permute-done((bf16[1,2560,128]{2,1,0:T(8,128)(2,1)}, bf16[1,2560,128]{2,1,0:T(8,128)(2,1)S(1)}, u32[]{:S(2)}, u32[]{:S(2)}) %collective-permute-start) | collective-permute-done | bytes 655392 | tf_op jit(solution)/shard_map/ppermute | solution.py:142
  42.6 0.8 copy-done.2
  43.4 1.9 %collective-permute-start.5 = (bf16[1,2560,128]{2,1,0:T(8,128)(2,1)}, bf16[1,2560,128]{2,1,0:T(8,128)(2,1)}, u32[]{:S(2)}, u32[]{:S(2)}) collective-permute-start(bf16[1,2560,128]{2,1,0:T(8,128)(2,1)} %refs_1_), channel_id=1, source_target_pairs={{0,64},{64,128},{128,192},{192,0},{1,65},{65,129},{129,193},{193,1... | collective-permute-start | bytes 1966088 | tf_op jit(solution)/shard_map/ppermute | solution.py:142
  45.3 25.2 %collective-permute-done.1.refs_1_ = bf16[1,2560,128]{2,1,0:T(8,128)(2,1)} collective-permute-done((bf16[1,2560,128]{2,1,0:T(8,128)(2,1)}, bf16[1,2560,128]{2,1,0:T(8,128)(2,1)}, u32[]{:S(2)}, u32[]{:S(2)}) %collective-permute-start.1) | collective-permute-done | bytes 655392 | tf_op jit(solution)/shard_map/ppermute | solution.py:142
  70.6 6.2 %collective-permute-done.4.refs_2_ = bf16[1,2560,128]{2,1,0:T(8,128)(2,1)} collective-permute-done((bf16[1,2560,128]{2,1,0:T(8,128)(2,1)}, bf16[1,2560,128]{2,1,0:T(8,128)(2,1)}, u32[]{:S(2)}, u32[]{:S(2)}) %collective-permute-start.4) | collective-permute-done | bytes 655392 | tf_op jit(solution)/shard_map/ppermute | solution.py:142
  76.8 14.0 %collective-permute-done.5.refs_3_ = bf16[1,2560,128]{2,1,0:T(8,128)(2,1)} collective-permute-done((bf16[1,2560,128]{2,1,0:T(8,128)(2,1)}, bf16[1,2560,128]{2,1,0:T(8,128)(2,1)}, u32[]{:S(2)}, u32[]{:S(2)}) %collective-permute-start.5) | collective-permute-done | bytes 655392 | tf_op jit(solution)/shard_map/ppermute | solution.py:142
  90.8 6.2 %all-to-all-done.recv_ref = bf16[128,4,3072]{2,1,0:T(4,128)(2,1)S(1)} async-done(((bf16[128,4,3072]{2,1,0:T(4,128)(2,1)}), bf16[128,4,3072]{2,1,0:T(4,128)(2,1)S(1)}, u32[]{:S(2)}, u32[]{:S(2)}) %all-to-all-start) | async-done | bytes 3145760 | tf_op jit(solution)/shard_map/all_to_all | solution.py:171
  97.0 3.9 %slice_grads.4 = (bf16[1,2560,128]{2,1,0:T(8,128)(2,1)}, bf16[1,2560,128]{2,1,0:T(8,128)(2,1)S(1)}) custom-call(s32[1]{0:T(128)} %bitcast.6.which_ref, bf16[128,4,3072]{2,1,0:T(4,128)(2,1)S(1)} %all-to-all-done.recv_ref, bf16[1,2560,128]{2,1,0:T(8,128)(2,1)} %collective-permute-done.2.refs_0_, bf16[1,2560,128]{2,1,0:T(8,128)(2,1)} %collective-permute-done.3.refs_1_), custom_call_target="tpu_custom_call" | custom-call | flops 1342177280 | bytes 5767168 | tf_op jit(solution)/shard_map/slice_grads/pallas_call | solution.py:119
  101.0 0.8 copy-done.4
  101.8 3.1 %collective-permute-start.6 = (bf16[1,2560,128]{2,1,0:T(8,128)(2,1)}, bf16[1,2560,128]{2,1,0:T(8,128)(2,1)}, u32[]{:S(2)}, u32[]{:S(2)}) collective-permute-start(bf16[1,2560,128]{2,1,0:T(8,128)(2,1)} %get-tuple-element.36), channel_id=1, source_target_pairs={{0,64},{64,128},{128,192},{192,0},{1,65},{65,129},{129,193},{193,1... | collective-permute-start | bytes 1966088 | tf_op jit(solution)/shard_map/ppermute | solution.py:142
  105.2 3.4 %collective-permute-start.7 = (bf16[1,2560,128]{2,1,0:T(8,128)(2,1)}, bf16[1,2560,128]{2,1,0:T(8,128)(2,1)S(1)}, u32[]{:S(2)}, u32[]{:S(2)}) collective-permute-start(bf16[1,2560,128]{2,1,0:T(8,128)(2,1)} %copy-done.4), channel_id=1, source_target_pairs={{0,192},{64,0},{128,64},{192,128},{1,193},{65,1},{129,65},{193,129... | collective-permute-start | bytes 1966088 | tf_op jit(solution)/shard_map/ppermute | solution.py:142
  108.5 1.1 copy-done.3
  109.6 5.1 %slice_grads.3 = (bf16[1,2560,128]{2,1,0:T(8,128)(2,1)S(1)}, bf16[1,2560,128]{2,1,0:T(8,128)(2,1)S(1)}, bf16[1,2560,128]{2,1,0:T(8,128)(2,1)S(1)}, bf16[1,2560,128]{2,1,0:T(8,128)(2,1)S(1)}) custom-call(s32[2]{0:T(128)S(1)} %slice.3.which_ref, bf16[128,4,3072]{2,1,0:T(4,128)(2,1)S(1)} %all-to-all-done.recv_ref, bf16[1,2560,128]{2,1,0:T(8,128)(2,1)S(1)} %copy-done.3, ...), custom_call_target="tpu_custom_call" | custom-call | flops 2684354560 | bytes 8388608 | tf_op jit(solution)/shard_map/slice_grads/pallas_call | solution.py:119
  114.7 1.9 %collective-permute-start.8 = (bf16[1,2560,128]{2,1,0:T(8,128)(2,1)S(1)}, bf16[1,2560,128]{2,1,0:T(8,128)(2,1)S(1)}, u32[]{:S(2)}, u32[]{:S(2)}) collective-permute-start(bf16[1,2560,128]{2,1,0:T(8,128)(2,1)S(1)} %get-tuple-element.42), channel_id=1, source_target_pairs={{0,64},{64,128},{128,192},{192,0},{1,65},{65,129},{129,193},{193,1... | collective-permute-start | bytes 1966088 | tf_op jit(solution)/shard_map/ppermute | solution.py:142
  116.7 4.6 %collective-permute-start.9 = (bf16[1,2560,128]{2,1,0:T(8,128)(2,1)S(1)}, bf16[1,2560,128]{2,1,0:T(8,128)(2,1)S(1)}, u32[]{:S(2)}, u32[]{:S(2)}) collective-permute-start(bf16[1,2560,128]{2,1,0:T(8,128)(2,1)S(1)} %get-tuple-element.43), channel_id=1, source_target_pairs={{0,192},{64,0},{128,64},{192,128},{1,193},{65,1},{129,65},{193,129... | collective-permute-start | bytes 1966088 | tf_op jit(solution)/shard_map/ppermute | solution.py:142
  121.3 1.3 add_convert_fusion.3
  122.6 2.1 %collective-permute-start.10 = (bf16[1,2560,128]{2,1,0:T(8,128)(2,1)S(1)}, bf16[1,2560,128]{2,1,0:T(8,128)(2,1)S(1)}, u32[]{:S(2)}, u32[]{:S(2)}) collective-permute-start(bf16[1,2560,128]{2,1,0:T(8,128)(2,1)S(1)} %add_convert_fusion.3), channel_id=1, source_target_pairs={{0,64},{64,128},{128,192},{192,0},{1,65},{65,129},{129,193},{193,1... | collective-permute-start | bytes 1966088 | tf_op jit(solution)/shard_map/ppermute | solution.py:142
  124.8 4.8 %collective-permute-start.11 = (bf16[1,2560,128]{2,1,0:T(8,128)(2,1)S(1)}, bf16[1,2560,128]{2,1,0:T(8,128)(2,1)S(1)}, u32[]{:S(2)}, u32[]{:S(2)}) collective-permute-start(bf16[1,2560,128]{2,1,0:T(8,128)(2,1)S(1)} %add_convert_fusion.2), channel_id=1, source_target_pairs={{0,192},{64,0},{128,64},{192,128},{1,193},{65,1},{129,65},{193,129... | collective-permute-start | bytes 1966088 | tf_op jit(solution)/shard_map/ppermute | solution.py:142
  129.6 2.4 %slice_grads.5 = (f32[1,2560,128]{2,1,0:T(8,128)S(1)}, f32[1,2560,128]{2,1,0:T(8,128)S(1)}) custom-call(s32[1]{0:T(128)} %bitcast.which_ref, bf16[128,4,3072]{2,1,0:T(4,128)(2,1)S(1)} %all-to-all-done.recv_ref, bf16[1,2560,128]{2,1,0:T(8,128)(2,1)S(1)} %copy-done, bf16[1,2560,128]{2,1,0:T(8,128)(2,1)S(1)} %copy-done.1), custom_call_target="tpu_custom_call" | custom-call | flops 1342177280 | bytes 5767168 | tf_op jit(solution)/shard_map/slice_grads/pallas_call | solution.py:119
  132.0 2.7 %collective-permute-done.8 = bf16[1,2560,128]{2,1,0:T(8,128)(2,1)S(1)} collective-permute-done((bf16[1,2560,128]{2,1,0:T(8,128)(2,1)S(1)}, bf16[1,2560,128]{2,1,0:T(8,128)(2,1)S(1)}, u32[]{:S(2)}, u32[]{:S(2)}) %collective-permute-start.8) | collective-permute-done | bytes 655392 | tf_op jit(solution)/shard_map/ppermute | solution.py:142
  134.7 1.4 collective-permute-done.9
  136.1 12.6 %collective-permute-done.10 = bf16[1,2560,128]{2,1,0:T(8,128)(2,1)S(1)} collective-permute-done((bf16[1,2560,128]{2,1,0:T(8,128)(2,1)S(1)}, bf16[1,2560,128]{2,1,0:T(8,128)(2,1)S(1)}, u32[]{:S(2)}, u32[]{:S(2)}) %collective-permute-start.10) | collective-permute-done | bytes 655392 | tf_op jit(solution)/shard_map/ppermute | solution.py:142
  148.7 1.1 add_convert_fusion.1
  149.8 0.3 collective-permute-done.11
  150.1 1.1 add_convert_fusion
  (14 shorter events, 0.4 us)
Async XLA Ops:
  5.5 91.5 %all-to-all-start = ((bf16[128,4,3072]{2,1,0:T(4,128)(2,1)}), bf16[128,4,3072]{2,1,0:T(4,128)(2,1)S(1)}, u32[]{:S(2)}, u32[]{:S(2)}) async-start(bf16[128,4,3072]{2,1,0:T(4,128)(2,1)} %pack_rows.1), calls=%async_computation | async-start | bytes 6291456 | tf_op jit(solution)/shard_map/all_to_all | solution.py:171
  23.9 18.6 %collective-permute-start = (bf16[1,2560,128]{2,1,0:T(8,128)(2,1)}, bf16[1,2560,128]{2,1,0:T(8,128)(2,1)S(1)}, u32[]{:S(2)}, u32[]{:S(2)}) collective-permute-start(bf16[1,2560,128]{2,1,0:T(8,128)(2,1)} %refs_0_), channel_id=1, source_target_pairs={{0,192},{64,0},{128,64},{192,128},{1,193},{65,1},{129,65},{193,129... | collective-permute-start | bytes 1966088 | tf_op jit(solution)/shard_map/ppermute | solution.py:142
  28.3 42.3 %collective-permute-start.2 = (bf16[1,2560,128]{2,1,0:T(8,128)(2,1)}, bf16[1,2560,128]{2,1,0:T(8,128)(2,1)}, u32[]{:S(2)}, u32[]{:S(2)}) collective-permute-start(bf16[1,2560,128]{2,1,0:T(8,128)(2,1)} %refs_0_), channel_id=1, source_target_pairs={{0,128},{64,192},{128,0},{192,64},{1,129},{65,193},{129,1},{193,65... | collective-permute-start | bytes 1966088 | tf_op jit(solution)/shard_map/ppermute | solution.py:142
  30.8 39.8 %collective-permute-start.1 = (bf16[1,2560,128]{2,1,0:T(8,128)(2,1)}, bf16[1,2560,128]{2,1,0:T(8,128)(2,1)}, u32[]{:S(2)}, u32[]{:S(2)}) collective-permute-start(bf16[1,2560,128]{2,1,0:T(8,128)(2,1)} %refs_1_), channel_id=1, source_target_pairs={{0,192},{64,0},{128,64},{192,128},{1,193},{65,1},{129,65},{193,129... | collective-permute-start | bytes 1966088 | tf_op jit(solution)/shard_map/ppermute | solution.py:142
  33.5 37.1 %collective-permute-start.3 = (bf16[1,2560,128]{2,1,0:T(8,128)(2,1)}, bf16[1,2560,128]{2,1,0:T(8,128)(2,1)}, u32[]{:S(2)}, u32[]{:S(2)}) collective-permute-start(bf16[1,2560,128]{2,1,0:T(8,128)(2,1)} %refs_1_), channel_id=1, source_target_pairs={{0,128},{64,192},{128,0},{192,64},{1,129},{65,193},{129,1},{193,65... | collective-permute-start | bytes 1966088 | tf_op jit(solution)/shard_map/ppermute | solution.py:142
  37.1 39.7 %collective-permute-start.4 = (bf16[1,2560,128]{2,1,0:T(8,128)(2,1)}, bf16[1,2560,128]{2,1,0:T(8,128)(2,1)}, u32[]{:S(2)}, u32[]{:S(2)}) collective-permute-start(bf16[1,2560,128]{2,1,0:T(8,128)(2,1)} %refs_0_), channel_id=1, source_target_pairs={{0,64},{64,128},{128,192},{192,0},{1,65},{65,129},{129,193},{193,1... | collective-permute-start | bytes 1966088 | tf_op jit(solution)/shard_map/ppermute | solution.py:142
  42.6 0.8 copy-start.2
  43.4 47.4 %collective-permute-start.5 = (bf16[1,2560,128]{2,1,0:T(8,128)(2,1)}, bf16[1,2560,128]{2,1,0:T(8,128)(2,1)}, u32[]{:S(2)}, u32[]{:S(2)}) collective-permute-start(bf16[1,2560,128]{2,1,0:T(8,128)(2,1)} %refs_1_), channel_id=1, source_target_pairs={{0,64},{64,128},{128,192},{192,0},{1,65},{65,129},{129,193},{193,1... | collective-permute-start | bytes 1966088 | tf_op jit(solution)/shard_map/ppermute | solution.py:142
  101.0 0.9 copy-start.4
  101.8 19.4 %collective-permute-start.6 = (bf16[1,2560,128]{2,1,0:T(8,128)(2,1)}, bf16[1,2560,128]{2,1,0:T(8,128)(2,1)}, u32[]{:S(2)}, u32[]{:S(2)}) collective-permute-start(bf16[1,2560,128]{2,1,0:T(8,128)(2,1)} %get-tuple-element.36), channel_id=1, source_target_pairs={{0,64},{64,128},{128,192},{192,0},{1,65},{65,129},{129,193},{193,1... | collective-permute-start | bytes 1966088 | tf_op jit(solution)/shard_map/ppermute | solution.py:142
  105.2 19.5 %collective-permute-start.7 = (bf16[1,2560,128]{2,1,0:T(8,128)(2,1)}, bf16[1,2560,128]{2,1,0:T(8,128)(2,1)S(1)}, u32[]{:S(2)}, u32[]{:S(2)}) collective-permute-start(bf16[1,2560,128]{2,1,0:T(8,128)(2,1)} %copy-done.4), channel_id=1, source_target_pairs={{0,192},{64,0},{128,64},{192,128},{1,193},{65,1},{129,65},{193,129... | collective-permute-start | bytes 1966088 | tf_op jit(solution)/shard_map/ppermute | solution.py:142
  108.5 1.1 copy-start.3
  114.7 19.9 %collective-permute-start.8 = (bf16[1,2560,128]{2,1,0:T(8,128)(2,1)S(1)}, bf16[1,2560,128]{2,1,0:T(8,128)(2,1)S(1)}, u32[]{:S(2)}, u32[]{:S(2)}) collective-permute-start(bf16[1,2560,128]{2,1,0:T(8,128)(2,1)S(1)} %get-tuple-element.42), channel_id=1, source_target_pairs={{0,64},{64,128},{128,192},{192,0},{1,65},{65,129},{129,193},{193,1... | collective-permute-start | bytes 1966088 | tf_op jit(solution)/shard_map/ppermute | solution.py:142
  116.7 19.4 %collective-permute-start.9 = (bf16[1,2560,128]{2,1,0:T(8,128)(2,1)S(1)}, bf16[1,2560,128]{2,1,0:T(8,128)(2,1)S(1)}, u32[]{:S(2)}, u32[]{:S(2)}) collective-permute-start(bf16[1,2560,128]{2,1,0:T(8,128)(2,1)S(1)} %get-tuple-element.43), channel_id=1, source_target_pairs={{0,192},{64,0},{128,64},{192,128},{1,193},{65,1},{129,65},{193,129... | collective-permute-start | bytes 1966088 | tf_op jit(solution)/shard_map/ppermute | solution.py:142
  122.5 7.0 %copy-start = (bf16[1,2560,128]{2,1,0:T(8,128)(2,1)S(1)}, bf16[1,2560,128]{2,1,0:T(8,128)(2,1)}, u32[]{:S(2)}) copy-start(bf16[1,2560,128]{2,1,0:T(8,128)(2,1)} %refs_0_) | copy-start | bytes 1966084
  122.5 7.0 %copy-start.1 = (bf16[1,2560,128]{2,1,0:T(8,128)(2,1)S(1)}, bf16[1,2560,128]{2,1,0:T(8,128)(2,1)}, u32[]{:S(2)}) copy-start(bf16[1,2560,128]{2,1,0:T(8,128)(2,1)} %refs_1_) | copy-start | bytes 1966084
  122.6 26.2 %collective-permute-start.10 = (bf16[1,2560,128]{2,1,0:T(8,128)(2,1)S(1)}, bf16[1,2560,128]{2,1,0:T(8,128)(2,1)S(1)}, u32[]{:S(2)}, u32[]{:S(2)}) collective-permute-start(bf16[1,2560,128]{2,1,0:T(8,128)(2,1)S(1)} %add_convert_fusion.3), channel_id=1, source_target_pairs={{0,64},{64,128},{128,192},{192,0},{1,65},{65,129},{129,193},{193,1... | collective-permute-start | bytes 1966088 | tf_op jit(solution)/shard_map/ppermute | solution.py:142
  124.8 25.3 %collective-permute-start.11 = (bf16[1,2560,128]{2,1,0:T(8,128)(2,1)S(1)}, bf16[1,2560,128]{2,1,0:T(8,128)(2,1)S(1)}, u32[]{:S(2)}, u32[]{:S(2)}) collective-permute-start(bf16[1,2560,128]{2,1,0:T(8,128)(2,1)S(1)} %add_convert_fusion.2), channel_id=1, source_target_pairs={{0,192},{64,0},{128,64},{192,128},{1,193},{65,1},{129,65},{193,129... | collective-permute-start | bytes 1966088 | tf_op jit(solution)/shard_map/ppermute | solution.py:142

commit v8 on v7

--- a/solution.py
+++ b/solution.py
@@ -8,6 +8,7 @@
 from jax.sharding import Mesh, PartitionSpec as P
 
 CAP = 2
+PIECES = 2
 OVF = 2
 SLOTS = CAP + OVF
 VMEM = 60 * 2**20
@@ -17,12 +18,19 @@
 EXPERT = ("yl", "z", "c")
 
 
-def pack_kernel(ids_ref, probs_ref, hot_ref, tok_ref, act_ref, out_ref):
+def pack_kernel(ids_hbm, hot_hbm, tok_hbm, act_hbm, probs_hbm, out_hbm, *scratch):
+    ids_ref, hot_ref, tok_ref, act_ref, probs_ref, toks, acts, in_sems, out_sems = scratch
     top, block = ids_ref.shape
-    experts = out_ref.shape[0] // 2
+    experts = toks.shape[0]
     rows = experts * SLOTS
     width = tok_ref.shape[1]
-    half = out_ref.shape[2] - width
+    half = acts.shape[2]
+    pairs = [(ids_hbm, ids_ref), (hot_hbm, hot_ref), (tok_hbm, tok_ref), (probs_hbm, probs_ref)]
+    pairs += [(act_hbm.at[k], act_ref.at[k]) for k in range(top)]
+    loads = [pltpu.make_async_copy(*pair, in_sems.at[i]) for i, pair in enumerate(pairs)]
+    for load in loads:
+        load.start()
+    loads[0].wait()
     row = lax.broadcasted_iota(jnp.int32, (rows, block), 0)
     expert, slot = row // SLOTS, row % SLOTS
     hits = [ids_ref[k : k + 1, :] == expert for k in range(top)]
@@ -37,25 +45,45 @@
         jnp.where(before, 1.0, 0.0).astype(jnp.bfloat16),
         preferred_element_type=jnp.float32,
     ).astype(jnp.int32)
+    loads[1].wait()
     hots = hot_ref.shape[1]
     owner = lax.broadcasted_iota(jnp.int32, (rows, hots), 0) // SLOTS
     hot = jnp.max(jnp.where(hot_ref[...] == owner, 1, 0), axis=1, keepdims=True)
     kept = named & (position == slot) & ((slot < CAP) | (hot > 0))
     pick = jnp.where(kept, 1.0, 0.0).astype(jnp.bfloat16)
-    toks = jnp.dot(pick, tok_ref[...], preferred_element_type=jnp.float32)
-    toks = toks.astype(jnp.bfloat16).reshape(experts, SLOTS, width)
-    out_ref[:experts, :, :width] = toks
-    out_ref[experts:, :, :width] = toks
-    acts = jnp.zeros((rows, act_ref.shape[2]), jnp.float32)
+    sends = []
+    loads[2].wait()
+    piece = width // PIECES
+    for p in range(PIECES):
+        cols = slice(p * piece, (p + 1) * piece)
+        got = jnp.dot(pick, tok_ref[:, cols], preferred_element_type=jnp.float32)
+        toks[:, :, cols] = got.astype(jnp.bfloat16).reshape(experts, SLOTS, piece)
+        for copy in range(2):
+            part = (pl.ds(copy * experts, experts), slice(None), pl.ds(p * piece, piece))
+            sends.append(
+                pltpu.make_async_copy(
+                    toks.at[:, :, pl.ds(p * piece, piece)], out_hbm.at[part], out_sems.at[p, copy]
+                )
+            )
+            sends[-1].start()
+    total = jnp.zeros((rows, act_ref.shape[2]), jnp.float32)
     scale = jnp.zeros((rows, block), jnp.float32)
+    loads[3].wait()
     for k in range(top):
+        loads[4 + k].wait()
         chosen = jnp.where(kept & hits[k], 1.0, 0.0)
-        acts += jnp.dot(chosen.astype(jnp.bfloat16), act_ref[k], preferred_element_type=jnp.float32)
+        total += jnp.dot(chosen.astype(jnp.bfloat16), act_ref[k], preferred_element_type=jnp.float32)
         scale += chosen * probs_ref[k : k + 1, :]
-    acts = jnp.sum(scale, axis=1, keepdims=True) * acts
-    acts = acts.astype(jnp.bfloat16)
-    out_ref[:experts, :, width:] = acts[:, :half].reshape(experts, SLOTS, half)
-    out_ref[experts:, :, width:] = acts[:, half:].reshape(experts, SLOTS, half)
+    total = (jnp.sum(scale, axis=1, keepdims=True) * total).astype(jnp.bfloat16)
+    for copy in range(2):
+        here = slice(copy * experts, (copy + 1) * experts)
+        acts[here] = total[:, copy * half : (copy + 1) * half].reshape(experts, SLOTS, half)
+    sends.append(
+        pltpu.make_async_copy(acts, out_hbm.at[:, :, pl.ds(width, half)], out_sems.at[PIECES, 0])
+    )
+    sends[-1].start()
+    for send in sends:
+        send.wait()
 
 
 def pre_grads(gate, up, act):
@@ -153,19 +181,35 @@
     experts = lax.axis_size(EXPERT)
     planes = lax.axis_size("x")
     here = lax.axis_index("x")
+    anywhere = pl.BlockSpec(memory_space=pl.ANY)
+    block, top, _ = act_grad.shape
+    vmem = lambda *shape: pltpu.VMEM(shape, jnp.bfloat16)
     send = pl.pallas_call(
         pack_kernel,
+        in_specs=[anywhere] * 5,
+        out_specs=anywhere,
         out_shape=jax.ShapeDtypeStruct(
             (copies * experts, SLOTS, width + ff // copies), jnp.bfloat16
         ),
+        scratch_shapes=[
+            pltpu.VMEM((top, block), jnp.int32),
+            pltpu.VMEM((1, hot_experts.size), jnp.int32),
+            vmem(block, width),
+            vmem(top, block, ff),
+            pltpu.VMEM((top, block), jnp.float32),
+            vmem(experts, SLOTS, width),
+            vmem(copies * experts, SLOTS, ff // copies),
+            pltpu.SemaphoreType.DMA((4 + top,)),
+            pltpu.SemaphoreType.DMA((PIECES + 1, copies)),
+        ],
         compiler_params=pltpu.CompilerParams(vmem_limit_bytes=VMEM),
         name="pack_rows",
     )(
         expert_ids.T,
-        gate_probs.T,
         hot_experts.reshape(1, -1),
         tokens,
         jnp.swapaxes(act_grad, 0, 1),
+        gate_probs.T,
     )
     send, w_gate, w_up = lax.optimization_barrier((send, w_gate, w_up))
     recv = lax.all_to_all(send, PLANE, 0, 0, tiled=True)

time: 154 us -> 153 us (level)
  no operation moved by 1% of the time
where the time goes in v8:
time: 153 us; the launch traced here: 150 us
  waiting for transfers between devices  71.4 us (47%)
  starting transfers between devices  56 us (37%)
  Pallas kernels  15.3 us (10%)
  other arithmetic  3.73 us (2%)
  local copies, waits for them, and re-layouts  2.88 us (2%)
    ppermute x12, waiting for transfers between devices, moved(): lax.ppermute(block, 'x', [(i, (i + distance) % planes) for i in range(pla...  65.2 us
    ppermute x12, starting transfers between devices, moved(): lax.ppermute(block, 'x', [(i, (i + distance) % planes) for i in range(pla...  37.6 us
    all_to_all x1, starting transfers between devices, body(): recv = lax.all_to_all(send, PLANE, 0, 0, tiled=True)  18.4 us
    pallas_call x3, Pallas kernels, slice_grads(): pl.pallas_call(functools.partial(slices_kernel, count), in_specs=[pl.Bloc...  11.5 us
    all_to_all x1, waiting for transfers between devices, body(): recv = lax.all_to_all(send, PLANE, 0, 0, tiled=True)  6.21 us
    pallas_call x1, Pallas kernels, body(): pl.pallas_call(pack_kernel, in_specs=[anywhere] * 5, out_specs=anywhere,...  3.82 us
  transfers between devices with their start and end apart: 13, of which 9 were waited for; matrix products, arithmetic and copies ran while one was open for 2% of the time, Pallas kernels for 5%

profile of v8, /device:TPU:1, one launch (start us, length us, event | category | flops | bytes accessed | tf_op | source)
XLA Modules:
  0.0 150.2 jit_solution(14061469889234208136)
XLA Ops:
  0.6 3.8 %pack_rows.1 = bf16[128,4,3072]{2,1,0:T(4,128)(2,1)} custom-call(s32[6,128]{1,0:T(8,128)} %bitcast.9, s32[1,32]{1,0:T(1,128)} %bitcast.11, bf16[128,2560]{1,0:T(8,128)(2,1)} %tok_hbm.1, bf16[6,128,1024]{2,1,0:T(8,128)(2,1)} %bitcast.8, f32[6,128]{1,0:T(8,128)} %bitcast.10), custom_call_target="tpu_custom_call" | custom-call | tf_op jit(solution)/shard_map/pack_rows/pallas_call | solution.py:187
  4.5 18.4 %all-to-all-start = ((bf16[128,4,3072]{2,1,0:T(4,128)(2,1)}), bf16[128,4,3072]{2,1,0:T(4,128)(2,1)S(1)}, u32[]{:S(2)}, u32[]{:S(2)}) async-start(bf16[128,4,3072]{2,1,0:T(4,128)(2,1)} %pack_rows.1), calls=%async_computation | async-start | bytes 6291456 | tf_op jit(solution)/shard_map/all_to_all | solution.py:215
  22.9 4.4 %collective-permute-start = (bf16[1,2560,128]{2,1,0:T(8,128)(2,1)}, bf16[1,2560,128]{2,1,0:T(8,128)(2,1)S(1)}, u32[]{:S(2)}, u32[]{:S(2)}) collective-permute-start(bf16[1,2560,128]{2,1,0:T(8,128)(2,1)} %refs_0_), channel_id=1, source_target_pairs={{0,192},{64,0},{128,64},{192,128},{1,193},{65,1},{129,65},{193,129... | collective-permute-start | bytes 1966088 | tf_op jit(solution)/shard_map/ppermute | solution.py:170
  27.3 2.4 %collective-permute-start.2 = (bf16[1,2560,128]{2,1,0:T(8,128)(2,1)}, bf16[1,2560,128]{2,1,0:T(8,128)(2,1)}, u32[]{:S(2)}, u32[]{:S(2)}) collective-permute-start(bf16[1,2560,128]{2,1,0:T(8,128)(2,1)} %refs_0_), channel_id=1, source_target_pairs={{0,128},{64,192},{128,0},{192,64},{1,129},{65,193},{129,1},{193,65... | collective-permute-start | bytes 1966088 | tf_op jit(solution)/shard_map/ppermute | solution.py:170
  29.7 2.8 %collective-permute-start.1 = (bf16[1,2560,128]{2,1,0:T(8,128)(2,1)}, bf16[1,2560,128]{2,1,0:T(8,128)(2,1)}, u32[]{:S(2)}, u32[]{:S(2)}) collective-permute-start(bf16[1,2560,128]{2,1,0:T(8,128)(2,1)} %refs_1_), channel_id=1, source_target_pairs={{0,192},{64,0},{128,64},{192,128},{1,193},{65,1},{129,65},{193,129... | collective-permute-start | bytes 1966088 | tf_op jit(solution)/shard_map/ppermute | solution.py:170
  32.5 3.5 %collective-permute-start.3 = (bf16[1,2560,128]{2,1,0:T(8,128)(2,1)}, bf16[1,2560,128]{2,1,0:T(8,128)(2,1)}, u32[]{:S(2)}, u32[]{:S(2)}) collective-permute-start(bf16[1,2560,128]{2,1,0:T(8,128)(2,1)} %refs_1_), channel_id=1, source_target_pairs={{0,128},{64,192},{128,0},{192,64},{1,129},{65,193},{129,1},{193,65... | collective-permute-start | bytes 1966088 | tf_op jit(solution)/shard_map/ppermute | solution.py:170
  36.0 2.8 %collective-permute-start.4 = (bf16[1,2560,128]{2,1,0:T(8,128)(2,1)}, bf16[1,2560,128]{2,1,0:T(8,128)(2,1)}, u32[]{:S(2)}, u32[]{:S(2)}) collective-permute-start(bf16[1,2560,128]{2,1,0:T(8,128)(2,1)} %refs_0_), channel_id=1, source_target_pairs={{0,64},{64,128},{128,192},{192,0},{1,65},{65,129},{129,193},{193,1... | collective-permute-start | bytes 1966088 | tf_op jit(solution)/shard_map/ppermute | solution.py:170
  38.8 2.7 %collective-permute-done.refs_0_ = bf16[1,2560,128]{2,1,0:T(8,128)(2,1)S(1)} collective-permute-done((bf16[1,2560,128]{2,1,0:T(8,128)(2,1)}, bf16[1,2560,128]{2,1,0:T(8,128)(2,1)S(1)}, u32[]{:S(2)}, u32[]{:S(2)}) %collective-permute-start) | collective-permute-done | bytes 655392 | tf_op jit(solution)/shard_map/ppermute | solution.py:170
  41.5 0.8 copy-done.2
  42.4 1.9 %collective-permute-start.5 = (bf16[1,2560,128]{2,1,0:T(8,128)(2,1)}, bf16[1,2560,128]{2,1,0:T(8,128)(2,1)}, u32[]{:S(2)}, u32[]{:S(2)}) collective-permute-start(bf16[1,2560,128]{2,1,0:T(8,128)(2,1)} %refs_1_), channel_id=1, source_target_pairs={{0,64},{64,128},{128,192},{192,0},{1,65},{65,129},{129,193},{193,1... | collective-permute-start | bytes 1966088 | tf_op jit(solution)/shard_map/ppermute | solution.py:170
  44.3 25.2 %collective-permute-done.1.refs_1_ = bf16[1,2560,128]{2,1,0:T(8,128)(2,1)} collective-permute-done((bf16[1,2560,128]{2,1,0:T(8,128)(2,1)}, bf16[1,2560,128]{2,1,0:T(8,128)(2,1)}, u32[]{:S(2)}, u32[]{:S(2)}) %collective-permute-start.1) | collective-permute-done | bytes 655392 | tf_op jit(solution)/shard_map/ppermute | solution.py:170
  69.6 6.2 %collective-permute-done.4.refs_2_ = bf16[1,2560,128]{2,1,0:T(8,128)(2,1)} collective-permute-done((bf16[1,2560,128]{2,1,0:T(8,128)(2,1)}, bf16[1,2560,128]{2,1,0:T(8,128)(2,1)}, u32[]{:S(2)}, u32[]{:S(2)}) %collective-permute-start.4) | collective-permute-done | bytes 655392 | tf_op jit(solution)/shard_map/ppermute | solution.py:170
  75.7 14.0 %collective-permute-done.5.refs_3_ = bf16[1,2560,128]{2,1,0:T(8,128)(2,1)} collective-permute-done((bf16[1,2560,128]{2,1,0:T(8,128)(2,1)}, bf16[1,2560,128]{2,1,0:T(8,128)(2,1)}, u32[]{:S(2)}, u32[]{:S(2)}) %collective-permute-start.5) | collective-permute-done | bytes 655392 | tf_op jit(solution)/shard_map/ppermute | solution.py:170
  89.8 6.2 %all-to-all-done.recv_ref = bf16[128,4,3072]{2,1,0:T(4,128)(2,1)S(1)} async-done(((bf16[128,4,3072]{2,1,0:T(4,128)(2,1)}), bf16[128,4,3072]{2,1,0:T(4,128)(2,1)S(1)}, u32[]{:S(2)}, u32[]{:S(2)}) %all-to-all-start) | async-done | bytes 3145760 | tf_op jit(solution)/shard_map/all_to_all | solution.py:215
  96.0 3.9 %slice_grads.4 = (bf16[1,2560,128]{2,1,0:T(8,128)(2,1)}, bf16[1,2560,128]{2,1,0:T(8,128)(2,1)S(1)}) custom-call(s32[1]{0:T(128)} %bitcast.6.which_ref, bf16[128,4,3072]{2,1,0:T(4,128)(2,1)S(1)} %all-to-all-done.recv_ref, bf16[1,2560,128]{2,1,0:T(8,128)(2,1)} %collective-permute-done.2.refs_0_, bf16[1,2560,128]{2,1,0:T(8,128)(2,1)} %collective-permute-done.3.refs_1_), custom_call_target="tpu_custom_call" | custom-call | flops 1342177280 | bytes 5767168 | tf_op jit(solution)/shard_map/slice_grads/pallas_call | solution.py:147
  100.0 0.8 copy-done.4
  100.8 3.1 %collective-permute-start.6 = (bf16[1,2560,128]{2,1,0:T(8,128)(2,1)}, bf16[1,2560,128]{2,1,0:T(8,128)(2,1)}, u32[]{:S(2)}, u32[]{:S(2)}) collective-permute-start(bf16[1,2560,128]{2,1,0:T(8,128)(2,1)} %get-tuple-element.36), channel_id=1, source_target_pairs={{0,64},{64,128},{128,192},{192,0},{1,65},{65,129},{129,193},{193,1... | collective-permute-start | bytes 1966088 | tf_op jit(solution)/shard_map/ppermute | solution.py:170
  104.1 3.4 %collective-permute-start.7 = (bf16[1,2560,128]{2,1,0:T(8,128)(2,1)}, bf16[1,2560,128]{2,1,0:T(8,128)(2,1)S(1)}, u32[]{:S(2)}, u32[]{:S(2)}) collective-permute-start(bf16[1,2560,128]{2,1,0:T(8,128)(2,1)} %copy-done.4), channel_id=1, source_target_pairs={{0,192},{64,0},{128,64},{192,128},{1,193},{65,1},{129,65},{193,129... | collective-permute-start | bytes 1966088 | tf_op jit(solution)/shard_map/ppermute | solution.py:170
  107.5 1.1 copy-done.3
  108.6 5.1 %slice_grads.3 = (bf16[1,2560,128]{2,1,0:T(8,128)(2,1)S(1)}, bf16[1,2560,128]{2,1,0:T(8,128)(2,1)S(1)}, bf16[1,2560,128]{2,1,0:T(8,128)(2,1)S(1)}, bf16[1,2560,128]{2,1,0:T(8,128)(2,1)S(1)}) custom-call(s32[2]{0:T(128)S(1)} %slice.3.which_ref, bf16[128,4,3072]{2,1,0:T(4,128)(2,1)S(1)} %all-to-all-done.recv_ref, bf16[1,2560,128]{2,1,0:T(8,128)(2,1)S(1)} %copy-done.3, ...), custom_call_target="tpu_custom_call" | custom-call | flops 2684354560 | bytes 8388608 | tf_op jit(solution)/shard_map/slice_grads/pallas_call | solution.py:147
  113.7 1.9 %collective-permute-start.8 = (bf16[1,2560,128]{2,1,0:T(8,128)(2,1)S(1)}, bf16[1,2560,128]{2,1,0:T(8,128)(2,1)S(1)}, u32[]{:S(2)}, u32[]{:S(2)}) collective-permute-start(bf16[1,2560,128]{2,1,0:T(8,128)(2,1)S(1)} %get-tuple-element.42), channel_id=1, source_target_pairs={{0,64},{64,128},{128,192},{192,0},{1,65},{65,129},{129,193},{193,1... | collective-permute-start | bytes 1966088 | tf_op jit(solution)/shard_map/ppermute | solution.py:170
  115.7 4.6 %collective-permute-start.9 = (bf16[1,2560,128]{2,1,0:T(8,128)(2,1)S(1)}, bf16[1,2560,128]{2,1,0:T(8,128)(2,1)S(1)}, u32[]{:S(2)}, u32[]{:S(2)}) collective-permute-start(bf16[1,2560,128]{2,1,0:T(8,128)(2,1)S(1)} %get-tuple-element.43), channel_id=1, source_target_pairs={{0,192},{64,0},{128,64},{192,128},{1,193},{65,1},{129,65},{193,129... | collective-permute-start | bytes 1966088 | tf_op jit(solution)/shard_map/ppermute | solution.py:170
  120.3 1.3 add_convert_fusion.3
  121.5 2.1 %collective-permute-start.10 = (bf16[1,2560,128]{2,1,0:T(8,128)(2,1)S(1)}, bf16[1,2560,128]{2,1,0:T(8,128)(2,1)S(1)}, u32[]{:S(2)}, u32[]{:S(2)}) collective-permute-start(bf16[1,2560,128]{2,1,0:T(8,128)(2,1)S(1)} %add_convert_fusion.3), channel_id=1, source_target_pairs={{0,64},{64,128},{128,192},{192,0},{1,65},{65,129},{129,193},{193,1... | collective-permute-start | bytes 1966088 | tf_op jit(solution)/shard_map/ppermute | solution.py:170
  123.8 4.8 %collective-permute-start.11 = (bf16[1,2560,128]{2,1,0:T(8,128)(2,1)S(1)}, bf16[1,2560,128]{2,1,0:T(8,128)(2,1)S(1)}, u32[]{:S(2)}, u32[]{:S(2)}) collective-permute-start(bf16[1,2560,128]{2,1,0:T(8,128)(2,1)S(1)} %add_convert_fusion.2), channel_id=1, source_target_pairs={{0,192},{64,0},{128,64},{192,128},{1,193},{65,1},{129,65},{193,129... | collective-permute-start | bytes 1966088 | tf_op jit(solution)/shard_map/ppermute | solution.py:170
  128.6 2.4 %slice_grads.5 = (f32[1,2560,128]{2,1,0:T(8,128)S(1)}, f32[1,2560,128]{2,1,0:T(8,128)S(1)}) custom-call(s32[1]{0:T(128)} %bitcast.which_ref, bf16[128,4,3072]{2,1,0:T(4,128)(2,1)S(1)} %all-to-all-done.recv_ref, bf16[1,2560,128]{2,1,0:T(8,128)(2,1)S(1)} %copy-done, bf16[1,2560,128]{2,1,0:T(8,128)(2,1)S(1)} %copy-done.1), custom_call_target="tpu_custom_call" | custom-call | flops 1342177280 | bytes 5767168 | tf_op jit(solution)/shard_map/slice_grads/pallas_call | solution.py:147
  131.0 2.7 %collective-permute-done.8 = bf16[1,2560,128]{2,1,0:T(8,128)(2,1)S(1)} collective-permute-done((bf16[1,2560,128]{2,1,0:T(8,128)(2,1)S(1)}, bf16[1,2560,128]{2,1,0:T(8,128)(2,1)S(1)}, u32[]{:S(2)}, u32[]{:S(2)}) %collective-permute-start.8) | collective-permute-done | bytes 655392 | tf_op jit(solution)/shard_map/ppermute | solution.py:170
  133.7 1.4 collective-permute-done.9
  135.0 12.6 %collective-permute-done.10 = bf16[1,2560,128]{2,1,0:T(8,128)(2,1)S(1)} collective-permute-done((bf16[1,2560,128]{2,1,0:T(8,128)(2,1)S(1)}, bf16[1,2560,128]{2,1,0:T(8,128)(2,1)S(1)}, u32[]{:S(2)}, u32[]{:S(2)}) %collective-permute-start.10) | collective-permute-done | bytes 655392 | tf_op jit(solution)/shard_map/ppermute | solution.py:170
  147.7 1.1 add_convert_fusion.1
  148.8 0.3 collective-permute-done.11
  149.1 1.1 add_convert_fusion
  (14 shorter events, 0.4 us)
Async XLA Ops:
  4.5 91.5 %all-to-all-start = ((bf16[128,4,3072]{2,1,0:T(4,128)(2,1)}), bf16[128,4,3072]{2,1,0:T(4,128)(2,1)S(1)}, u32[]{:S(2)}, u32[]{:S(2)}) async-start(bf16[128,4,3072]{2,1,0:T(4,128)(2,1)} %pack_rows.1), calls=%async_computation | async-start | bytes 6291456 | tf_op jit(solution)/shard_map/all_to_all | solution.py:215
  22.9 18.6 %collective-permute-start = (bf16[1,2560,128]{2,1,0:T(8,128)(2,1)}, bf16[1,2560,128]{2,1,0:T(8,128)(2,1)S(1)}, u32[]{:S(2)}, u32[]{:S(2)}) collective-permute-start(bf16[1,2560,128]{2,1,0:T(8,128)(2,1)} %refs_0_), channel_id=1, source_target_pairs={{0,192},{64,0},{128,64},{192,128},{1,193},{65,1},{129,65},{193,129... | collective-permute-start | bytes 1966088 | tf_op jit(solution)/shard_map/ppermute | solution.py:170
  27.3 42.3 %collective-permute-start.2 = (bf16[1,2560,128]{2,1,0:T(8,128)(2,1)}, bf16[1,2560,128]{2,1,0:T(8,128)(2,1)}, u32[]{:S(2)}, u32[]{:S(2)}) collective-permute-start(bf16[1,2560,128]{2,1,0:T(8,128)(2,1)} %refs_0_), channel_id=1, source_target_pairs={{0,128},{64,192},{128,0},{192,64},{1,129},{65,193},{129,1},{193,65... | collective-permute-start | bytes 1966088 | tf_op jit(solution)/shard_map/ppermute | solution.py:170
  29.7 39.8 %collective-permute-start.1 = (bf16[1,2560,128]{2,1,0:T(8,128)(2,1)}, bf16[1,2560,128]{2,1,0:T(8,128)(2,1)}, u32[]{:S(2)}, u32[]{:S(2)}) collective-permute-start(bf16[1,2560,128]{2,1,0:T(8,128)(2,1)} %refs_1_), channel_id=1, source_target_pairs={{0,192},{64,0},{128,64},{192,128},{1,193},{65,1},{129,65},{193,129... | collective-permute-start | bytes 1966088 | tf_op jit(solution)/shard_map/ppermute | solution.py:170
  32.5 37.1 %collective-permute-start.3 = (bf16[1,2560,128]{2,1,0:T(8,128)(2,1)}, bf16[1,2560,128]{2,1,0:T(8,128)(2,1)}, u32[]{:S(2)}, u32[]{:S(2)}) collective-permute-start(bf16[1,2560,128]{2,1,0:T(8,128)(2,1)} %refs_1_), channel_id=1, source_target_pairs={{0,128},{64,192},{128,0},{192,64},{1,129},{65,193},{129,1},{193,65... | collective-permute-start | bytes 1966088 | tf_op jit(solution)/shard_map/ppermute | solution.py:170
  36.0 39.7 %collective-permute-start.4 = (bf16[1,2560,128]{2,1,0:T(8,128)(2,1)}, bf16[1,2560,128]{2,1,0:T(8,128)(2,1)}, u32[]{:S(2)}, u32[]{:S(2)}) collective-permute-start(bf16[1,2560,128]{2,1,0:T(8,128)(2,1)} %refs_0_), channel_id=1, source_target_pairs={{0,64},{64,128},{128,192},{192,0},{1,65},{65,129},{129,193},{193,1... | collective-permute-start | bytes 1966088 | tf_op jit(solution)/shard_map/ppermute | solution.py:170
  41.5 0.8 copy-start.2
  42.4 47.4 %collective-permute-start.5 = (bf16[1,2560,128]{2,1,0:T(8,128)(2,1)}, bf16[1,2560,128]{2,1,0:T(8,128)(2,1)}, u32[]{:S(2)}, u32[]{:S(2)}) collective-permute-start(bf16[1,2560,128]{2,1,0:T(8,128)(2,1)} %refs_1_), channel_id=1, source_target_pairs={{0,64},{64,128},{128,192},{192,0},{1,65},{65,129},{129,193},{193,1... | collective-permute-start | bytes 1966088 | tf_op jit(solution)/shard_map/ppermute | solution.py:170
  99.9 0.9 copy-start.4
  100.8 19.4 %collective-permute-start.6 = (bf16[1,2560,128]{2,1,0:T(8,128)(2,1)}, bf16[1,2560,128]{2,1,0:T(8,128)(2,1)}, u32[]{:S(2)}, u32[]{:S(2)}) collective-permute-start(bf16[1,2560,128]{2,1,0:T(8,128)(2,1)} %get-tuple-element.36), channel_id=1, source_target_pairs={{0,64},{64,128},{128,192},{192,0},{1,65},{65,129},{129,193},{193,1... | collective-permute-start | bytes 1966088 | tf_op jit(solution)/shard_map/ppermute | solution.py:170
  104.1 19.5 %collective-permute-start.7 = (bf16[1,2560,128]{2,1,0:T(8,128)(2,1)}, bf16[1,2560,128]{2,1,0:T(8,128)(2,1)S(1)}, u32[]{:S(2)}, u32[]{:S(2)}) collective-permute-start(bf16[1,2560,128]{2,1,0:T(8,128)(2,1)} %copy-done.4), channel_id=1, source_target_pairs={{0,192},{64,0},{128,64},{192,128},{1,193},{65,1},{129,65},{193,129... | collective-permute-start | bytes 1966088 | tf_op jit(solution)/shard_map/ppermute | solution.py:170
  107.5 1.1 copy-start.3
  113.7 19.9 %collective-permute-start.8 = (bf16[1,2560,128]{2,1,0:T(8,128)(2,1)S(1)}, bf16[1,2560,128]{2,1,0:T(8,128)(2,1)S(1)}, u32[]{:S(2)}, u32[]{:S(2)}) collective-permute-start(bf16[1,2560,128]{2,1,0:T(8,128)(2,1)S(1)} %get-tuple-element.42), channel_id=1, source_target_pairs={{0,64},{64,128},{128,192},{192,0},{1,65},{65,129},{129,193},{193,1... | collective-permute-start | bytes 1966088 | tf_op jit(solution)/shard_map/ppermute | solution.py:170
  115.7 19.4 %collective-permute-start.9 = (bf16[1,2560,128]{2,1,0:T(8,128)(2,1)S(1)}, bf16[1,2560,128]{2,1,0:T(8,128)(2,1)S(1)}, u32[]{:S(2)}, u32[]{:S(2)}) collective-permute-start(bf16[1,2560,128]{2,1,0:T(8,128)(2,1)S(1)} %get-tuple-element.43), channel_id=1, source_target_pairs={{0,192},{64,0},{128,64},{192,128},{1,193},{65,1},{129,65},{193,129... | collective-permute-start | bytes 1966088 | tf_op jit(solution)/shard_map/ppermute | solution.py:170
  121.5 7.0 %copy-start = (bf16[1,2560,128]{2,1,0:T(8,128)(2,1)S(1)}, bf16[1,2560,128]{2,1,0:T(8,128)(2,1)}, u32[]{:S(2)}) copy-start(bf16[1,2560,128]{2,1,0:T(8,128)(2,1)} %refs_0_) | copy-start | bytes 1966084
  121.5 7.0 %copy-start.1 = (bf16[1,2560,128]{2,1,0:T(8,128)(2,1)S(1)}, bf16[1,2560,128]{2,1,0:T(8,128)(2,1)}, u32[]{:S(2)}) copy-start(bf16[1,2560,128]{2,1,0:T(8,128)(2,1)} %refs_1_) | copy-start | bytes 1966084
  121.5 26.2 %collective-permute-start.10 = (bf16[1,2560,128]{2,1,0:T(8,128)(2,1)S(1)}, bf16[1,2560,128]{2,1,0:T(8,128)(2,1)S(1)}, u32[]{:S(2)}, u32[]{:S(2)}) collective-permute-start(bf16[1,2560,128]{2,1,0:T(8,128)(2,1)S(1)} %add_convert_fusion.3), channel_id=1, source_target_pairs={{0,64},{64,128},{128,192},{192,0},{1,65},{65,129},{129,193},{193,1... | collective-permute-start | bytes 1966088 | tf_op jit(solution)/shard_map/ppermute | solution.py:170
  123.8 25.3 %collective-permute-start.11 = (bf16[1,2560,128]{2,1,0:T(8,128)(2,1)S(1)}, bf16[1,2560,128]{2,1,0:T(8,128)(2,1)S(1)}, u32[]{:S(2)}, u32[]{:S(2)}) collective-permute-start(bf16[1,2560,128]{2,1,0:T(8,128)(2,1)S(1)} %add_convert_fusion.2), channel_id=1, source_target_pairs={{0,192},{64,0},{128,64},{192,128},{1,193},{65,1},{129,65},{193,129... | collective-permute-start | bytes 1966088 | tf_op jit(solution)/shard_map/ppermute | solution.py:170

commit v9 on v8

--- a/solution.py
+++ b/solution.py
@@ -157,7 +157,7 @@
         ],
         compiler_params=pltpu.CompilerParams(vmem_limit_bytes=SLICE_VMEM),
         cost_estimate=pl.CostEstimate(
-            flops=8 * rows * count * width * hidden,
+            flops=32 * rows * count * width * hidden,
             bytes_accessed=2 * recv.size + 8 * count * width * hidden,
             transcendentals=0,
         ),

time: 153 us -> 151 us (0.987)
  local copies, waits for them, and re-layouts: 2.88 us -> 0.95 us
  waiting for transfers between devices: 71.4 us -> 73.2 us
    unnamed x10 -> x8, local copies, waits for them, and re-layouts: 2.78 us -> 0.85 us
    ppermute x12, waiting for transfers between devices: 65.2 us -> 67 us  [moved(): lax.ppermute(block, 'x', [(i, (i + distance) % planes) for i in range(pla...]
  transfers between devices with their start and end apart: 13 -> 13, of which waited for: 9 -> 9; matrix products, arithmetic and copies ran while one was open for 2% -> 1% of each run, Pallas kernels for 5% -> 5%
where the time goes in v9:
time: 151 us; the launch traced here: 148 us
  waiting for transfers between devices  73.2 us (48%)
  starting transfers between devices  56 us (37%)
  Pallas kernels  14.5 us (10%)
  other arithmetic  2.65 us (2%)
    ppermute x12, waiting for transfers between devices, moved(): lax.ppermute(block, 'x', [(i, (i + distance) % planes) for i in range(pla...  67 us
    ppermute x12, starting transfers between devices, moved(): lax.ppermute(block, 'x', [(i, (i + distance) % planes) for i in range(pla...  37.6 us
    all_to_all x1, starting transfers between devices, body(): recv = lax.all_to_all(send, PLANE, 0, 0, tiled=True)  18.4 us
    pallas_call x3, Pallas kernels, slice_grads(): pl.pallas_call(functools.partial(slices_kernel, count), in_specs=[pl.Bloc...  10.7 us
    all_to_all x1, waiting for transfers between devices, body(): recv = lax.all_to_all(send, PLANE, 0, 0, tiled=True)  6.21 us
    pallas_call x1, Pallas kernels, body(): pl.pallas_call(pack_kernel, in_specs=[anywhere] * 5, out_specs=anywhere,...  3.79 us
  transfers between devices with their start and end apart: 13, of which 9 were waited for; matrix products, arithmetic and copies ran while one was open for 1% of the time, Pallas kernels for 5%

profile of v9, /device:TPU:1, one launch (start us, length us, event | category | flops | bytes accessed | tf_op | source)
XLA Modules:
  0.0 148.2 jit_solution(15467483133589193465)
XLA Ops:
  0.6 3.8 %pack_rows.1 = bf16[128,4,3072]{2,1,0:T(4,128)(2,1)} custom-call(s32[6,128]{1,0:T(8,128)} %bitcast.9, s32[1,32]{1,0:T(1,128)} %bitcast.11, bf16[128,2560]{1,0:T(8,128)(2,1)} %tok_hbm.1, bf16[6,128,1024]{2,1,0:T(8,128)(2,1)} %bitcast.8, f32[6,128]{1,0:T(8,128)} %bitcast.10), custom_call_target="tpu_custom_call" | custom-call | tf_op jit(solution)/shard_map/pack_rows/pallas_call | solution.py:187
  4.4 18.4 %all-to-all-start = ((bf16[128,4,3072]{2,1,0:T(4,128)(2,1)}), bf16[128,4,3072]{2,1,0:T(4,128)(2,1)S(1)}, u32[]{:S(2)}, u32[]{:S(2)}) async-start(bf16[128,4,3072]{2,1,0:T(4,128)(2,1)} %pack_rows.1), calls=%async_computation | async-start | bytes 6291456 | tf_op jit(solution)/shard_map/all_to_all | solution.py:215
  22.9 4.4 %collective-permute-start = (bf16[1,2560,128]{2,1,0:T(8,128)(2,1)}, bf16[1,2560,128]{2,1,0:T(8,128)(2,1)S(1)}, u32[]{:S(2)}, u32[]{:S(2)}) collective-permute-start(bf16[1,2560,128]{2,1,0:T(8,128)(2,1)} %refs_0_), channel_id=1, source_target_pairs={{0,192},{64,0},{128,64},{192,128},{1,193},{65,1},{129,65},{193,129... | collective-permute-start | bytes 1966088 | tf_op jit(solution)/shard_map/ppermute | solution.py:170
  27.3 2.4 %collective-permute-start.2 = (bf16[1,2560,128]{2,1,0:T(8,128)(2,1)}, bf16[1,2560,128]{2,1,0:T(8,128)(2,1)}, u32[]{:S(2)}, u32[]{:S(2)}) collective-permute-start(bf16[1,2560,128]{2,1,0:T(8,128)(2,1)} %refs_0_), channel_id=1, source_target_pairs={{0,128},{64,192},{128,0},{192,64},{1,129},{65,193},{129,1},{193,65... | collective-permute-start | bytes 1966088 | tf_op jit(solution)/shard_map/ppermute | solution.py:170
  29.7 2.8 %collective-permute-start.1 = (bf16[1,2560,128]{2,1,0:T(8,128)(2,1)}, bf16[1,2560,128]{2,1,0:T(8,128)(2,1)}, u32[]{:S(2)}, u32[]{:S(2)}) collective-permute-start(bf16[1,2560,128]{2,1,0:T(8,128)(2,1)} %refs_1_), channel_id=1, source_target_pairs={{0,192},{64,0},{128,64},{192,128},{1,193},{65,1},{129,65},{193,129... | collective-permute-start | bytes 1966088 | tf_op jit(solution)/shard_map/ppermute | solution.py:170
  32.5 3.5 %collective-permute-start.3 = (bf16[1,2560,128]{2,1,0:T(8,128)(2,1)}, bf16[1,2560,128]{2,1,0:T(8,128)(2,1)}, u32[]{:S(2)}, u32[]{:S(2)}) collective-permute-start(bf16[1,2560,128]{2,1,0:T(8,128)(2,1)} %refs_1_), channel_id=1, source_target_pairs={{0,128},{64,192},{128,0},{192,64},{1,129},{65,193},{129,1},{193,65... | collective-permute-start | bytes 1966088 | tf_op jit(solution)/shard_map/ppermute | solution.py:170
  36.0 2.8 %collective-permute-start.4 = (bf16[1,2560,128]{2,1,0:T(8,128)(2,1)}, bf16[1,2560,128]{2,1,0:T(8,128)(2,1)}, u32[]{:S(2)}, u32[]{:S(2)}) collective-permute-start(bf16[1,2560,128]{2,1,0:T(8,128)(2,1)} %refs_0_), channel_id=1, source_target_pairs={{0,64},{64,128},{128,192},{192,0},{1,65},{65,129},{129,193},{193,1... | collective-permute-start | bytes 1966088 | tf_op jit(solution)/shard_map/ppermute | solution.py:170
  38.8 2.7 %collective-permute-done.refs_0_ = bf16[1,2560,128]{2,1,0:T(8,128)(2,1)S(1)} collective-permute-done((bf16[1,2560,128]{2,1,0:T(8,128)(2,1)}, bf16[1,2560,128]{2,1,0:T(8,128)(2,1)S(1)}, u32[]{:S(2)}, u32[]{:S(2)}) %collective-permute-start) | collective-permute-done | bytes 655392 | tf_op jit(solution)/shard_map/ppermute | solution.py:170
  41.5 0.8 copy-done.2
  42.3 1.9 %collective-permute-start.5 = (bf16[1,2560,128]{2,1,0:T(8,128)(2,1)}, bf16[1,2560,128]{2,1,0:T(8,128)(2,1)}, u32[]{:S(2)}, u32[]{:S(2)}) collective-permute-start(bf16[1,2560,128]{2,1,0:T(8,128)(2,1)} %refs_1_), channel_id=1, source_target_pairs={{0,64},{64,128},{128,192},{192,0},{1,65},{65,129},{129,193},{193,1... | collective-permute-start | bytes 1966088 | tf_op jit(solution)/shard_map/ppermute | solution.py:170
  44.4 0.1 slice.3.which_ref
  44.5 25.1 %collective-permute-done.1.refs_1_ = bf16[1,2560,128]{2,1,0:T(8,128)(2,1)} collective-permute-done((bf16[1,2560,128]{2,1,0:T(8,128)(2,1)}, bf16[1,2560,128]{2,1,0:T(8,128)(2,1)}, u32[]{:S(2)}, u32[]{:S(2)}) %collective-permute-start.1) | collective-permute-done | bytes 655392 | tf_op jit(solution)/shard_map/ppermute | solution.py:170
  69.5 6.2 %collective-permute-done.4.refs_2_ = bf16[1,2560,128]{2,1,0:T(8,128)(2,1)} collective-permute-done((bf16[1,2560,128]{2,1,0:T(8,128)(2,1)}, bf16[1,2560,128]{2,1,0:T(8,128)(2,1)}, u32[]{:S(2)}, u32[]{:S(2)}) %collective-permute-start.4) | collective-permute-done | bytes 655392 | tf_op jit(solution)/shard_map/ppermute | solution.py:170
  75.7 14.0 %collective-permute-done.5.refs_3_ = bf16[1,2560,128]{2,1,0:T(8,128)(2,1)} collective-permute-done((bf16[1,2560,128]{2,1,0:T(8,128)(2,1)}, bf16[1,2560,128]{2,1,0:T(8,128)(2,1)}, u32[]{:S(2)}, u32[]{:S(2)}) %collective-permute-start.5) | collective-permute-done | bytes 655392 | tf_op jit(solution)/shard_map/ppermute | solution.py:170
  89.8 6.2 %all-to-all-done.recv_ref = bf16[128,4,3072]{2,1,0:T(4,128)(2,1)S(1)} async-done(((bf16[128,4,3072]{2,1,0:T(4,128)(2,1)}), bf16[128,4,3072]{2,1,0:T(4,128)(2,1)S(1)}, u32[]{:S(2)}, u32[]{:S(2)}) %all-to-all-start) | async-done | bytes 3145760 | tf_op jit(solution)/shard_map/all_to_all | solution.py:215
  96.0 3.2 %slice_grads.4 = (bf16[1,2560,128]{2,1,0:T(8,128)(2,1)S(1)}, bf16[1,2560,128]{2,1,0:T(8,128)(2,1)S(1)}) custom-call(s32[1]{0:T(128)} %bitcast.6.which_ref, bf16[128,4,3072]{2,1,0:T(4,128)(2,1)S(1)} %all-to-all-done.recv_ref, bf16[1,2560,128]{2,1,0:T(8,128)(2,1)} %collective-permute-done.2.refs_0_, bf16[1,2560,128]{2,1,0:T(8,128)(2,1)} %collective-permute-done.3.refs_1_), custom_call_target="tpu_custom_call" | custom-call | flops 5368709120 | bytes 5767168 | tf_op jit(solution)/shard_map/slice_grads/pallas_call | solution.py:147
  99.1 3.1 %collective-permute-start.6 = (bf16[1,2560,128]{2,1,0:T(8,128)(2,1)S(1)}, bf16[1,2560,128]{2,1,0:T(8,128)(2,1)S(1)}, u32[]{:S(2)}, u32[]{:S(2)}) collective-permute-start(bf16[1,2560,128]{2,1,0:T(8,128)(2,1)S(1)} %get-tuple-element.36), channel_id=1, source_target_pairs={{0,64},{64,128},{128,192},{192,0},{1,65},{65,129},{129,193},{193,1... | collective-permute-start | bytes 1966088 | tf_op jit(solution)/shard_map/ppermute | solution.py:170
  102.3 3.4 %collective-permute-start.7 = (bf16[1,2560,128]{2,1,0:T(8,128)(2,1)S(1)}, bf16[1,2560,128]{2,1,0:T(8,128)(2,1)S(1)}, u32[]{:S(2)}, u32[]{:S(2)}) collective-permute-start(bf16[1,2560,128]{2,1,0:T(8,128)(2,1)S(1)} %get-tuple-element.38), channel_id=1, source_target_pairs={{0,192},{64,0},{128,64},{192,128},{1,193},{65,1},{129,65},{193,129... | collective-permute-start | bytes 1966088 | tf_op jit(solution)/shard_map/ppermute | solution.py:170
  105.7 5.1 %slice_grads.3 = (bf16[1,2560,128]{2,1,0:T(8,128)(2,1)S(1)}, bf16[1,2560,128]{2,1,0:T(8,128)(2,1)S(1)}, bf16[1,2560,128]{2,1,0:T(8,128)(2,1)S(1)}, bf16[1,2560,128]{2,1,0:T(8,128)(2,1)S(1)}) custom-call(s32[2]{0:T(128)S(1)} %slice.3.which_ref, bf16[128,4,3072]{2,1,0:T(4,128)(2,1)S(1)} %all-to-all-done.recv_ref, bf16[1,2560,128]{2,1,0:T(8,128)(2,1)S(1)} %copy-done.3, ...), custom_call_target="tpu_custom_call" | custom-call | flops 10737418240 | bytes 8388608 | tf_op jit(solution)/shard_map/slice_grads/pallas_call | solution.py:147
  110.8 1.9 %collective-permute-start.8 = (bf16[1,2560,128]{2,1,0:T(8,128)(2,1)S(1)}, bf16[1,2560,128]{2,1,0:T(8,128)(2,1)S(1)}, u32[]{:S(2)}, u32[]{:S(2)}) collective-permute-start(bf16[1,2560,128]{2,1,0:T(8,128)(2,1)S(1)} %get-tuple-element.42), channel_id=1, source_target_pairs={{0,64},{64,128},{128,192},{192,0},{1,65},{65,129},{129,193},{193,1... | collective-permute-start | bytes 1966088 | tf_op jit(solution)/shard_map/ppermute | solution.py:170
  112.7 4.6 %collective-permute-start.9 = (bf16[1,2560,128]{2,1,0:T(8,128)(2,1)S(1)}, bf16[1,2560,128]{2,1,0:T(8,128)(2,1)S(1)}, u32[]{:S(2)}, u32[]{:S(2)}) collective-permute-start(bf16[1,2560,128]{2,1,0:T(8,128)(2,1)S(1)} %get-tuple-element.43), channel_id=1, source_target_pairs={{0,192},{64,0},{128,64},{192,128},{1,193},{65,1},{129,65},{193,129... | collective-permute-start | bytes 1966088 | tf_op jit(solution)/shard_map/ppermute | solution.py:170
  117.3 0.2 add_convert_fusion.3
  117.5 2.1 %collective-permute-start.10 = (bf16[1,2560,128]{2,1,0:T(8,128)(2,1)S(1)}, bf16[1,2560,128]{2,1,0:T(8,128)(2,1)S(1)}, u32[]{:S(2)}, u32[]{:S(2)}) collective-permute-start(bf16[1,2560,128]{2,1,0:T(8,128)(2,1)S(1)} %add_convert_fusion.3), channel_id=1, source_target_pairs={{0,64},{64,128},{128,192},{192,0},{1,65},{65,129},{129,193},{193,1... | collective-permute-start | bytes 1966088 | tf_op jit(solution)/shard_map/ppermute | solution.py:170
  119.6 0.2 add_convert_fusion.2
  119.8 4.8 %collective-permute-start.11 = (bf16[1,2560,128]{2,1,0:T(8,128)(2,1)S(1)}, bf16[1,2560,128]{2,1,0:T(8,128)(2,1)S(1)}, u32[]{:S(2)}, u32[]{:S(2)}) collective-permute-start(bf16[1,2560,128]{2,1,0:T(8,128)(2,1)S(1)} %add_convert_fusion.2), channel_id=1, source_target_pairs={{0,192},{64,0},{128,64},{192,128},{1,193},{65,1},{129,65},{193,129... | collective-permute-start | bytes 1966088 | tf_op jit(solution)/shard_map/ppermute | solution.py:170
  124.6 2.4 %slice_grads.5 = (f32[1,2560,128]{2,1,0:T(8,128)S(1)}, f32[1,2560,128]{2,1,0:T(8,128)S(1)}) custom-call(s32[1]{0:T(128)} %bitcast.which_ref, bf16[128,4,3072]{2,1,0:T(4,128)(2,1)S(1)} %all-to-all-done.recv_ref, bf16[1,2560,128]{2,1,0:T(8,128)(2,1)S(1)} %copy-done, bf16[1,2560,128]{2,1,0:T(8,128)(2,1)S(1)} %copy-done.1), custom_call_target="tpu_custom_call" | custom-call | flops 5368709120 | bytes 5767168 | tf_op jit(solution)/shard_map/slice_grads/pallas_call | solution.py:147
  127.0 4.4 %collective-permute-done.8 = bf16[1,2560,128]{2,1,0:T(8,128)(2,1)S(1)} collective-permute-done((bf16[1,2560,128]{2,1,0:T(8,128)(2,1)S(1)}, bf16[1,2560,128]{2,1,0:T(8,128)(2,1)S(1)}, u32[]{:S(2)}, u32[]{:S(2)}) %collective-permute-start.8) | collective-permute-done | bytes 655392 | tf_op jit(solution)/shard_map/ppermute | solution.py:170
  131.4 1.6 %collective-permute-done.9 = bf16[1,2560,128]{2,1,0:T(8,128)(2,1)S(1)} collective-permute-done((bf16[1,2560,128]{2,1,0:T(8,128)(2,1)S(1)}, bf16[1,2560,128]{2,1,0:T(8,128)(2,1)S(1)}, u32[]{:S(2)}, u32[]{:S(2)}) %collective-permute-start.9) | collective-permute-done | bytes 655392 | tf_op jit(solution)/shard_map/ppermute | solution.py:170
  133.0 12.4 %collective-permute-done.10 = bf16[1,2560,128]{2,1,0:T(8,128)(2,1)S(1)} collective-permute-done((bf16[1,2560,128]{2,1,0:T(8,128)(2,1)S(1)}, bf16[1,2560,128]{2,1,0:T(8,128)(2,1)S(1)}, u32[]{:S(2)}, u32[]{:S(2)}) %collective-permute-start.10) | collective-permute-done | bytes 655392 | tf_op jit(solution)/shard_map/ppermute | solution.py:170
  145.4 1.1 add_convert_fusion.1
  146.5 0.5 collective-permute-done.11
  147.0 1.1 add_convert_fusion
  (12 shorter events, 0.1 us)
Async XLA Ops:
  4.4 91.5 %all-to-all-start = ((bf16[128,4,3072]{2,1,0:T(4,128)(2,1)}), bf16[128,4,3072]{2,1,0:T(4,128)(2,1)S(1)}, u32[]{:S(2)}, u32[]{:S(2)}) async-start(bf16[128,4,3072]{2,1,0:T(4,128)(2,1)} %pack_rows.1), calls=%async_computation | async-start | bytes 6291456 | tf_op jit(solution)/shard_map/all_to_all | solution.py:215
  22.9 18.6 %collective-permute-start = (bf16[1,2560,128]{2,1,0:T(8,128)(2,1)}, bf16[1,2560,128]{2,1,0:T(8,128)(2,1)S(1)}, u32[]{:S(2)}, u32[]{:S(2)}) collective-permute-start(bf16[1,2560,128]{2,1,0:T(8,128)(2,1)} %refs_0_), channel_id=1, source_target_pairs={{0,192},{64,0},{128,64},{192,128},{1,193},{65,1},{129,65},{193,129... | collective-permute-start | bytes 1966088 | tf_op jit(solution)/shard_map/ppermute | solution.py:170
  27.3 42.3 %collective-permute-start.2 = (bf16[1,2560,128]{2,1,0:T(8,128)(2,1)}, bf16[1,2560,128]{2,1,0:T(8,128)(2,1)}, u32[]{:S(2)}, u32[]{:S(2)}) collective-permute-start(bf16[1,2560,128]{2,1,0:T(8,128)(2,1)} %refs_0_), channel_id=1, source_target_pairs={{0,128},{64,192},{128,0},{192,64},{1,129},{65,193},{129,1},{193,65... | collective-permute-start | bytes 1966088 | tf_op jit(solution)/shard_map/ppermute | solution.py:170
  29.7 39.8 %collective-permute-start.1 = (bf16[1,2560,128]{2,1,0:T(8,128)(2,1)}, bf16[1,2560,128]{2,1,0:T(8,128)(2,1)}, u32[]{:S(2)}, u32[]{:S(2)}) collective-permute-start(bf16[1,2560,128]{2,1,0:T(8,128)(2,1)} %refs_1_), channel_id=1, source_target_pairs={{0,192},{64,0},{128,64},{192,128},{1,193},{65,1},{129,65},{193,129... | collective-permute-start | bytes 1966088 | tf_op jit(solution)/shard_map/ppermute | solution.py:170
  32.5 37.1 %collective-permute-start.3 = (bf16[1,2560,128]{2,1,0:T(8,128)(2,1)}, bf16[1,2560,128]{2,1,0:T(8,128)(2,1)}, u32[]{:S(2)}, u32[]{:S(2)}) collective-permute-start(bf16[1,2560,128]{2,1,0:T(8,128)(2,1)} %refs_1_), channel_id=1, source_target_pairs={{0,128},{64,192},{128,0},{192,64},{1,129},{65,193},{129,1},{193,65... | collective-permute-start | bytes 1966088 | tf_op jit(solution)/shard_map/ppermute | solution.py:170
  36.0 39.7 %collective-permute-start.4 = (bf16[1,2560,128]{2,1,0:T(8,128)(2,1)}, bf16[1,2560,128]{2,1,0:T(8,128)(2,1)}, u32[]{:S(2)}, u32[]{:S(2)}) collective-permute-start(bf16[1,2560,128]{2,1,0:T(8,128)(2,1)} %refs_0_), channel_id=1, source_target_pairs={{0,64},{64,128},{128,192},{192,0},{1,65},{65,129},{129,193},{193,1... | collective-permute-start | bytes 1966088 | tf_op jit(solution)/shard_map/ppermute | solution.py:170
  41.5 0.8 copy-start.2
  42.3 47.4 %collective-permute-start.5 = (bf16[1,2560,128]{2,1,0:T(8,128)(2,1)}, bf16[1,2560,128]{2,1,0:T(8,128)(2,1)}, u32[]{:S(2)}, u32[]{:S(2)}) collective-permute-start(bf16[1,2560,128]{2,1,0:T(8,128)(2,1)} %refs_1_), channel_id=1, source_target_pairs={{0,64},{64,128},{128,192},{192,0},{1,65},{65,129},{129,193},{193,1... | collective-permute-start | bytes 1966088 | tf_op jit(solution)/shard_map/ppermute | solution.py:170
  96.0 9.7 %copy-start.3 = (bf16[1,2560,128]{2,1,0:T(8,128)(2,1)S(1)}, bf16[1,2560,128]{2,1,0:T(8,128)(2,1)}, u32[]{:S(2)}) copy-start(bf16[1,2560,128]{2,1,0:T(8,128)(2,1)} %copy-done.2) | copy-start | bytes 1966084
  99.1 18.2 %collective-permute-start.6 = (bf16[1,2560,128]{2,1,0:T(8,128)(2,1)S(1)}, bf16[1,2560,128]{2,1,0:T(8,128)(2,1)S(1)}, u32[]{:S(2)}, u32[]{:S(2)}) collective-permute-start(bf16[1,2560,128]{2,1,0:T(8,128)(2,1)S(1)} %get-tuple-element.36), channel_id=1, source_target_pairs={{0,64},{64,128},{128,192},{192,0},{1,65},{65,129},{129,193},{193,1... | collective-permute-start | bytes 1966088 | tf_op jit(solution)/shard_map/ppermute | solution.py:170
  102.3 17.3 %collective-permute-start.7 = (bf16[1,2560,128]{2,1,0:T(8,128)(2,1)S(1)}, bf16[1,2560,128]{2,1,0:T(8,128)(2,1)S(1)}, u32[]{:S(2)}, u32[]{:S(2)}) collective-permute-start(bf16[1,2560,128]{2,1,0:T(8,128)(2,1)S(1)} %get-tuple-element.38), channel_id=1, source_target_pairs={{0,192},{64,0},{128,64},{192,128},{1,193},{65,1},{129,65},{193,129... | collective-permute-start | bytes 1966088 | tf_op jit(solution)/shard_map/ppermute | solution.py:170
  110.8 20.6 %collective-permute-start.8 = (bf16[1,2560,128]{2,1,0:T(8,128)(2,1)S(1)}, bf16[1,2560,128]{2,1,0:T(8,128)(2,1)S(1)}, u32[]{:S(2)}, u32[]{:S(2)}) collective-permute-start(bf16[1,2560,128]{2,1,0:T(8,128)(2,1)S(1)} %get-tuple-element.42), channel_id=1, source_target_pairs={{0,64},{64,128},{128,192},{192,0},{1,65},{65,129},{129,193},{193,1... | collective-permute-start | bytes 1966088 | tf_op jit(solution)/shard_map/ppermute | solution.py:170
  112.7 20.3 %collective-permute-start.9 = (bf16[1,2560,128]{2,1,0:T(8,128)(2,1)S(1)}, bf16[1,2560,128]{2,1,0:T(8,128)(2,1)S(1)}, u32[]{:S(2)}, u32[]{:S(2)}) collective-permute-start(bf16[1,2560,128]{2,1,0:T(8,128)(2,1)S(1)} %get-tuple-element.43), channel_id=1, source_target_pairs={{0,192},{64,0},{128,64},{192,128},{1,193},{65,1},{129,65},{193,129... | collective-permute-start | bytes 1966088 | tf_op jit(solution)/shard_map/ppermute | solution.py:170
  117.5 7.0 %copy-start = (bf16[1,2560,128]{2,1,0:T(8,128)(2,1)S(1)}, bf16[1,2560,128]{2,1,0:T(8,128)(2,1)}, u32[]{:S(2)}) copy-start(bf16[1,2560,128]{2,1,0:T(8,128)(2,1)} %refs_0_) | copy-start | bytes 1966084
  117.5 7.0 %copy-start.1 = (bf16[1,2560,128]{2,1,0:T(8,128)(2,1)S(1)}, bf16[1,2560,128]{2,1,0:T(8,128)(2,1)}, u32[]{:S(2)}) copy-start(bf16[1,2560,128]{2,1,0:T(8,128)(2,1)} %refs_1_) | copy-start | bytes 1966084
  117.5 27.9 %collective-permute-start.10 = (bf16[1,2560,128]{2,1,0:T(8,128)(2,1)S(1)}, bf16[1,2560,128]{2,1,0:T(8,128)(2,1)S(1)}, u32[]{:S(2)}, u32[]{:S(2)}) collective-permute-start(bf16[1,2560,128]{2,1,0:T(8,128)(2,1)S(1)} %add_convert_fusion.3), channel_id=1, source_target_pairs={{0,64},{64,128},{128,192},{192,0},{1,65},{65,129},{129,193},{193,1... | collective-permute-start | bytes 1966088 | tf_op jit(solution)/shard_map/ppermute | solution.py:170
  119.8 27.3 %collective-permute-start.11 = (bf16[1,2560,128]{2,1,0:T(8,128)(2,1)S(1)}, bf16[1,2560,128]{2,1,0:T(8,128)(2,1)S(1)}, u32[]{:S(2)}, u32[]{:S(2)}) collective-permute-start(bf16[1,2560,128]{2,1,0:T(8,128)(2,1)S(1)} %add_convert_fusion.2), channel_id=1, source_target_pairs={{0,192},{64,0},{128,64},{192,128},{1,193},{65,1},{129,65},{193,129... | collective-permute-start | bytes 1966088 | tf_op jit(solution)/shard_map/ppermute | solution.py:170

commit v10 on v9

--- a/solution.py
+++ b/solution.py
@@ -94,7 +94,7 @@
     return [d_gate.astype(jnp.bfloat16), d_up.astype(jnp.bfloat16)]
 
 
-CHUNKS = 2
+CHUNKS = 1
 TILES = 5
 
 

time: 151 us -> 152 us (level)
  Pallas kernels: 14.5 us -> 18 us
  waiting for transfers between devices: 73.2 us -> 70.8 us
    pallas_call x3, Pallas kernels: 10.7 us -> 14.2 us  [slice_grads(): pl.pallas_call(functools.partial(slices_kernel, count), in_specs=[pl.Bloc...]
    ppermute x12, waiting for transfers between devices: 67 us -> 64.6 us  [moved(): lax.ppermute(block, 'x', [(i, (i + distance) % planes) for i in range(pla...]
  transfers between devices with their start and end apart: 13 -> 13, of which waited for: 9 -> 8; matrix products, arithmetic and copies ran while one was open for 1% -> 1% of each run, Pallas kernels for 5% -> 7%
where the time goes in v10:
time: 152 us; the launch traced here: 149 us
  waiting for transfers between devices  70.8 us (47%)
  starting transfers between devices  56 us (37%)
  Pallas kernels  18 us (12%)
  other arithmetic  2.65 us (2%)
    ppermute x12, waiting for transfers between devices, moved(): lax.ppermute(block, 'x', [(i, (i + distance) % planes) for i in range(pla...  64.6 us
    ppermute x12, starting transfers between devices, moved(): lax.ppermute(block, 'x', [(i, (i + distance) % planes) for i in range(pla...  37.6 us
    all_to_all x1, starting transfers between devices, body(): recv = lax.all_to_all(send, PLANE, 0, 0, tiled=True)  18.4 us
    pallas_call x3, Pallas kernels, slice_grads(): pl.pallas_call(functools.partial(slices_kernel, count), in_specs=[pl.Bloc...  14.2 us
    all_to_all x1, waiting for transfers between devices, body(): recv = lax.all_to_all(send, PLANE, 0, 0, tiled=True)  6.21 us
    pallas_call x1, Pallas kernels, body(): pl.pallas_call(pack_kernel, in_specs=[anywhere] * 5, out_specs=anywhere,...  3.79 us
  transfers between devices with their start and end apart: 13, of which 8 were waited for; matrix products, arithmetic and copies ran while one was open for 1% of the time, Pallas kernels for 7%

profile of v10, /device:TPU:1, one launch (start us, length us, event | category | flops | bytes accessed | tf_op | source)
XLA Modules:
  0.0 149.3 jit_solution(892661461040679841)
XLA Ops:
  0.6 3.8 %pack_rows.1 = bf16[128,4,3072]{2,1,0:T(4,128)(2,1)} custom-call(s32[6,128]{1,0:T(8,128)} %bitcast.9, s32[1,32]{1,0:T(1,128)} %bitcast.11, bf16[128,2560]{1,0:T(8,128)(2,1)} %tok_hbm.1, bf16[6,128,1024]{2,1,0:T(8,128)(2,1)} %bitcast.8, f32[6,128]{1,0:T(8,128)} %bitcast.10), custom_call_target="tpu_custom_call" | custom-call | tf_op jit(solution)/shard_map/pack_rows/pallas_call | solution.py:187
  4.4 18.4 %all-to-all-start = ((bf16[128,4,3072]{2,1,0:T(4,128)(2,1)}), bf16[128,4,3072]{2,1,0:T(4,128)(2,1)S(1)}, u32[]{:S(2)}, u32[]{:S(2)}) async-start(bf16[128,4,3072]{2,1,0:T(4,128)(2,1)} %pack_rows.1), calls=%async_computation | async-start | bytes 6291456 | tf_op jit(solution)/shard_map/all_to_all | solution.py:215
  22.9 4.4 %collective-permute-start = (bf16[1,2560,128]{2,1,0:T(8,128)(2,1)}, bf16[1,2560,128]{2,1,0:T(8,128)(2,1)S(1)}, u32[]{:S(2)}, u32[]{:S(2)}) collective-permute-start(bf16[1,2560,128]{2,1,0:T(8,128)(2,1)} %refs_0_), channel_id=1, source_target_pairs={{0,192},{64,0},{128,64},{192,128},{1,193},{65,1},{129,65},{193,129... | collective-permute-start | bytes 1966088 | tf_op jit(solution)/shard_map/ppermute | solution.py:170
  27.3 2.4 %collective-permute-start.2 = (bf16[1,2560,128]{2,1,0:T(8,128)(2,1)}, bf16[1,2560,128]{2,1,0:T(8,128)(2,1)}, u32[]{:S(2)}, u32[]{:S(2)}) collective-permute-start(bf16[1,2560,128]{2,1,0:T(8,128)(2,1)} %refs_0_), channel_id=1, source_target_pairs={{0,128},{64,192},{128,0},{192,64},{1,129},{65,193},{129,1},{193,65... | collective-permute-start | bytes 1966088 | tf_op jit(solution)/shard_map/ppermute | solution.py:170
  29.7 2.8 %collective-permute-start.1 = (bf16[1,2560,128]{2,1,0:T(8,128)(2,1)}, bf16[1,2560,128]{2,1,0:T(8,128)(2,1)}, u32[]{:S(2)}, u32[]{:S(2)}) collective-permute-start(bf16[1,2560,128]{2,1,0:T(8,128)(2,1)} %refs_1_), channel_id=1, source_target_pairs={{0,192},{64,0},{128,64},{192,128},{1,193},{65,1},{129,65},{193,129... | collective-permute-start | bytes 1966088 | tf_op jit(solution)/shard_map/ppermute | solution.py:170
  32.5 3.5 %collective-permute-start.3 = (bf16[1,2560,128]{2,1,0:T(8,128)(2,1)}, bf16[1,2560,128]{2,1,0:T(8,128)(2,1)}, u32[]{:S(2)}, u32[]{:S(2)}) collective-permute-start(bf16[1,2560,128]{2,1,0:T(8,128)(2,1)} %refs_1_), channel_id=1, source_target_pairs={{0,128},{64,192},{128,0},{192,64},{1,129},{65,193},{129,1},{193,65... | collective-permute-start | bytes 1966088 | tf_op jit(solution)/shard_map/ppermute | solution.py:170
  36.0 2.8 %collective-permute-start.4 = (bf16[1,2560,128]{2,1,0:T(8,128)(2,1)}, bf16[1,2560,128]{2,1,0:T(8,128)(2,1)}, u32[]{:S(2)}, u32[]{:S(2)}) collective-permute-start(bf16[1,2560,128]{2,1,0:T(8,128)(2,1)} %refs_0_), channel_id=1, source_target_pairs={{0,64},{64,128},{128,192},{192,0},{1,65},{65,129},{129,193},{193,1... | collective-permute-start | bytes 1966088 | tf_op jit(solution)/shard_map/ppermute | solution.py:170
  38.8 2.7 %collective-permute-done.refs_0_ = bf16[1,2560,128]{2,1,0:T(8,128)(2,1)S(1)} collective-permute-done((bf16[1,2560,128]{2,1,0:T(8,128)(2,1)}, bf16[1,2560,128]{2,1,0:T(8,128)(2,1)S(1)}, u32[]{:S(2)}, u32[]{:S(2)}) %collective-permute-start) | collective-permute-done | bytes 655392 | tf_op jit(solution)/shard_map/ppermute | solution.py:170
  41.5 0.8 copy-done.2
  42.3 1.9 %collective-permute-start.5 = (bf16[1,2560,128]{2,1,0:T(8,128)(2,1)}, bf16[1,2560,128]{2,1,0:T(8,128)(2,1)}, u32[]{:S(2)}, u32[]{:S(2)}) collective-permute-start(bf16[1,2560,128]{2,1,0:T(8,128)(2,1)} %refs_1_), channel_id=1, source_target_pairs={{0,64},{64,128},{128,192},{192,0},{1,65},{65,129},{129,193},{193,1... | collective-permute-start | bytes 1966088 | tf_op jit(solution)/shard_map/ppermute | solution.py:170
  44.3 0.1 pad_add_fusion
  44.4 0.1 slice.3.which_ref
  44.5 25.1 %collective-permute-done.1.refs_1_ = bf16[1,2560,128]{2,1,0:T(8,128)(2,1)} collective-permute-done((bf16[1,2560,128]{2,1,0:T(8,128)(2,1)}, bf16[1,2560,128]{2,1,0:T(8,128)(2,1)}, u32[]{:S(2)}, u32[]{:S(2)}) %collective-permute-start.1) | collective-permute-done | bytes 655392 | tf_op jit(solution)/shard_map/ppermute | solution.py:170
  69.5 6.2 %collective-permute-done.4.refs_2_ = bf16[1,2560,128]{2,1,0:T(8,128)(2,1)} collective-permute-done((bf16[1,2560,128]{2,1,0:T(8,128)(2,1)}, bf16[1,2560,128]{2,1,0:T(8,128)(2,1)}, u32[]{:S(2)}, u32[]{:S(2)}) %collective-permute-start.4) | collective-permute-done | bytes 655392 | tf_op jit(solution)/shard_map/ppermute | solution.py:170
  75.7 14.0 %collective-permute-done.5.refs_3_ = bf16[1,2560,128]{2,1,0:T(8,128)(2,1)} collective-permute-done((bf16[1,2560,128]{2,1,0:T(8,128)(2,1)}, bf16[1,2560,128]{2,1,0:T(8,128)(2,1)}, u32[]{:S(2)}, u32[]{:S(2)}) %collective-permute-start.5) | collective-permute-done | bytes 655392 | tf_op jit(solution)/shard_map/ppermute | solution.py:170
  89.8 6.2 %all-to-all-done.recv_ref = bf16[128,4,3072]{2,1,0:T(4,128)(2,1)S(1)} async-done(((bf16[128,4,3072]{2,1,0:T(4,128)(2,1)}), bf16[128,4,3072]{2,1,0:T(4,128)(2,1)S(1)}, u32[]{:S(2)}, u32[]{:S(2)}) %all-to-all-start) | async-done | bytes 3145760 | tf_op jit(solution)/shard_map/all_to_all | solution.py:215
  96.0 4.3 %slice_grads.4 = (bf16[1,2560,128]{2,1,0:T(8,128)(2,1)S(1)}, bf16[1,2560,128]{2,1,0:T(8,128)(2,1)S(1)}) custom-call(s32[1]{0:T(128)} %bitcast.6.which_ref, bf16[128,4,3072]{2,1,0:T(4,128)(2,1)S(1)} %all-to-all-done.recv_ref, bf16[1,2560,128]{2,1,0:T(8,128)(2,1)} %collective-permute-done.2.refs_0_, bf16[1,2560,128]{2,1,0:T(8,128)(2,1)} %collective-permute-done.3.refs_1_), custom_call_target="tpu_custom_call" | custom-call | flops 5368709120 | bytes 5767168 | tf_op jit(solution)/shard_map/slice_grads/pallas_call | solution.py:147
  100.3 3.1 %collective-permute-start.6 = (bf16[1,2560,128]{2,1,0:T(8,128)(2,1)S(1)}, bf16[1,2560,128]{2,1,0:T(8,128)(2,1)S(1)}, u32[]{:S(2)}, u32[]{:S(2)}) collective-permute-start(bf16[1,2560,128]{2,1,0:T(8,128)(2,1)S(1)} %get-tuple-element.36), channel_id=1, source_target_pairs={{0,64},{64,128},{128,192},{192,0},{1,65},{65,129},{129,193},{193,1... | collective-permute-start | bytes 1966088 | tf_op jit(solution)/shard_map/ppermute | solution.py:170
  103.5 3.4 %collective-permute-start.7 = (bf16[1,2560,128]{2,1,0:T(8,128)(2,1)S(1)}, bf16[1,2560,128]{2,1,0:T(8,128)(2,1)S(1)}, u32[]{:S(2)}, u32[]{:S(2)}) collective-permute-start(bf16[1,2560,128]{2,1,0:T(8,128)(2,1)S(1)} %get-tuple-element.38), channel_id=1, source_target_pairs={{0,192},{64,0},{128,64},{192,128},{1,193},{65,1},{129,65},{193,129... | collective-permute-start | bytes 1966088 | tf_op jit(solution)/shard_map/ppermute | solution.py:170
  106.8 6.3 %slice_grads.3 = (bf16[1,2560,128]{2,1,0:T(8,128)(2,1)S(1)}, bf16[1,2560,128]{2,1,0:T(8,128)(2,1)S(1)}, bf16[1,2560,128]{2,1,0:T(8,128)(2,1)S(1)}, bf16[1,2560,128]{2,1,0:T(8,128)(2,1)S(1)}) custom-call(s32[2]{0:T(128)S(1)} %slice.3.which_ref, bf16[128,4,3072]{2,1,0:T(4,128)(2,1)S(1)} %all-to-all-done.recv_ref, bf16[1,2560,128]{2,1,0:T(8,128)(2,1)S(1)} %copy-done.3, ...), custom_call_target="tpu_custom_call" | custom-call | flops 10737418240 | bytes 8388608 | tf_op jit(solution)/shard_map/slice_grads/pallas_call | solution.py:147
  113.1 1.9 %collective-permute-start.8 = (bf16[1,2560,128]{2,1,0:T(8,128)(2,1)S(1)}, bf16[1,2560,128]{2,1,0:T(8,128)(2,1)S(1)}, u32[]{:S(2)}, u32[]{:S(2)}) collective-permute-start(bf16[1,2560,128]{2,1,0:T(8,128)(2,1)S(1)} %get-tuple-element.42), channel_id=1, source_target_pairs={{0,64},{64,128},{128,192},{192,0},{1,65},{65,129},{129,193},{193,1... | collective-permute-start | bytes 1966088 | tf_op jit(solution)/shard_map/ppermute | solution.py:170
  115.1 4.6 %collective-permute-start.9 = (bf16[1,2560,128]{2,1,0:T(8,128)(2,1)S(1)}, bf16[1,2560,128]{2,1,0:T(8,128)(2,1)S(1)}, u32[]{:S(2)}, u32[]{:S(2)}) collective-permute-start(bf16[1,2560,128]{2,1,0:T(8,128)(2,1)S(1)} %get-tuple-element.43), channel_id=1, source_target_pairs={{0,192},{64,0},{128,64},{192,128},{1,193},{65,1},{129,65},{193,129... | collective-permute-start | bytes 1966088 | tf_op jit(solution)/shard_map/ppermute | solution.py:170
  119.7 0.2 add_convert_fusion.3
  119.9 2.1 %collective-permute-start.10 = (bf16[1,2560,128]{2,1,0:T(8,128)(2,1)S(1)}, bf16[1,2560,128]{2,1,0:T(8,128)(2,1)S(1)}, u32[]{:S(2)}, u32[]{:S(2)}) collective-permute-start(bf16[1,2560,128]{2,1,0:T(8,128)(2,1)S(1)} %add_convert_fusion.3), channel_id=1, source_target_pairs={{0,64},{64,128},{128,192},{192,0},{1,65},{65,129},{129,193},{193,1... | collective-permute-start | bytes 1966088 | tf_op jit(solution)/shard_map/ppermute | solution.py:170
  121.9 0.2 add_convert_fusion.2
  122.1 4.8 %collective-permute-start.11 = (bf16[1,2560,128]{2,1,0:T(8,128)(2,1)S(1)}, bf16[1,2560,128]{2,1,0:T(8,128)(2,1)S(1)}, u32[]{:S(2)}, u32[]{:S(2)}) collective-permute-start(bf16[1,2560,128]{2,1,0:T(8,128)(2,1)S(1)} %add_convert_fusion.2), channel_id=1, source_target_pairs={{0,192},{64,0},{128,64},{192,128},{1,193},{65,1},{129,65},{193,129... | collective-permute-start | bytes 1966088 | tf_op jit(solution)/shard_map/ppermute | solution.py:170
  126.9 3.6 %slice_grads.5 = (f32[1,2560,128]{2,1,0:T(8,128)S(1)}, f32[1,2560,128]{2,1,0:T(8,128)S(1)}) custom-call(s32[1]{0:T(128)} %bitcast.which_ref, bf16[128,4,3072]{2,1,0:T(4,128)(2,1)S(1)} %all-to-all-done.recv_ref, bf16[1,2560,128]{2,1,0:T(8,128)(2,1)S(1)} %copy-done, bf16[1,2560,128]{2,1,0:T(8,128)(2,1)S(1)} %copy-done.1), custom_call_target="tpu_custom_call" | custom-call | flops 5368709120 | bytes 5767168 | tf_op jit(solution)/shard_map/slice_grads/pallas_call | solution.py:147
  130.5 2.6 %collective-permute-done.8 = bf16[1,2560,128]{2,1,0:T(8,128)(2,1)S(1)} collective-permute-done((bf16[1,2560,128]{2,1,0:T(8,128)(2,1)S(1)}, bf16[1,2560,128]{2,1,0:T(8,128)(2,1)S(1)}, u32[]{:S(2)}, u32[]{:S(2)}) %collective-permute-start.8) | collective-permute-done | bytes 655392 | tf_op jit(solution)/shard_map/ppermute | solution.py:170
  133.1 1.1 collective-permute-done.9
  134.2 12.9 %collective-permute-done.10 = bf16[1,2560,128]{2,1,0:T(8,128)(2,1)S(1)} collective-permute-done((bf16[1,2560,128]{2,1,0:T(8,128)(2,1)S(1)}, bf16[1,2560,128]{2,1,0:T(8,128)(2,1)S(1)}, u32[]{:S(2)}, u32[]{:S(2)}) %collective-permute-start.10) | collective-permute-done | bytes 655392 | tf_op jit(solution)/shard_map/ppermute | solution.py:170
  147.1 1.1 add_convert_fusion.1
  148.2 1.1 add_convert_fusion
  (12 shorter events, 0.0 us)
Async XLA Ops:
  4.4 91.5 %all-to-all-start = ((bf16[128,4,3072]{2,1,0:T(4,128)(2,1)}), bf16[128,4,3072]{2,1,0:T(4,128)(2,1)S(1)}, u32[]{:S(2)}, u32[]{:S(2)}) async-start(bf16[128,4,3072]{2,1,0:T(4,128)(2,1)} %pack_rows.1), calls=%async_computation | async-start | bytes 6291456 | tf_op jit(solution)/shard_map/all_to_all | solution.py:215
  22.9 18.6 %collective-permute-start = (bf16[1,2560,128]{2,1,0:T(8,128)(2,1)}, bf16[1,2560,128]{2,1,0:T(8,128)(2,1)S(1)}, u32[]{:S(2)}, u32[]{:S(2)}) collective-permute-start(bf16[1,2560,128]{2,1,0:T(8,128)(2,1)} %refs_0_), channel_id=1, source_target_pairs={{0,192},{64,0},{128,64},{192,128},{1,193},{65,1},{129,65},{193,129... | collective-permute-start | bytes 1966088 | tf_op jit(solution)/shard_map/ppermute | solution.py:170
  27.3 42.3 %collective-permute-start.2 = (bf16[1,2560,128]{2,1,0:T(8,128)(2,1)}, bf16[1,2560,128]{2,1,0:T(8,128)(2,1)}, u32[]{:S(2)}, u32[]{:S(2)}) collective-permute-start(bf16[1,2560,128]{2,1,0:T(8,128)(2,1)} %refs_0_), channel_id=1, source_target_pairs={{0,128},{64,192},{128,0},{192,64},{1,129},{65,193},{129,1},{193,65... | collective-permute-start | bytes 1966088 | tf_op jit(solution)/shard_map/ppermute | solution.py:170
  29.7 39.8 %collective-permute-start.1 = (bf16[1,2560,128]{2,1,0:T(8,128)(2,1)}, bf16[1,2560,128]{2,1,0:T(8,128)(2,1)}, u32[]{:S(2)}, u32[]{:S(2)}) collective-permute-start(bf16[1,2560,128]{2,1,0:T(8,128)(2,1)} %refs_1_), channel_id=1, source_target_pairs={{0,192},{64,0},{128,64},{192,128},{1,193},{65,1},{129,65},{193,129... | collective-permute-start | bytes 1966088 | tf_op jit(solution)/shard_map/ppermute | solution.py:170
  32.5 37.1 %collective-permute-start.3 = (bf16[1,2560,128]{2,1,0:T(8,128)(2,1)}, bf16[1,2560,128]{2,1,0:T(8,128)(2,1)}, u32[]{:S(2)}, u32[]{:S(2)}) collective-permute-start(bf16[1,2560,128]{2,1,0:T(8,128)(2,1)} %refs_1_), channel_id=1, source_target_pairs={{0,128},{64,192},{128,0},{192,64},{1,129},{65,193},{129,1},{193,65... | collective-permute-start | bytes 1966088 | tf_op jit(solution)/shard_map/ppermute | solution.py:170
  36.0 39.7 %collective-permute-start.4 = (bf16[1,2560,128]{2,1,0:T(8,128)(2,1)}, bf16[1,2560,128]{2,1,0:T(8,128)(2,1)}, u32[]{:S(2)}, u32[]{:S(2)}) collective-permute-start(bf16[1,2560,128]{2,1,0:T(8,128)(2,1)} %refs_0_), channel_id=1, source_target_pairs={{0,64},{64,128},{128,192},{192,0},{1,65},{65,129},{129,193},{193,1... | collective-permute-start | bytes 1966088 | tf_op jit(solution)/shard_map/ppermute | solution.py:170
  41.5 0.8 copy-start.2
  42.3 47.4 %collective-permute-start.5 = (bf16[1,2560,128]{2,1,0:T(8,128)(2,1)}, bf16[1,2560,128]{2,1,0:T(8,128)(2,1)}, u32[]{:S(2)}, u32[]{:S(2)}) collective-permute-start(bf16[1,2560,128]{2,1,0:T(8,128)(2,1)} %refs_1_), channel_id=1, source_target_pairs={{0,64},{64,128},{128,192},{192,0},{1,65},{65,129},{129,193},{193,1... | collective-permute-start | bytes 1966088 | tf_op jit(solution)/shard_map/ppermute | solution.py:170
  96.0 10.9 %copy-start.3 = (bf16[1,2560,128]{2,1,0:T(8,128)(2,1)S(1)}, bf16[1,2560,128]{2,1,0:T(8,128)(2,1)}, u32[]{:S(2)}) copy-start(bf16[1,2560,128]{2,1,0:T(8,128)(2,1)} %copy-done.2) | copy-start | bytes 1966084
  100.3 19.3 %collective-permute-start.6 = (bf16[1,2560,128]{2,1,0:T(8,128)(2,1)S(1)}, bf16[1,2560,128]{2,1,0:T(8,128)(2,1)S(1)}, u32[]{:S(2)}, u32[]{:S(2)}) collective-permute-start(bf16[1,2560,128]{2,1,0:T(8,128)(2,1)S(1)} %get-tuple-element.36), channel_id=1, source_target_pairs={{0,64},{64,128},{128,192},{192,0},{1,65},{65,129},{129,193},{193,1... | collective-permute-start | bytes 1966088 | tf_op jit(solution)/shard_map/ppermute | solution.py:170
  103.5 18.5 %collective-permute-start.7 = (bf16[1,2560,128]{2,1,0:T(8,128)(2,1)S(1)}, bf16[1,2560,128]{2,1,0:T(8,128)(2,1)S(1)}, u32[]{:S(2)}, u32[]{:S(2)}) collective-permute-start(bf16[1,2560,128]{2,1,0:T(8,128)(2,1)S(1)} %get-tuple-element.38), channel_id=1, source_target_pairs={{0,192},{64,0},{128,64},{192,128},{1,193},{65,1},{129,65},{193,129... | collective-permute-start | bytes 1966088 | tf_op jit(solution)/shard_map/ppermute | solution.py:170
  113.1 19.9 %collective-permute-start.8 = (bf16[1,2560,128]{2,1,0:T(8,128)(2,1)S(1)}, bf16[1,2560,128]{2,1,0:T(8,128)(2,1)S(1)}, u32[]{:S(2)}, u32[]{:S(2)}) collective-permute-start(bf16[1,2560,128]{2,1,0:T(8,128)(2,1)S(1)} %get-tuple-element.42), channel_id=1, source_target_pairs={{0,64},{64,128},{128,192},{192,0},{1,65},{65,129},{129,193},{193,1... | collective-permute-start | bytes 1966088 | tf_op jit(solution)/shard_map/ppermute | solution.py:170
  115.1 19.1 %collective-permute-start.9 = (bf16[1,2560,128]{2,1,0:T(8,128)(2,1)S(1)}, bf16[1,2560,128]{2,1,0:T(8,128)(2,1)S(1)}, u32[]{:S(2)}, u32[]{:S(2)}) collective-permute-start(bf16[1,2560,128]{2,1,0:T(8,128)(2,1)S(1)} %get-tuple-element.43), channel_id=1, source_target_pairs={{0,192},{64,0},{128,64},{192,128},{1,193},{65,1},{129,65},{193,129... | collective-permute-start | bytes 1966088 | tf_op jit(solution)/shard_map/ppermute | solution.py:170
  119.8 7.0 %copy-start = (bf16[1,2560,128]{2,1,0:T(8,128)(2,1)S(1)}, bf16[1,2560,128]{2,1,0:T(8,128)(2,1)}, u32[]{:S(2)}) copy-start(bf16[1,2560,128]{2,1,0:T(8,128)(2,1)} %refs_0_) | copy-start | bytes 1966084
  119.9 7.0 %copy-start.1 = (bf16[1,2560,128]{2,1,0:T(8,128)(2,1)S(1)}, bf16[1,2560,128]{2,1,0:T(8,128)(2,1)}, u32[]{:S(2)}) copy-start(bf16[1,2560,128]{2,1,0:T(8,128)(2,1)} %refs_1_) | copy-start | bytes 1966084
  119.9 27.2 %collective-permute-start.10 = (bf16[1,2560,128]{2,1,0:T(8,128)(2,1)S(1)}, bf16[1,2560,128]{2,1,0:T(8,128)(2,1)S(1)}, u32[]{:S(2)}, u32[]{:S(2)}) collective-permute-start(bf16[1,2560,128]{2,1,0:T(8,128)(2,1)S(1)} %add_convert_fusion.3), channel_id=1, source_target_pairs={{0,64},{64,128},{128,192},{192,0},{1,65},{65,129},{129,193},{193,1... | collective-permute-start | bytes 1966088 | tf_op jit(solution)/shard_map/ppermute | solution.py:170
  122.1 26.1 %collective-permute-start.11 = (bf16[1,2560,128]{2,1,0:T(8,128)(2,1)S(1)}, bf16[1,2560,128]{2,1,0:T(8,128)(2,1)S(1)}, u32[]{:S(2)}, u32[]{:S(2)}) collective-permute-start(bf16[1,2560,128]{2,1,0:T(8,128)(2,1)S(1)} %add_convert_fusion.2), channel_id=1, source_target_pairs={{0,192},{64,0},{128,64},{192,128},{1,193},{65,1},{129,65},{193,129... | collective-permute-start | bytes 1966088 | tf_op jit(solution)/shard_map/ppermute | solution.py:170
